TPU v7x, 512 devices: a whole 4x8x8 slice. The times are simulated.
512 devices in a mesh: strip: 16 (over z, core), date: 32 (over x, y).
Axes of the slice: x: 4, y: 8, z: 8, core: 2. Of those that a mesh axis runs over, the one named last changes fastest.
Arguments:
- images: bfloat16 [512, 1024, 128], P('date', 'strip'), may hold values from 0.19921875 to 5
- inverse_blocks: float32 [2, 32, 512, 512], P(None, 'strip', 'date'), as said below
- pair_first: int32 [1024], P('date'), may hold values from 0 to 15
- pair_block: int32 [1024, 1], P('date'), may hold values from 0 to 31; in each aligned block of 32 rows (0 to 31, 32 to 63, ...) at most 2 rows name the same one
- pair_second: int32 [1024], P('date'), may hold values from 0 to 15
- pair_count: int32 [32], P('date'), may hold values from 8 to 32, as said below
- shifts: int32 [1024, 2, 32], P('date', None, 'strip'), may hold values from -8 to 8
- anchors: int32 [32], P('strip'), may hold values from 0 to 96, as said below
Outputs:
- pair_offsets: float32 [1024, 2, 32], P('date', None, 'strip')
- series: float32 [2, 32, 512], P(None, 'strip', 'date')
Inputs may be any that keep to these rules, and one draw needn't show every extreme that they name: `pair_block`: among the 32 slots of one date block at most 2 name one partner block, and some block is named that often. `pair_count`: slots 0 to count - 1 of a date block are live; slots at or past the count carry no pair, and their partner windows need not be sent. One block has all 32 live, one has 8, every other block 24 or more. `anchors`: chip q starts at column (q % 2) * 64 plus 0 to 32. `inverse_blocks`: symmetric in its last two dimensions.
All inputs are finite; a program needn't handle non-finite values.
Results may differ from a plain program's by a relative error of at most 0.008.
Values may be sent and summed in bfloat16 or wider, within the bound.
No kernel may reach another device: no remote copies, remote signals or barrier semaphores. Data moves between devices by JAX's collectives and lax.ppermute only.
A program may use at most 64 MiB of HBM per device.

v0:
```python
import math

import jax
import jax.numpy as jnp
from jax import lax
from jax.sharding import PartitionSpec as P

SMAX = 8


def padded(cells, sides, width):
    for axis, dim in sides:
        count = lax.axis_size(axis)
        ends = count - 1
        head = lax.slice_in_dim(cells, 0, width, axis=dim)
        tail = lax.slice_in_dim(cells, cells.shape[dim] - width, cells.shape[dim], axis=dim)
        cells = jnp.concatenate(
            [
                lax.ppermute(tail, axis, [(i, (i + 1) % count) for i in range(ends)]),
                cells,
                lax.ppermute(head, axis, [((i + 1) % count, i) for i in range(ends)]),
            ],
            axis=dim,
        )
    return cells


def make_tables(length):
    counter = jnp.arange(length, dtype=jnp.int32)
    products = counter[:, None] * counter[None, :] % length
    radians = products.astype(jnp.float32) * (2.0 * math.pi / length)
    cosine = jnp.cos(radians)
    sine_part = -jnp.sin(radians)
    forward = jnp.concatenate([cosine, sine_part], axis=1).astype(jnp.bfloat16)
    over_len = 2 * length
    signed = jnp.where(counter < length // 2, counter, counter - length)
    places = jnp.arange(over_len, dtype=jnp.int32)
    turned = signed[:, None] * places[None, :] % over_len
    angles = turned.astype(jnp.float32) * (2.0 * math.pi / over_len)
    vcosine = jnp.cos(angles)
    vsine = jnp.sin(angles)
    top_rows = jnp.concatenate([vcosine, vsine], axis=1)
    low_rows = jnp.concatenate([-vsine, vcosine], axis=1)
    inverse_rows = jnp.concatenate([top_rows, low_rows], axis=0).astype(jnp.bfloat16)
    displace = ((places + length) % over_len - length).astype(jnp.float32) * 0.5
    return (
        forward,
        cosine.astype(jnp.bfloat16),
        sine_part.astype(jnp.bfloat16),
        inverse_rows,
        vcosine.T.astype(jnp.bfloat16),
        vsine.T.astype(jnp.bfloat16),
        displace,
    )


def spectra(windows, tables):
    forward, cosine_b, sine_b = (tables[0], tables[1], tables[2])
    length = windows.shape[-1]
    values = windows.astype(jnp.float32)
    centred = (values - jnp.mean(values, axis=(1, 2), keepdims=True)).astype(jnp.bfloat16)
    section_one = jnp.einsum(
        "bmn,nk->bmk", centred, forward, preferred_element_type=jnp.float32
    ).astype(jnp.bfloat16)
    with_cos = jnp.einsum("km,bmj->bkj", cosine_b, section_one, preferred_element_type=jnp.float32)
    with_sin = jnp.einsum("km,bmj->bkj", sine_b, section_one, preferred_element_type=jnp.float32)
    real_part = with_cos[:, :, :length] - with_sin[:, :, length:]
    imag_part = with_sin[:, :, :length] + with_cos[:, :, length:]
    return jnp.concatenate([real_part, imag_part], axis=2).astype(jnp.bfloat16)


def centroid(near_spec, far_spec, tables):
    inverse_rows, back_cos, back_sin, displace = (tables[3], tables[4], tables[5], tables[6])
    length = near_spec.shape[-1] // 2
    near_re = near_spec[:, :, :length].astype(jnp.float32)
    near_im = near_spec[:, :, length:].astype(jnp.float32)
    far_re = far_spec[:, :, :length].astype(jnp.float32)
    far_im = far_spec[:, :, length:].astype(jnp.float32)
    cross_re = near_re * far_re + near_im * far_im
    cross_im = near_im * far_re - near_re * far_im
    cross_spec = jnp.concatenate([cross_re, cross_im], axis=2).astype(jnp.bfloat16)
    along = jnp.einsum(
        "bun,nl->bul", cross_spec, inverse_rows, preferred_element_type=jnp.float32
    ).astype(jnp.bfloat16)
    half_width = along.shape[-1] // 2
    surface = jnp.einsum(
        "ku,bul->bkl", back_cos, along[:, :, :half_width], preferred_element_type=jnp.float32
    )
    surface = surface - jnp.einsum(
        "ku,bul->bkl", back_sin, along[:, :, half_width:], preferred_element_type=jnp.float32
    )
    energy = surface * surface
    norm_val = jnp.mean(energy, axis=(1, 2)) + 1e-06
    row_shift = jnp.mean(energy * displace[None, :, None], axis=(1, 2)) / norm_val
    col_shift = jnp.mean(energy * displace[None, None, :], axis=(1, 2)) / norm_val
    return jnp.stack([row_shift, col_shift], axis=1)


def body(images, inverse_blocks, pair_first, pair_block, pair_second, pair_count, shifts, anchors):
    devices = lax.axis_size("date")
    block_id = lax.axis_index("date")
    dates_dev, length, columns = images.shape
    pair_dev = pair_first.shape[0]
    chip_count = anchors.shape[0]
    capacity = max(2, 2 * pair_dev // devices)
    margin = SMAX
    extent = length + 2 * margin
    tables = make_tables(length)
    target = pair_block[:, 0]
    hit_table = (target[:, None] == jnp.arange(devices, dtype=jnp.int32)[None, :]).astype(jnp.int32)
    earlier = jnp.cumsum(hit_table, axis=0) - hit_table
    rank_in = jnp.sum(earlier * hit_table, axis=1)
    slot_of = target * capacity + rank_in
    requests = (
        jnp.zeros((devices * capacity,), jnp.int32)
        .at[slot_of]
        .set(pair_second)
        .reshape(devices, capacity)
    )
    asked_for = lax.all_to_all(requests, "date", split_axis=0, concat_axis=0, tiled=True)
    wanted = asked_for.reshape(-1)
    picked = jnp.take(images, wanted, axis=0).reshape(devices, capacity, length, columns)
    arrived = lax.all_to_all(picked, "date", split_axis=0, concat_axis=0, tiled=True)
    framed = padded(arrived, (("strip", 2),), margin)
    framed = framed.reshape(devices * capacity, extent, columns)
    framed = jnp.pad(framed, ((0, 0), (0, 0), (margin, margin + length // 2)))
    own_pad = jnp.pad(images, ((0, 0), (0, 0), (0, length // 2)))
    own_list = []
    region_list = []
    for chip_one in range(chip_count):
        own_list.append(lax.dynamic_slice_in_dim(own_pad, anchors[chip_one], length, 2))
        region_list.append(lax.dynamic_slice_in_dim(framed, anchors[chip_one], extent, 2))
    own_windows = jnp.stack(own_list, axis=1)
    regions = jnp.stack(region_list, axis=1)
    own_spec = spectra(own_windows.reshape(-1, length, length), tables).reshape(
        dates_dev, chip_count, length, 2 * length
    )
    step_pairs = math.gcd(pair_dev, max(1, 512 // chip_count))
    turn_count = pair_dev // step_pairs
    inside = jnp.arange(length, dtype=jnp.int32)
    across = jnp.arange(extent, dtype=jnp.int32)

    def one_turn(packed):
        slots_turn, firsts_turn, shifts_turn = packed
        regions_turn = jnp.take(regions, slots_turn, axis=0)
        row_start = margin + shifts_turn[:, 0, :]
        col_start = margin + shifts_turn[:, 1, :]
        row_pick = (
            across[None, None, None, :] == row_start[:, :, None, None] + inside[None, None, :, None]
        ).astype(jnp.bfloat16)
        col_pick = (
            across[None, None, :, None] == col_start[:, :, None, None] + inside[None, None, None, :]
        ).astype(jnp.bfloat16)
        row_cut = jnp.einsum(
            "pcie,pcef->pcif", row_pick, regions_turn, preferred_element_type=jnp.float32
        ).astype(jnp.bfloat16)
        far_windows = jnp.einsum(
            "pcif,pcfj->pcij", row_cut, col_pick, preferred_element_type=jnp.float32
        ).astype(jnp.bfloat16)
        far_spec = spectra(far_windows.reshape(-1, length, length), tables)
        near_spec = jnp.take(own_spec, firsts_turn, axis=0).reshape(-1, length, 2 * length)
        return centroid(near_spec, far_spec, tables).reshape(step_pairs, chip_count, 2)

    packed = (
        slot_of.reshape(turn_count, step_pairs),
        pair_first.reshape(turn_count, step_pairs),
        shifts.reshape(turn_count, step_pairs, 2, chip_count),
    )
    centroids = lax.map(one_turn, packed).reshape(pair_dev, chip_count, 2)
    live_mask = (jnp.arange(pair_dev, dtype=jnp.int32) < pair_count[0]).astype(jnp.float32)
    pair_offsets = (shifts.astype(jnp.float32) + jnp.swapaxes(centroids, 1, 2)) * live_mask[
        :, None, None
    ]
    dates_all = dates_dev * devices
    date_ids = jnp.arange(dates_all, dtype=jnp.int32)
    second_id = target * dates_dev + pair_second
    first_id = block_id * dates_dev + pair_first
    incidence = (second_id[:, None] == date_ids[None, :]).astype(jnp.float32) - (
        first_id[:, None] == date_ids[None, :]
    ).astype(jnp.float32)
    partial_value = jnp.einsum(
        "pxc,pd->xcd", pair_offsets, incidence, precision=lax.Precision.HIGHEST
    )
    rhs_whole = lax.psum(partial_value, "date")
    series = jnp.einsum("xcde,xce->xcd", inverse_blocks, rhs_whole, precision=lax.Precision.HIGHEST)
    return (pair_offsets, series)


def solution(mesh):
    return jax.shard_map(
        body,
        mesh=mesh,
        in_specs=(
            P("date", "strip", None),
            P(None, "strip", "date", None),
            P("date"),
            P("date", None),
            P("date"),
            P("date"),
            P("date", None, "strip"),
            P("strip"),
        ),
        out_specs=(P("date", None, "strip"), P(None, "strip", "date")),
        check_vma=False,
    )
```

profile of v0, /device:TPU:448, one launch (start us, length us, event | category | flops | bytes accessed | tf_op | source)
XLA Modules:
  0.0 169.3 jit_solution(13657500790757236929)
XLA Ops:
  0.7 0.8 fusion.78
  1.5 0.8 select_reduce_fusion
  2.3 1.2 and_bitcast_fusion
  3.5 0.8 scatter_custom_fusion
  4.3 0.7 all_to_all.9
  5.0 10.0 %all-to-all-start = ((s32[32,1,2]{2,1,0:T(1,128)}), s32[32,1,2]{2,1,0:T(1,128)S(1)}, u32[]{:S(2)}, u32[]{:S(2)}) async-start(s32[32,1,2]{2,1,0:T(1,128)} %bitcast.18), calls=%async_computation | async-start | bytes 32768 | tf_op jit(solution)/shard_map/all_to_all | solution.py:120
  15.0 0.2 negate_convert_fusion.1
  15.2 1.3 fusion.122
  20.3 1.3 fusion.32
  21.6 0.1 maximum_convert_fusion
  21.7 0.2 fusion.34
  22.0 0.1 div.58
  22.1 0.2 fusion.26
  22.3 0.3 convolution_convert_fusion.2
  22.6 0.4 convolution_bitcast_fusion.2
  23.0 0.6 broadcast_add_fusion
  23.6 1.1 all-to-all-done
  24.8 0.5 broadcast.369
  25.3 0.7 reduce.8
  26.0 0.1 reshape.257
  26.1 1.7 gather_fusion.1
  27.8 0.1 copy.25
  27.9 0.1 copy.26
  28.0 2.4 %broadcast_select_fusion = bf16[32,2,64,128]{3,2,1,0:T(8,128)(2,1)} fusion(bf16[32,2,64,128]{3,2,1,0:T(8,128)(2,1)} %bitcast.99, pred[32,2]{1,0:T(8,128)(4,1)S(1)} %copy.26), kind=kLoop, calls=%fused_computation.58 | loop fusion | flops 524288 | bytes 2097216 | tf_op jit(solution)/shard_map/jit(_take)/select_n | solution.py:122
  30.4 8.6 %all-to-all-start.1 = ((bf16[32,2,64,128]{3,2,1,0:T(8,128)(2,1)}), bf16[32,2,64,128]{3,2,1,0:T(8,128)(2,1)S(1)}, u32[]{:S(2)}, u32[]{:S(2)}) async-start(bf16[32,2,64,128]{3,2,1,0:T(8,128)(2,1)} %broadcast_select_fusion), calls=%async_computation.1 | async-start | bytes 2097152 | tf_op jit(solution)/shard_map/all_to_all | solution.py:123
  39.0 0.1 copy.23
  39.1 0.1 copy.27
  39.3 0.1 broadcast_in_dim.84
  40.1 0.4 convolution_bitcast_fusion.3
  40.5 0.6 fusion.22
  41.1 0.3 pad_maximum_fusion.2
  41.4 0.7 gather_fusion
  42.2 0.5 fusion.91
  42.7 0.5 multiply_add_fusion
  43.2 0.8 fusion.77
  44.0 0.8 iota_add_fusion
  44.8 0.2 bitcast_select_fusion
  45.0 22.2 %all-to-all-done.1 = bf16[32,2,64,128]{3,2,1,0:T(8,128)(2,1)S(1)} async-done(((bf16[32,2,64,128]{3,2,1,0:T(8,128)(2,1)}), bf16[32,2,64,128]{3,2,1,0:T(8,128)(2,1)S(1)}, u32[]{:S(2)}, u32[]{:S(2)}) %all-to-all-start.1) | async-done | bytes 1048608 | tf_op jit(solution)/shard_map/all_to_all | solution.py:123
  67.3 1.9 %collective-permute-start = (bf16[32,2,8,128]{3,2,1,0:T(8,128)(2,1)S(1)}, bf16[32,2,8,128]{3,2,1,0:T(8,128)(2,1)S(1)}, u32[]{:S(2)}, u32[]{:S(2)}) collective-permute-start(bf16[32,2,8,128]{3,2,1,0:T(8,128)(2,1)S(1)} %get-tuple-element.68), channel_id=1, source_target_pairs={{0,32},{32,64},{64,96},{96,128},{128,160},{160,192},{192,224},{224... | collective-permute-start | bytes 393224 | tf_op jit(solution)/shard_map/ppermute | solution.py:19
  69.2 3.8 %collective-permute-start.1 = (bf16[32,2,8,128]{3,2,1,0:T(8,128)(2,1)S(1)}, bf16[32,2,8,128]{3,2,1,0:T(8,128)(2,1)S(1)}, u32[]{:S(2)}, u32[]{:S(2)}) collective-permute-start(bf16[32,2,8,128]{3,2,1,0:T(8,128)(2,1)S(1)} %get-tuple-element.69), channel_id=1, source_target_pairs={{32,0},{64,32},{96,64},{128,96},{160,128},{192,160},{224,192},{256... | collective-permute-start | bytes 393224 | tf_op jit(solution)/shard_map/ppermute | solution.py:21
  73.1 0.5 compare_convert_fusion
  76.1 0.6 pad_clamp_fusion
  76.7 0.1 pad_maximum_fusion.1
  76.9 1.1 fusion.12
  77.9 2.1 %pad_maximum_fusion = bf16[64,2,80,80]{3,2,0,1:T(8,128)(2,1)} fusion(bf16[64,1,80,80]{3,2,0,1:T(8,128)(2,1)S(1)} %get-tuple-element.67, bf16[64,1,80,80]{3,2,0,1:T(8,128)(2,1)S(1)} %get-tuple-element.66), kind=kLoop, calls=%fused_computation.13 | loop fusion | flops 819200 | bytes 3276800 | tf_op jit(solution)/shard_map/stack | solution.py:134
  80.0 2.7 %gather_fusion.2 = bf16[32,2,80,80]{3,2,1,0:T(8,128)(2,1)S(1)} fusion(bf16[64,2,80,80]{3,2,0,1:T(8,128)(2,1)} %pad_maximum_fusion, s32[1024]{0:T(1024)} %pad_clamp_fusion), kind=kCustom, calls=%fused_computation.2 | custom fusion | bytes 1638528 | tf_op jit(solution)/shard_map/while/body/eval_jaxpr/jit(_take)/gather | solution.py:145
  82.7 2.7 %fusion.123 = (f32[32,2]{1,0:T(8,128)S(1)}, f32[32,2,64,64]{3,2,1,0:T(8,128)}) fusion(s32[32,2,64]{2,1,0:T(2,128)S(1)} %copy-done.7, bf16[32,2,80,80]{3,2,1,0:T(8,128)(2,1)S(1)} %gather_fusion.2, pred[32]{0:T(512)(128)(4,1)S(1)} %copy-done.17, s32[32,2,64]{2,1,0:T(2,128)S(1)} %copy-done.8), kind=kOutput, calls=%fused_computation.198 | convolution fusion | flops 96550848 | bytes 1900832 | tf_op jit(solution)/shard_map/while/body/eval_jaxpr/pcif,pcfj->pcij/dot_general | solution.py:157
  85.4 0.1 div.60
  85.5 1.8 %fusion.6 = bf16[64,64,64]{2,1,0:T(8,128)(2,1)S(1)} fusion(f32[32,2,64,64]{3,2,1,0:T(8,128)} %get-tuple-element.84, f32[64]{0:T(128)S(1)} %div.60), kind=kLoop, calls=%fused_computation.23 | loop fusion | flops 524288 | bytes 1573120 | tf_op jit(solution)/shard_map/while/body/eval_jaxpr/convert_element_type | solution.py:61
  87.4 0.5 convolution_convert_fusion.1
  87.9 0.5 convolution_bitcast_fusion
  88.4 0.5 convolution_bitcast_fusion.1
  88.9 1.5 fusion.1
  90.4 0.8 fusion.3
  91.3 0.8 convolution_convert_fusion
  92.1 0.9 fusion.19
  93.1 1.9 %multiply_reduce_fusion.1 = (f32[64]{0:T(128)S(1)}, f32[64]{0:T(128)S(1)}, f32[64]{0:T(128)S(1)}) fusion(f32[128]{0:T(128)S(1)} %copy-done.21, f32[64,128,128]{2,1,0:T(8,128)S(1)} %fusion.19, s32[64]{0:T(128)S(1)} %copy-done.14, bf16[64,64,256]{2,1,0:T(8,128)(2,1)S(1)} %convolution_convert_fusion), kind=kOutput, calls=%fused_computation.5 | convolution fusion | flops 141680448 | bytes 5245184 | tf_op jit(solution)/shard_map/while/body/eval_jaxpr/ku,bul->bkl/dot_general | solution.py:89
  94.9 0.1 div.64
  95.0 0.1 copy.28
  95.1 0.1 div.67
  95.2 0.1 copy.29
  95.4 0.2 fusion.41
  95.6 72.8 %psum.7 = f32[2,2,512]{2,1,0:T(2,128)S(1)} all-reduce(f32[2,2,512]{2,1,0:T(2,128)S(1)} %fusion.41), channel_id=1, replica_groups=mesh['strip'=16,'date'=32] {'date'}, use_global_device_ids=true, to_apply=%region_8.9 | all-reduce | flops 2048 | bytes 16384 | tf_op jit(solution)/shard_map/psum | solution.py:184
  168.5 0.8 fusion.79
  (61 shorter events, 0.4 us)
Async XLA Ops:
  0.6 167.8 %copy-start = (f32[2,2,16,512]{3,2,1,0:T(8,128)S(1)}, f32[2,2,16,512]{3,2,1,0:T(8,128)}, u32[]{:S(2)}) copy-start(f32[2,2,16,512]{3,2,1,0:T(8,128)} %param.9) | copy-start | bytes 393220
  0.6 21.3 %copy-start.9 = (s32[32,2,2]{0,2,1:T(2,128)S(1)}, s32[32,2,2]{0,2,1:T(2,128)}, u32[]{:S(2)}) copy-start(s32[32,2,2]{0,2,1:T(2,128)} %param.14) | copy-start | bytes 1540
  5.0 19.7 %all-to-all-start = ((s32[32,1,2]{2,1,0:T(1,128)}), s32[32,1,2]{2,1,0:T(1,128)S(1)}, u32[]{:S(2)}, u32[]{:S(2)}) async-start(s32[32,1,2]{2,1,0:T(1,128)} %bitcast.18), calls=%async_computation | async-start | bytes 32768 | tf_op jit(solution)/shard_map/all_to_all | solution.py:120
  15.1 7.1 %copy-start.2 = (bf16[64,64]{1,0:T(8,128)(2,1)}, bf16[64,64]{1,0:T(8,128)(2,1)S(1)}, u32[]{:S(2)}) copy-start(bf16[64,64]{1,0:T(8,128)(2,1)S(1)} %get-tuple-element.86) | copy-start | bytes 24580
  22.1 0.9 copy-start.15
  22.1 4.0 %copy-start.1 = (bf16[16,64,128]{2,1,0:T(8,128)(2,1)S(1)}, bf16[16,64,128]{2,1,0:T(8,128)(2,1)}, u32[]{:S(2)}) copy-start(bf16[16,64,128]{2,1,0:T(8,128)(2,1)} %param.8) | copy-start | bytes 786436
  30.4 36.9 %all-to-all-start.1 = ((bf16[32,2,64,128]{3,2,1,0:T(8,128)(2,1)}), bf16[32,2,64,128]{3,2,1,0:T(8,128)(2,1)S(1)}, u32[]{:S(2)}, u32[]{:S(2)}) async-start(bf16[32,2,64,128]{3,2,1,0:T(8,128)(2,1)} %broadcast_select_fusion), calls=%async_computation.1 | async-start | bytes 2097152 | tf_op jit(solution)/shard_map/all_to_all | solution.py:123
  41.1 1.6 copy-start.11
  41.1 1.6 copy-start.19
  42.2 34.7 %copy-start.13 = (s32[64]{0:T(128)}, s32[64]{0:T(128)S(1)}, u32[]{:S(2)}) copy-start(s32[64]{0:T(128)S(1)} %compare_select_fusion.1) | copy-start | bytes 772
  67.3 9.4 %collective-permute-start = (bf16[32,2,8,128]{3,2,1,0:T(8,128)(2,1)S(1)}, bf16[32,2,8,128]{3,2,1,0:T(8,128)(2,1)S(1)}, u32[]{:S(2)}, u32[]{:S(2)}) collective-permute-start(bf16[32,2,8,128]{3,2,1,0:T(8,128)(2,1)S(1)} %get-tuple-element.68), channel_id=1, source_target_pairs={{0,32},{32,64},{64,96},{96,128},{128,160},{160,192},{192,224},{224... | collective-permute-start | bytes 393224 | tf_op jit(solution)/shard_map/ppermute | solution.py:19
  69.2 7.5 %collective-permute-start.1 = (bf16[32,2,8,128]{3,2,1,0:T(8,128)(2,1)S(1)}, bf16[32,2,8,128]{3,2,1,0:T(8,128)(2,1)S(1)}, u32[]{:S(2)}, u32[]{:S(2)}) collective-permute-start(bf16[32,2,8,128]{3,2,1,0:T(8,128)(2,1)S(1)} %get-tuple-element.69), channel_id=1, source_target_pairs={{32,0},{64,32},{96,64},{128,96},{160,128},{192,160},{224,192},{256... | collective-permute-start | bytes 393224 | tf_op jit(solution)/shard_map/ppermute | solution.py:21
  80.0 2.7 %copy-start.7 = (s32[32,2,64]{2,1,0:T(2,128)S(1)}, s32[32,2,64]{2,1,0:T(2,128)}, u32[]{:S(2)}) copy-start(s32[32,2,64]{2,1,0:T(2,128)} %get-tuple-element.87) | copy-start | bytes 49156
  80.0 2.7 %copy-start.8 = (s32[32,2,64]{2,1,0:T(2,128)S(1)}, s32[32,2,64]{2,1,0:T(2,128)}, u32[]{:S(2)}) copy-start(s32[32,2,64]{2,1,0:T(2,128)} %get-tuple-element.88) | copy-start | bytes 49156
  80.0 2.7 %copy-start.17 = (pred[32]{0:T(512)(128)(4,1)S(1)}, pred[32]{0:T(512)(128)(4,1)}, u32[]{:S(2)}) copy-start(pred[32]{0:T(512)(128)(4,1)} %get-tuple-element.46) | copy-start | bytes 100
  85.4 1.9 %copy-start.3 = (bf16[64,64]{1,0:T(8,128)(2,1)S(1)}, bf16[64,64]{1,0:T(8,128)(2,1)}, u32[]{:S(2)}) copy-start(bf16[64,64]{1,0:T(8,128)(2,1)} %copy-done.2) | copy-start | bytes 24580
  90.4 0.8 copy-start.4
  90.4 0.8 copy-start.5
  90.4 0.8 copy-start.6
  91.3 0.8 copy-start.14
  92.1 0.9 copy-start.21
  93.0 2.3 %copy-start.10 = (s32[32,2,2]{0,2,1:T(2,128)S(1)}, s32[32,2,2]{0,2,1:T(2,128)}, u32[]{:S(2)}) copy-start(s32[32,2,2]{0,2,1:T(2,128)} %param.14) | copy-start | bytes 1540
  93.0 2.3 %copy-start.18 = (f32[32]{0:T(128)S(1)}, f32[32]{0:T(128)}, u32[]{:S(2)}) copy-start(f32[32]{0:T(128)} %compare_convert_fusion) | copy-start | bytes 388
  93.0 2.3 %copy-start.16 = (s32[32]{0:T(128)S(1)}, s32[32]{0:T(128)}, u32[]{:S(2)}) copy-start(s32[32]{0:T(128)} %get-tuple-element.74) | copy-start | bytes 388
  93.0 2.3 %copy-start.20 = (s32[32]{0:T(128)S(1)}, s32[32]{0:T(128)}, u32[]{:S(2)}) copy-start(s32[32]{0:T(128)} %multiply_add_fusion) | copy-start | bytes 388
  95.3 74.0 %copy-start.12 = (f32[32,2,2]{0,2,1:T(2,128)}, f32[32,2,2]{0,2,1:T(2,128)S(1)}, u32[]{:S(2)}) copy-start(f32[32,2,2]{0,2,1:T(2,128)S(1)} %copy.31) | copy-start | bytes 1540
where the time goes:
time: 171 us; the launch traced here: 169 us
  blocking collectives  72.8 us (43%)
  starting transfers between devices  24.3 us (14%)
  waiting for transfers between devices  23.4 us (14%)
  other arithmetic  18.4 us (11%)
  local copies, waits for them, and re-layouts  12.2 us (7%)
  matrix products  9.96 us (6%)
  between operations  8.2 us (5%)
    psum x1, blocking collectives, body(): rhs_whole = lax.psum(partial_value, 'date')  72.8 us
    all_to_all x1, waiting for transfers between devices, body(): lax.all_to_all(picked, 'date', split_axis=0, concat_axis=0, tiled=True)  22.2 us
    all_to_all x1, starting transfers between devices, body(): lax.all_to_all(requests, 'date', split_axis=0, concat_axis=0, tiled=True)  9.95 us
    all_to_all x1, starting transfers between devices, body(): lax.all_to_all(picked, 'date', split_axis=0, concat_axis=0, tiled=True)  8.64 us
    another operation x5, other arithmetic  3.88 us
    ppermute x1, starting transfers between devices, padded(): lax.ppermute(head, axis, [((i + 1) % count, i) for i in range(ends)])  3.82 us
  transfers between devices with their start and end apart: 4, of which 2 were waited for; matrix products, arithmetic and copies ran while one was open for 7% of the time, Pallas kernels for 0%

commit v1 on v0

v1 whole, which is shorter than its diff:
```python
import math

import jax
import jax.numpy as jnp
import ml_dtypes
import numpy as np
from jax import lax
from jax.experimental import pallas as pl
from jax.experimental.pallas import tpu as pltpu
from jax.sharding import PartitionSpec as P

SMAX = 8
CHIP = 64
LANES = 128
BATCH = 4
HIGH = lax.Precision.HIGHEST
F32 = jnp.float32
BF16 = jnp.bfloat16


def make_tables():
    counter = np.arange(CHIP)
    turn = 2.0 * math.pi * (counter[:, None] * counter[None, :] % CHIP) / CHIP
    cosine, sine = np.cos(turn), -np.sin(turn)
    zero = np.zeros((CHIP, CHIP))
    two = np.eye(2)
    columns = np.concatenate([np.kron(two, cosine), np.kron(two, sine)], axis=1)
    rows = np.block([[cosine, -sine], [sine, cosine]])
    over = 2 * CHIP
    places = np.arange(over)
    displace = ((places + CHIP) % over - CHIP) * 0.5
    odd = np.where(places == CHIP, 0.0, displace)
    signed = np.where(counter < CHIP // 2, counter, counter - CHIP)
    basis = np.exp(2j * math.pi * signed[:, None] * places[None, :] / over)
    basis[CHIP // 2] = np.cos(math.pi * places / 2)
    form = np.imag((basis.conj() * odd) @ basis.T) / over
    ends = -0.25 * np.outer((-1.0) ** counter, (-1.0) ** counter)
    left = np.block([[ends, -2.0 * form], [zero, ends]])
    ends2, form2 = np.kron(two, ends), np.kron(two, -2.0 * form.T)
    right = np.block([[ends2, np.zeros((LANES, LANES))], [form2, ends2]])
    return tuple(a.astype(ml_dtypes.bfloat16) for a in (columns, rows, left, right))


def dot(a, b, precision=None):
    return lax.dot_general(
        a, b, (((1,), (0,)), ((), ())), precision=precision, preferred_element_type=F32
    )


def dot_nt(a, b, precision=None):
    return lax.dot_general(
        a, b, (((1,), (1,)), ((), ())), precision=precision, preferred_element_type=F32
    )


def same_chip():
    row = lax.broadcasted_iota(jnp.int32, (LANES, LANES), 0)
    lane = lax.broadcasted_iota(jnp.int32, (LANES, LANES), 1)
    return ((row < CHIP) == (lane < CHIP)).astype(F32)


def pack_kernel(
    first_ref, block_ref, second_ref, count_ref, shifts_ref, anchors_ref, images_ref,
    send_ref, cut_ref, near_ref, facts_ref, tally_ref,
):
    dates = images_ref.shape[0]
    blocks = send_ref.shape[0]
    row = lax.broadcasted_iota(jnp.int32, (LANES, LANES), 0)
    lane = lax.broadcasted_iota(jnp.int32, (LANES, LANES), 1)
    column = lane + jnp.where(lane < CHIP, anchors_ref[0], anchors_ref[1] - CHIP)
    pick = (row == column).astype(F32).astype(BF16)
    sums = []
    for date in range(dates):
        window = dot(images_ref[date], pick)
        cut_ref[date] = window
        sums.append(jnp.sum(window, axis=0, keepdims=True))
    means = dot(jnp.concatenate(sums, axis=0), same_chip(), HIGH) * (1.0 / (CHIP * CHIP))
    for date in range(dates):
        near_ref[date] = (cut_ref[date] - means[date : date + 1]).astype(BF16)
    facts_ref[...] = jnp.zeros(facts_ref.shape, F32)
    for block in range(blocks):
        tally_ref[block] = 0
    place = lax.broadcasted_iota(jnp.int32, (1, LANES), 1)

    def one_slot(slot, carry):
        block = block_ref[slot, 0]
        rank = tally_ref[block]
        tally_ref[block] = rank + 1
        first = first_ref[slot]
        at = pl.multiple_of(rank * CHIP, CHIP)
        send_ref[block, pl.ds(at, CHIP), :] = near_ref[first]
        fact = jnp.where(place == 0, 1, 0)
        for index, value in enumerate(
            (
                second_ref[slot], first, shifts_ref[slot, 0, 0], shifts_ref[slot, 1, 0],
                shifts_ref[slot, 0, 1], shifts_ref[slot, 1, 1],
            )
        ):
            fact = jnp.where(place == index + 1, value, fact)
        facts_ref[pl.ds(block * 8 + rank, 1), :] = fact.astype(F32)
        return carry

    lax.fori_loop(0, count_ref[0], one_slot, 0)
    send_ref[:, 2 * CHIP : 2 * CHIP + 8, :] = (
        facts_ref[...].reshape(blocks, 8, LANES).astype(BF16)
    )


def match_kernel(
    anchors_ref, recv_ref, images_ref, above_ref, below_ref,
    columns_ref, rows_ref, left_ref, right_ref, out_ref,
    framed_ref, facts_ref, whole_ref, scalar_ref, list_ref, data_ref, section_ref,
    energy_ref, tall_ref, wide_ref, copy_sem,
):
    blocks = recv_ref.shape[0]
    dates = images_ref.shape[0]
    facts_ref[...] = recv_ref[:, 2 * CHIP : 2 * CHIP + 8, :].astype(F32).reshape(blocks * 8, LANES)
    whole_ref[...] = jnp.zeros(whole_ref.shape, jnp.int32)
    for rank in range(2):
        whole_ref[rank * blocks : (rank + 1) * blocks, :] = facts_ref[
            pl.ds(rank, blocks, stride=8), :
        ].astype(jnp.int32)
    copy = pltpu.make_async_copy(whole_ref, scalar_ref, copy_sem)
    copy.start()
    framed_ref[:, :SMAX, :] = above_ref[...].astype(F32)
    framed_ref[:, SMAX : SMAX + CHIP, :] = images_ref[...].astype(F32)
    framed_ref[:, SMAX + CHIP :, :] = below_ref[...].astype(F32)
    for ref in (energy_ref, tall_ref, wide_ref):
        ref[...] = jnp.zeros(ref.shape, F32)
    copy.wait()

    def note(slot, count):
        list_ref[count] = slot
        return count + scalar_ref[slot, 0]

    count = lax.fori_loop(0, 2 * blocks, note, 0)
    spare = 2 * CHIP // 2
    for extra in range(BATCH):
        list_ref[count + extra] = spare
    lane = lax.broadcasted_iota(jnp.int32, (1, LANES), 1)
    low = lane < CHIP
    ones = same_chip()

    def one_batch(turn, carry):
        rows_of = []
        windows = []
        for s in range(BATCH):
            slot = list_ref[turn * BATCH + s]
            rows_of.append(slot)
            source = jnp.where(slot == spare, 0, slot)
            rank = jnp.where(source >= blocks, 1, 0)
            second = scalar_ref[slot, 1]
            pieces = []
            starts = []
            for chip in range(2):
                down = scalar_ref[slot, 3 + 2 * chip] + SMAX
                start = scalar_ref[slot, 4 + 2 * chip] + anchors_ref[chip] - chip * CHIP
                piece = framed_ref[second, pl.ds(down, CHIP), :]
                pieces.append(pltpu.roll(piece, lax.rem(LANES - start, LANES), 1))
                starts.append(start)
            column = lane + jnp.where(low, starts[0], starts[1])
            inside = (column >= 0) & (column < LANES)
            window = jnp.where(low, pieces[0], pieces[1])
            windows.append(jnp.where(inside, window, 0.0))
            data_ref[s * 2 * CHIP : s * 2 * CHIP + CHIP, :] = recv_ref[
                source - rank * blocks, pl.ds(pl.multiple_of(rank * CHIP, CHIP), CHIP), :
            ]
        sums = [jnp.sum(w, axis=0, keepdims=True) for w in windows]
        sums += [jnp.zeros((1, LANES), F32)] * (8 - BATCH)
        means = dot(jnp.concatenate(sums, axis=0), ones, HIGH) * (1.0 / (CHIP * CHIP))
        for s in range(BATCH):
            data_ref[s * 2 * CHIP + CHIP : (s + 1) * 2 * CHIP, :] = (
                windows[s] - means[s : s + 1]
            ).astype(BF16)
        section_ref[...] = dot(data_ref[...], columns_ref[...]).astype(BF16)
        for s in range(BATCH):
            near = section_ref[s * 2 * CHIP : s * 2 * CHIP + CHIP, :]
            far = section_ref[s * 2 * CHIP + CHIP : (s + 1) * 2 * CHIP, :]
            real = jnp.concatenate([near[:, :LANES], far[:, :LANES]], axis=1)
            imag = jnp.concatenate([near[:, LANES:], far[:, LANES:]], axis=1)
            spectrum = dot(rows_ref[...], jnp.concatenate([real, imag], axis=0))
            near_re, far_re = spectrum[:CHIP, :LANES], spectrum[:CHIP, LANES:]
            near_im, far_im = spectrum[CHIP:, :LANES], spectrum[CHIP:, LANES:]
            cross_re = near_re * far_re + near_im * far_im
            cross_im = near_im * far_re - near_re * far_im
            short_re, short_im = cross_re.astype(BF16), cross_im.astype(BF16)
            tall = dot(left_ref[...], jnp.concatenate([short_re, short_im], axis=0))
            wide = dot(jnp.concatenate([short_re, short_im], axis=1), right_ref[...])
            power = cross_re * cross_re + cross_im * cross_im
            tall = cross_re * tall[:CHIP] + cross_im * tall[CHIP:]
            wide = cross_re * wide[:, :LANES] + cross_im * wide[:, LANES:]
            half = CHIP // 2
            middle = jnp.where(lane % CHIP == half, 0.0, 0.5 * power[half : half + 1])
            at = pl.ds(rows_of[s], 1)
            energy_ref[at, :] = jnp.sum(power, axis=0, keepdims=True) - middle
            tall_ref[at, :] = jnp.sum(tall, axis=0, keepdims=True)
            wide_ref[at, :] = jnp.sum(wide, axis=0, keepdims=True) - 0.5 * wide[half : half + 1]
        return carry

    lax.fori_loop(0, (count + BATCH - 1) // BATCH, one_batch, 0)

    lane8 = lax.broadcasted_iota(jnp.int32, (8, LANES), 1)
    row8 = lax.broadcasted_iota(jnp.int32, (8, LANES), 0)
    weights = jnp.where((row8 == 0) & (lane8 % CHIP == CHIP // 2), 0.5, 1.0)
    stack = []
    for ref in (energy_ref, tall_ref, wide_ref):
        value = ref[:CHIP, :]
        stack += [jnp.where(low, value, 0.0), jnp.where(low, 0.0, value)]
    found = dot_nt(weights, jnp.concatenate(stack, axis=0), HIGH)
    norm = found[0:1, :LANES] + 1e-6
    tall = found[0:1, LANES : 2 * LANES] / norm
    wide = found[1:2, 2 * LANES :] / norm
    whole = whole_ref[:CHIP, :].astype(F32).astype(BF16)
    choose = (lane8 == row8).astype(F32).astype(BF16)
    fact = dot_nt(choose, jnp.concatenate([whole, whole], axis=0))
    live = fact[0:1] > 0.5
    down = jnp.where(live, jnp.where(low, fact[3:4], fact[5:6]) + tall, 0.0)
    across = jnp.where(live, jnp.where(low, fact[4:5], fact[6:7]) + wide, 0.0)
    row = lax.broadcasted_iota(jnp.int32, (LANES, LANES), 0).astype(F32)
    base = (lax.rem(lax.axis_index("date"), LANES // dates) * dates).astype(F32)
    chosen = (row == fact[1:2] + base).astype(F32)
    value = jnp.where(row8 < 6, down, across)
    value = jnp.where((row8 >= 4) & ((row8 % 2 == 0) == (lane8 < CHIP)), value, 0.0)
    result = dot_nt(value, chosen, HIGH)
    result = jnp.where(row8 == 0, down, result)
    result = jnp.where(row8 == 1, across, result)
    result = jnp.where(row8 == 2, fact[2:3], result)
    for block in range(blocks):
        out_ref[block] = result


def series_kernel(
    block_ref, count_ref, result_ref, inverse_ref, turned_ref, offsets_ref, series_ref, tally_ref
):
    blocks = result_ref.shape[0]
    slots = block_ref.shape[0]
    dates = inverse_ref.shape[2]
    me = lax.axis_index("date")
    lane8 = lax.broadcasted_iota(jnp.int32, (8, LANES), 1)
    for block in range(blocks):
        tally_ref[block] = 0
    for slot in range(slots):
        block = block_ref[slot, 0]
        rank = tally_ref[block]
        tally_ref[block] = rank + 1
        turn = rank * blocks + me
        value = pltpu.roll(result_ref[block], lax.rem(2 * LANES - turn, LANES), 1)
        other = pltpu.roll(value, LANES - CHIP + 1, 1)
        value = jnp.where(lane8 == 0, value, other)
        value = jnp.where(slot < count_ref[0], value, 0.0)
        offsets_ref[slot] = value[:2, :2]
    sums = [jnp.zeros((8, LANES), F32) for _ in range(dates)]
    per = LANES // dates
    groups = [jnp.zeros((8, LANES), F32) for _ in range(blocks // per)]
    for block in range(blocks):
        value = result_ref[block]
        first = jnp.broadcast_to(value[2:3], (8, LANES))
        for date in range(dates):
            sums[date] = sums[date] + jnp.where(first == date, value, 0.0)
        groups[block // per] = groups[block // per] + value
    low = lax.broadcasted_iota(jnp.int32, (dates, LANES), 1) < CHIP
    ones = jnp.ones((8, LANES), F32)
    for axis in range(2):
        own = jnp.zeros((dates, LANES), F32)
        for date in range(dates):
            own = own + turned_ref[axis, date] * sums[date][axis : axis + 1]
        for chip in range(2):
            total = jnp.where(low if chip == 0 else ~low, -own, 0.0)
            at = 4 + 2 * axis + chip
            for g, group in enumerate(groups):
                total = total + inverse_ref[axis, chip, :, g * LANES : (g + 1) * LANES] * group[at : at + 1]
            series_ref[axis, chip : chip + 1, :] = dot_nt(ones, total, HIGH)[0:1, :]


def body(images, inverse_blocks, pair_first, pair_block, pair_second, pair_count, shifts, anchors):
    blocks = lax.axis_size("date")
    strips = lax.axis_size("strip")
    dates, length, columns = images.shape
    slots = pair_first.shape[0]
    smem = pl.BlockSpec(memory_space=pltpu.SMEM)
    vmem = pl.BlockSpec(memory_space=pltpu.VMEM)
    params = pltpu.CompilerParams(vmem_limit_bytes=48 * 2**20)
    ends = strips - 1
    above = lax.ppermute(
        images[:, length - SMAX :, :], "strip", [(i, i + 1) for i in range(ends)]
    )
    below = lax.ppermute(images[:, :SMAX, :], "strip", [(i + 1, i) for i in range(ends)])
    send = pl.pallas_call(
        pack_kernel,
        out_shape=jax.ShapeDtypeStruct((blocks, 2 * length + 8, columns), BF16),
        in_specs=[smem] * 6 + [vmem],
        out_specs=vmem,
        scratch_shapes=[
            pltpu.VMEM((dates, length, columns), F32),
            pltpu.VMEM((dates, length, columns), BF16),
            pltpu.VMEM((blocks * 8, columns), F32),
            pltpu.SMEM((blocks,), jnp.int32),
        ],
        compiler_params=params,
    )(pair_first, pair_block, pair_second, pair_count, shifts, anchors, images)
    recv = lax.all_to_all(send, "date", split_axis=0, concat_axis=0, tiled=True)
    tables = make_tables()
    result = pl.pallas_call(
        match_kernel,
        out_shape=jax.ShapeDtypeStruct((blocks, 8, columns), F32),
        in_specs=[smem] + [vmem] * 8,
        out_specs=vmem,
        scratch_shapes=[
            pltpu.VMEM((dates, length + 2 * SMAX, columns), F32),
            pltpu.VMEM((blocks * 8, columns), F32),
            pltpu.VMEM((CHIP + 8, columns), jnp.int32),
            pltpu.SMEM((CHIP + 8, columns), jnp.int32),
            pltpu.SMEM((CHIP + 8,), jnp.int32),
            pltpu.VMEM((BATCH * 2 * length, columns), BF16),
            pltpu.VMEM((BATCH * 2 * length, 2 * columns), BF16),
            pltpu.VMEM((CHIP + 8, columns), F32),
            pltpu.VMEM((CHIP + 8, columns), F32),
            pltpu.VMEM((CHIP + 8, columns), F32),
            pltpu.SemaphoreType.DMA,
        ],
        compiler_params=params,
    )(anchors, recv, images, above, below, *[jnp.asarray(t) for t in tables])
    result = lax.all_to_all(result, "date", split_axis=0, concat_axis=0, tiled=True)
    turned = inverse_blocks.reshape(2, 2, dates, blocks, dates).transpose(0, 4, 2, 1, 3)
    turned = jnp.concatenate([turned, turned], axis=4)
    turned = jnp.pad(turned, ((0, 0),) * 4 + ((0, CHIP - 2 * blocks),))
    turned = turned.reshape(2, dates, dates, LANES)
    return pl.pallas_call(
        series_kernel,
        out_shape=(
            jax.ShapeDtypeStruct((slots, 2, 2), F32),
            jax.ShapeDtypeStruct((2, 2, dates), F32),
        ),
        in_specs=[smem] * 2 + [vmem] * 3,
        out_specs=(vmem, vmem),
        scratch_shapes=[pltpu.SMEM((blocks,), jnp.int32)],
        compiler_params=params,
    )(pair_block, pair_count, result, inverse_blocks, turned)


def solution(mesh):
    return jax.shard_map(
        body,
        mesh=mesh,
        in_specs=(
            P("date", "strip", None),
            P(None, "strip", "date", None),
            P("date"),
            P("date", None),
            P("date"),
            P("date"),
            P("date", None, "strip"),
            P("strip"),
        ),
        out_specs=(P("date", None, "strip"), P(None, "strip", "date")),
        check_vma=False,
    )
```

time: 171 us -> 88.9 us (0.52)
  blocking collectives: 72.8 us -> 0 us
  other arithmetic: 18.4 us -> 0.23 us
  Pallas kernels: 0 us -> 16.6 us
  waiting for transfers between devices: 23.4 us -> 34 us
  matrix products: 9.96 us -> 0 us
  between operations: 8.2 us -> 1.45 us
  local copies, waits for them, and re-layouts: 12.2 us -> 6.89 us
  starting transfers between devices: 24.3 us -> 29.2 us
    psum x1 -> x0, blocking collectives: 72.8 us -> none  [body(): rhs_whole = lax.psum(partial_value, 'date')]
    pallas_call x0 -> x3, Pallas kernels: none -> 16.6 us  [the longest x1 11.5 us: body(): pl.pallas_call(match_kernel, out_shape=jax.ShapeDtypeStruct((blocks, 8, c...]
    dot_general x12 -> x0, matrix products: 9.96 us -> none  [the longest x1 2.68 us: one_turn(): jnp.einsum('pcif,pcfj->pcij', row_cut, col_pick, preferred_element_type=j...]
    all_to_all x2, waiting for transfers between devices: 23.4 us -> 31.2 us  [the longest x1 22.9 us: body(): recv = lax.all_to_all(send, 'date', split_axis=0, concat_axis=0, tiled=True)]
    all_to_all x2, starting transfers between devices: 18.6 us -> 24.9 us  [the longest x1 14.8 us: body(): lax.all_to_all(result, 'date', split_axis=0, concat_axis=0, tiled=True)]
    another operation x7 -> x0, other arithmetic: 6.03 us -> none
    gather x3 -> x0, local copies, waits for them, and re-layouts: 5.1 us -> none  [the longest x1 2.67 us: one_turn(): regions_turn = jnp.take(regions, slots_turn, axis=0)]
    unnamed x45 -> x24, local copies, waits for them, and re-layouts: 0.12 us -> 4.45 us
  transfers between devices with their start and end apart: 4 -> 4, of which waited for: 2 -> 3; matrix products, arithmetic and copies ran while one was open for 7% -> 2% of each run, Pallas kernels for 0% -> 0%
where the time goes in v1:
time: 88.9 us; the launch traced here: 88.4 us
  waiting for transfers between devices  34 us (38%)
  starting transfers between devices  29.2 us (33%)
  Pallas kernels  16.6 us (19%)
  local copies, waits for them, and re-layouts  6.89 us (8%)
  between operations  1.45 us (2%)
    all_to_all x1, waiting for transfers between devices, body(): recv = lax.all_to_all(send, 'date', split_axis=0, concat_axis=0, tiled=True)  22.9 us
    all_to_all x1, starting transfers between devices, body(): lax.all_to_all(result, 'date', split_axis=0, concat_axis=0, tiled=True)  14.8 us
    pallas_call x1, Pallas kernels, body(): pl.pallas_call(match_kernel, out_shape=jax.ShapeDtypeStruct((blocks, 8, c...  11.5 us
    all_to_all x1, starting transfers between devices, body(): recv = lax.all_to_all(send, 'date', split_axis=0, concat_axis=0, tiled=True)  10.1 us
    all_to_all x1, waiting for transfers between devices, body(): lax.all_to_all(result, 'date', split_axis=0, concat_axis=0, tiled=True)  8.37 us
    unnamed x24, local copies, waits for them, and re-layouts  4.45 us
    pallas_call x1, Pallas kernels, body(): pl.pallas_call(pack_kernel, out_shape=jax.ShapeDtypeStruct((blocks, 2 * l...  3.29 us
    ppermute x1, waiting for transfers between devices, body(): lax.ppermute(images[:, length - SMAX:, :], 'strip', [(i, i + 1) for i in...  2.81 us
  transfers between devices with their start and end apart: 4, of which 3 were waited for; matrix products, arithmetic and copies ran while one was open for 2% of the time, Pallas kernels for 0%

profile of v1, /device:TPU:448, one launch (start us, length us, event | category | flops | bytes accessed | tf_op | source)
XLA Modules:
  0.0 88.4 jit_solution(14588405443079429817)
XLA Ops:
  0.6 0.0 copy-start.5
  0.6 0.0 copy-start.8
  1.3 0.7 copy.34.block_ref
  2.1 0.8 copy.32.shifts_ref
  2.8 0.0 copy-start
  2.8 0.9 %copy-done = bf16[16,64,128]{2,1,0:T(8,128)(2,1)S(1)} copy-done((bf16[16,64,128]{2,1,0:T(8,128)(2,1)S(1)}, bf16[16,64,128]{2,1,0:T(8,128)(2,1)}, u32[]{:S(2)}) %copy-start) | copy-done | bytes 262168
  3.8 0.0 copy-start.7
  3.8 0.7 copy-done.7
  4.4 0.0 copy-start.9
  4.4 0.7 copy-done.9
  5.1 0.0 copy-start.10
  5.1 0.7 copy-done.10
  5.8 0.0 copy-start.1
  5.8 0.0 copy-start.3
  5.8 0.0 copy-start.4
  5.8 0.0 copy-start.6
  5.8 3.3 %shard_map.131 = bf16[32,136,128]{2,1,0:T(8,128)(2,1)} custom-call(s32[32]{0:T(128)S(1)} %copy-done.9, s32[32,1]{1,0:T(8,128)S(1)} %copy.34.block_ref, s32[32]{0:T(128)S(1)} %copy-done.10, s32[1]{0:T(128)S(6)} %copy.36.count_ref, s32[32,2,2]{2,1,0:T(2,128)S(1)} %copy.32.shifts_ref, s32[2]{0:T(128)S(1)} %copy-done.7, bf16[16,64,128]{2,1,0:T(8,128)(2,1)S(1)} %copy-done), custom_call_target="tpu_custom_call" | custom-call | tf_op jit(solution)/shard_map/pallas_call | solution.py:288
  9.1 0.0 copy-start.2
  9.1 10.1 %all-to-all-start = ((bf16[32,136,128]{2,1,0:T(8,128)(2,1)}), bf16[32,136,128]{2,1,0:T(8,128)(2,1)S(1)}, u32[]{:S(2)}, u32[]{:S(2)}) async-start(bf16[32,136,128]{2,1,0:T(8,128)(2,1)} %shard_map.131), calls=%async_computation | async-start | bytes 2228224 | tf_op jit(solution)/shard_map/all_to_all | solution.py:301
  19.1 0.0 copy-done.1
  19.2 1.9 %collective-permute-start.1 = (bf16[16,8,128]{2,1,0:T(8,128)(2,1)S(1)}, bf16[16,8,128]{2,1,0:T(8,128)(2,1)S(1)}, u32[]{:S(2)}, u32[]{:S(2)}) collective-permute-start(bf16[16,8,128]{2,1,0:T(8,128)(2,1)S(1)} %get-tuple-element.10), channel_id=1, source_target_pairs={{32,0},{64,32},{96,64},{128,96},{160,128},{192,160},{224,192},{256... | collective-permute-start | bytes 98312 | tf_op jit(solution)/shard_map/ppermute | solution.py:287
  21.1 2.4 %collective-permute-start = (bf16[16,8,128]{2,1,0:T(8,128)(2,1)S(1)}, bf16[16,8,128]{2,1,0:T(8,128)(2,1)S(1)}, u32[]{:S(2)}, u32[]{:S(2)}) collective-permute-start(bf16[16,8,128]{2,1,0:T(8,128)(2,1)S(1)} %get-tuple-element.11), channel_id=1, source_target_pairs={{0,32},{32,64},{64,96},{96,128},{128,160},{160,192},{192,224},{224... | collective-permute-start | bytes 98312 | tf_op jit(solution)/shard_map/ppermute | solution.py:284
  23.5 0.0 collective-permute-done.1.below_ref
  23.5 2.8 %collective-permute-done.above_ref = bf16[16,8,128]{2,1,0:T(8,128)(2,1)S(1)} collective-permute-done((bf16[16,8,128]{2,1,0:T(8,128)(2,1)S(1)}, bf16[16,8,128]{2,1,0:T(8,128)(2,1)S(1)}, u32[]{:S(2)}, u32[]{:S(2)}) %collective-permute-start) | collective-permute-done | bytes 32800 | tf_op jit(solution)/shard_map/ppermute | solution.py:284
  26.3 22.9 %all-to-all-done.recv_ref = bf16[32,136,128]{2,1,0:T(8,128)(2,1)S(1)} async-done(((bf16[32,136,128]{2,1,0:T(8,128)(2,1)}), bf16[32,136,128]{2,1,0:T(8,128)(2,1)S(1)}, u32[]{:S(2)}, u32[]{:S(2)}) %all-to-all-start) | async-done | bytes 1114144 | tf_op jit(solution)/shard_map/all_to_all | solution.py:301
  49.2 0.0 copy-done.5
  49.2 0.0 copy-done.8
  49.2 0.0 copy-done.3
  49.2 0.0 copy-done.4
  49.2 0.0 copy-done.6
  49.2 11.5 %shard_map.132 = f32[32,8,128]{2,1,0:T(8,128)} custom-call(s32[2]{0:T(128)S(1)} %copy-done.8, bf16[32,136,128]{2,1,0:T(8,128)(2,1)S(1)} %all-to-all-done.recv_ref, bf16[16,64,128]{2,1,0:T(8,128)(2,1)S(1)} %copy-done.1, bf16[16,8,128]{2,1,0:T(8,128)(2,1)S(1)} %collective-permute-done.above_ref, bf16[16,8,128]{2,1,0:T(8,128)(2,1)S(1)} %collective-permute-done.1.below_ref, ...), custom_call_target="tpu_custom_call" | custom-call | tf_op jit(solution)/shard_map/pallas_call | solution.py:303
  60.8 14.8 %all-to-all-start.1 = ((f32[32,8,128]{2,1,0:T(8,128)}), f32[32,8,128]{2,1,0:T(8,128)S(1)}, u32[]{:S(2)}, u32[]{:S(2)}) async-start(f32[32,8,128]{2,1,0:T(8,128)} %shard_map.132), calls=%async_computation.1 | async-start | bytes 262144 | tf_op jit(solution)/shard_map/all_to_all | solution.py:323
  75.6 0.0 copy-done.2
  75.6 0.4 reshape.10
  75.9 0.2 pad_maximum_fusion
  76.2 1.1 %copy.33 = f32[2,16,16,2,64]{4,3,2,1,0:T(2,128)S(1)} copy(f32[2,16,16,2,64]{1,4,2,3,0:T(8,128)S(1)} %pad_maximum_fusion) | data formatting | bytes 524288 | tf_op jit(solution)/shard_map/concatenate | solution.py:325
  77.3 0.3 reshape.11.turned_ref
  77.6 8.4 %all-to-all-done.1.result_ref = f32[32,8,128]{2,1,0:T(8,128)S(1)} async-done(((f32[32,8,128]{2,1,0:T(8,128)}), f32[32,8,128]{2,1,0:T(8,128)S(1)}, u32[]{:S(2)}, u32[]{:S(2)}) %all-to-all-start.1) | async-done | bytes 131104 | tf_op jit(solution)/shard_map/all_to_all | solution.py:323
  86.0 1.8 %shard_map.133 = (f32[32,2,2]{2,1,0:T(2,128)S(1)}, f32[2,2,16]{2,1,0:T(2,128)}) custom-call(s32[32,1]{1,0:T(8,128)S(1)} %copy.34.block_ref, s32[1]{0:T(128)S(6)} %copy.36.count_ref, f32[32,8,128]{2,1,0:T(8,128)S(1)} %all-to-all-done.1.result_ref, f32[2,2,16,512]{3,2,1,0:T(8,128)S(1)} %copy-done.2, f32[2,16,16,128]{3,2,1,0:T(8,128)S(1)} %reshape.11.turned_ref), custom_call_target="tpu_custom_call" | custom-call | tf_op jit(solution)/shard_map/pallas_call | solution.py:328
  87.7 0.7 copy.35
  (1 shorter events, 0.0 us)
Async XLA Ops:
  0.6 48.6 %copy-start.5 = (bf16[128,128]{1,0:T(8,128)(2,1)S(1)}, bf16[128,128]{1,0:T(8,128)(2,1)}, u32[]{:S(2)}) copy-start(bf16[128,128]{1,0:T(8,128)(2,1)} %constant.11.clone.left_ref) | copy-start | bytes 98308
  0.6 48.6 %copy-start.8 = (s32[2]{0:T(128)S(1)}, s32[2]{0:T(128)}, u32[]{:S(2)}) copy-start(s32[2]{0:T(128)} %anchors_ref.3) | copy-start | bytes 28
  2.8 1.0 %copy-start = (bf16[16,64,128]{2,1,0:T(8,128)(2,1)S(1)}, bf16[16,64,128]{2,1,0:T(8,128)(2,1)}, u32[]{:S(2)}) copy-start(bf16[16,64,128]{2,1,0:T(8,128)(2,1)} %images_ref.3) | copy-start | bytes 786436
  3.8 0.7 copy-start.7
  4.4 0.7 copy-start.9
  5.1 0.7 copy-start.10
  5.8 13.4 %copy-start.1 = (bf16[16,64,128]{2,1,0:T(8,128)(2,1)S(1)}, bf16[16,64,128]{2,1,0:T(8,128)(2,1)}, u32[]{:S(2)}) copy-start(bf16[16,64,128]{2,1,0:T(8,128)(2,1)} %images_ref.3) | copy-start | bytes 786436
  5.8 43.4 %copy-start.3 = (bf16[256,256]{1,0:T(8,128)(2,1)S(1)}, bf16[256,256]{1,0:T(8,128)(2,1)}, u32[]{:S(2)}) copy-start(bf16[256,256]{1,0:T(8,128)(2,1)} %constant.12.clone.right_ref) | copy-start | bytes 393220
  5.8 43.5 %copy-start.4 = (bf16[128,256]{1,0:T(8,128)(2,1)S(1)}, bf16[128,256]{1,0:T(8,128)(2,1)}, u32[]{:S(2)}) copy-start(bf16[128,256]{1,0:T(8,128)(2,1)} %constant.4.clone.columns_ref) | copy-start | bytes 196612
  5.8 43.5 %copy-start.6 = (bf16[128,128]{1,0:T(8,128)(2,1)S(1)}, bf16[128,128]{1,0:T(8,128)(2,1)}, u32[]{:S(2)}) copy-start(bf16[128,128]{1,0:T(8,128)(2,1)} %constant.10.clone.rows_ref) | copy-start | bytes 98308
  9.1 66.5 %copy-start.2 = (f32[2,2,16,512]{3,2,1,0:T(8,128)S(1)}, f32[2,2,16,512]{3,2,1,0:T(8,128)}, u32[]{:S(2)}) copy-start(f32[2,2,16,512]{3,2,1,0:T(8,128)} %inverse_ref.1) | copy-start | bytes 393220
  9.1 40.1 %all-to-all-start = ((bf16[32,136,128]{2,1,0:T(8,128)(2,1)}), bf16[32,136,128]{2,1,0:T(8,128)(2,1)S(1)}, u32[]{:S(2)}, u32[]{:S(2)}) async-start(bf16[32,136,128]{2,1,0:T(8,128)(2,1)} %shard_map.131), calls=%async_computation | async-start | bytes 2228224 | tf_op jit(solution)/shard_map/all_to_all | solution.py:301
  19.2 4.3 %collective-permute-start.1 = (bf16[16,8,128]{2,1,0:T(8,128)(2,1)S(1)}, bf16[16,8,128]{2,1,0:T(8,128)(2,1)S(1)}, u32[]{:S(2)}, u32[]{:S(2)}) collective-permute-start(bf16[16,8,128]{2,1,0:T(8,128)(2,1)S(1)} %get-tuple-element.10), channel_id=1, source_target_pairs={{32,0},{64,32},{96,64},{128,96},{160,128},{192,160},{224,192},{256... | collective-permute-start | bytes 98312 | tf_op jit(solution)/shard_map/ppermute | solution.py:287
  21.1 5.2 %collective-permute-start = (bf16[16,8,128]{2,1,0:T(8,128)(2,1)S(1)}, bf16[16,8,128]{2,1,0:T(8,128)(2,1)S(1)}, u32[]{:S(2)}, u32[]{:S(2)}) collective-permute-start(bf16[16,8,128]{2,1,0:T(8,128)(2,1)S(1)} %get-tuple-element.11), channel_id=1, source_target_pairs={{0,32},{32,64},{64,96},{96,128},{128,160},{160,192},{192,224},{224... | collective-permute-start | bytes 98312 | tf_op jit(solution)/shard_map/ppermute | solution.py:284
  60.8 25.2 %all-to-all-start.1 = ((f32[32,8,128]{2,1,0:T(8,128)}), f32[32,8,128]{2,1,0:T(8,128)S(1)}, u32[]{:S(2)}, u32[]{:S(2)}) async-start(f32[32,8,128]{2,1,0:T(8,128)} %shard_map.132), calls=%async_computation.1 | async-start | bytes 262144 | tf_op jit(solution)/shard_map/all_to_all | solution.py:323

commit v2 on v1

v2 whole, which is shorter than its diff:
```python
import math

import jax
import jax.numpy as jnp
import ml_dtypes
import numpy as np
from jax import lax
from jax.experimental import pallas as pl
from jax.experimental.pallas import tpu as pltpu
from jax.sharding import PartitionSpec as P

SMAX = 8
CHIP = 64
LANES = 128
BATCH = 8
HIGH = lax.Precision.HIGHEST
F32 = jnp.float32
BF16 = jnp.bfloat16


def make_tables():
    half = CHIP // 2
    counter = np.arange(CHIP)
    freq = counter % half
    def basis(places, length):
        turn = 2.0 * math.pi * freq[:, None] * places[None, :] / length
        value = np.where(counter[:, None] < half, np.cos(turn), np.sin(turn))
        value[half] = np.cos(2.0 * math.pi * half * places / length)
        return value
    scale = np.where(freq == 0, 1.0, math.sqrt(2.0))[:, None]
    forward = basis(counter, CHIP) * scale
    cosine, sine = forward[:half].T, forward[half:].T
    zero = np.zeros((CHIP, half))
    def spread(block):
        return np.concatenate([np.concatenate([block, zero], 1), np.concatenate([zero, block], 1)], 0)
    nyquist = cosine.copy(); nyquist[:, 0] = sine[:, 0]
    plain = sine.copy(); plain[:, 0] = 0.0
    near = np.concatenate([spread(cosine), spread(sine)], 1)
    far = np.concatenate([spread(cosine), spread(nyquist), spread(plain), spread(plain)], 1)
    places = np.arange(2 * CHIP)
    displace = ((places + CHIP) % (2 * CHIP) - CHIP) * 0.5
    wave = basis(places, 2 * CHIP)
    form = (wave * displace) @ wave.T / (2 * CHIP)
    cc, cs, sc, ss = form[:half, :half], form[:half, half:], form[half:, :half], form[half:, half:]
    two = np.eye(2)
    across = np.block([[np.kron(two, cc), np.kron(two, cs)], [np.kron(two, sc), np.kron(two, ss)]])
    tables = (near, far, forward, form, across)
    return tuple(a.astype(ml_dtypes.bfloat16) for a in tables)


def dot(a, b, precision=None):
    return lax.dot_general(
        a, b, (((1,), (0,)), ((), ())), precision=precision, preferred_element_type=F32
    )


def dot_nt(a, b, precision=None):
    return lax.dot_general(
        a, b, (((1,), (1,)), ((), ())), precision=precision, preferred_element_type=F32
    )


def level_lanes():
    lane = lax.broadcasted_iota(jnp.int32, (1, LANES), 1)
    return jnp.where((lane < CHIP) & (lane % (CHIP // 2) == 0), 1.0 / CHIP, 0.0)


def pack_kernel(
    first_hbm, block_hbm, second_hbm, count_hbm, shifts_hbm, anchors_hbm, images_hbm,
    table_ref, forward_ref,
    send_ref, own_ref, images_ref,
    first_ref, block_ref, second_ref, count_ref, shifts_ref, anchors_ref,
    near_ref, facts_ref, tally_ref, sems,
):
    dates = images_ref.shape[0]
    blocks = send_ref.shape[0]
    slots = first_ref.shape[0]
    copies = [
        pltpu.make_async_copy(source, target, sems.at[index])
        for index, (source, target) in enumerate(
            (
                (anchors_hbm, anchors_ref), (first_hbm, first_ref), (block_hbm, block_ref),
                (second_hbm, second_ref), (count_hbm, count_ref), (shifts_hbm, shifts_ref),
                (images_hbm, images_ref),
            )
        )
    ]
    for copy in copies:
        copy.start()
    facts_ref[...] = jnp.zeros(facts_ref.shape, F32)
    for block in range(blocks):
        tally_ref[block] = 0
    row = lax.broadcasted_iota(jnp.int32, (LANES, LANES), 0)
    lane = lax.broadcasted_iota(jnp.int32, (LANES, LANES), 1)
    for copy in copies:
        copy.wait()
    column = lane + jnp.where(lane < CHIP, anchors_ref[0], anchors_ref[1] - CHIP)
    pick = (row == column).astype(F32).astype(BF16)
    table = dot(pick, table_ref[...]).astype(BF16)
    section = dot(images_ref[...].reshape(dates * CHIP, LANES), table)
    level = level_lanes()
    parts = []
    for date in range(dates):
        part = section[date * CHIP : (date + 1) * CHIP]
        parts.append((part - level * jnp.sum(part, axis=0, keepdims=True)).astype(BF16))
    for date in range(0, dates, 2):
        pair = dot(forward_ref[...], jnp.concatenate(parts[date : date + 2], axis=1)).astype(BF16)
        near_ref[date] = pair[:, :LANES]
        near_ref[date + 1] = pair[:, LANES:]
    place = lax.broadcasted_iota(jnp.int32, (1, LANES), 1)
    for slot in range(slots):
        block = block_ref[slot]
        rank = tally_ref[block]
        tally_ref[block] = rank + 1
        live = jnp.where(slot < count_ref[0], 1, 0)
        first = first_ref[slot]
        at = pl.multiple_of(rank * CHIP, CHIP)
        send_ref[block, pl.ds(at, CHIP), :] = near_ref[first]
        fact = jnp.where(place == 0, live, 0)
        values = [second_ref[slot], first]
        for chip in range(2):
            values += [shifts_ref[0, chip, slot], shifts_ref[1, chip, slot]]
        for chip in range(2):
            values += [shifts_ref[1, chip, slot] + anchors_ref[chip] - chip * CHIP]
        for index, value in enumerate(values):
            fact = jnp.where(place == index + 1, value, fact)
        facts_ref[pl.ds(block * 8 + rank, 1), :] = fact.astype(F32)
        own = jnp.where(place == 0, block, jnp.where(live > 0, rank * blocks, -1))
        own_ref[slot : slot + 1, :] = own.astype(F32)
    send_ref[:, 2 * CHIP : 2 * CHIP + 8, :] = (
        facts_ref[...].reshape(blocks, 8, LANES).astype(BF16)
    )


def match_kernel(
    recv_ref, images_ref, above_ref, below_ref,
    table_ref, forward_ref, form_ref, across_ref, out_ref,
    framed_ref, facts_ref, whole_ref, scalar_ref, list_ref, data_ref, cross_ref,
    energy_ref, tall_ref, wide_ref, copy_sem,
):
    blocks = recv_ref.shape[0]
    dates = images_ref.shape[0]
    half = CHIP // 2
    facts_ref[...] = recv_ref[:, 2 * CHIP : 2 * CHIP + 8, :].astype(F32).reshape(blocks * 8, LANES)
    whole_ref[...] = jnp.zeros(whole_ref.shape, jnp.int32)
    for rank in range(2):
        whole_ref[rank * blocks : (rank + 1) * blocks, :] = facts_ref[
            pl.ds(rank, blocks, stride=8), :
        ].astype(jnp.int32)
    copy = pltpu.make_async_copy(whole_ref, scalar_ref, copy_sem)
    copy.start()
    framed_ref[:, :SMAX, :] = above_ref[...].astype(F32)
    framed_ref[:, SMAX : SMAX + CHIP, :] = images_ref[...].astype(F32)
    framed_ref[:, SMAX + CHIP :, :] = below_ref[...].astype(F32)
    for ref in (energy_ref, tall_ref, wide_ref):
        ref[...] = jnp.zeros(ref.shape, F32)
    copy.wait()

    def note(slot, count):
        list_ref[count] = slot
        return count + scalar_ref[slot, 0]

    count = lax.fori_loop(0, 2 * blocks, note, 0)
    spare = 2 * CHIP // 2
    for extra in range(BATCH):
        list_ref[count + extra] = spare
    lane = lax.broadcasted_iota(jnp.int32, (1, LANES), 1)
    low = lane < CHIP
    level = level_lanes()
    turn_sign = jnp.where(lane % half == 0, 0.0, jnp.where(low, 1.0, -1.0))
    corner = jnp.where((lane % half == 0) & (lane >= CHIP), 1.0, 0.0)
    top_row = lax.broadcasted_iota(jnp.int32, (8, LANES), 0) == 0

    def one_batch(turn, carry):
        rows_of = []
        near_of = []
        for s in range(BATCH):
            slot = list_ref[turn * BATCH + s]
            rows_of.append(slot)
            source = jnp.where(slot == spare, 0, slot)
            rank = jnp.where(source >= blocks, 1, 0)
            near_of.append((source - rank * blocks, pl.multiple_of(rank * CHIP, CHIP)))
            second = scalar_ref[slot, 1]
            pieces = []
            starts = []
            for chip in range(2):
                down = scalar_ref[slot, 3 + 2 * chip] + SMAX
                start = scalar_ref[slot, 7 + chip]
                piece = framed_ref[second, pl.ds(down, CHIP), :]
                pieces.append(pltpu.roll(piece, lax.rem(LANES - start, LANES), 1))
                starts.append(start)
            column = lane + jnp.where(low, starts[0], starts[1])
            inside = (column >= 0) & (column < LANES)
            window = jnp.where(low, pieces[0], pieces[1])
            data_ref[s * CHIP : (s + 1) * CHIP, :] = jnp.where(inside, window, 0.0).astype(BF16)
        section = dot(data_ref[...], table_ref[...])
        crosses = []
        for s in range(BATCH):
            part = section[s * CHIP : (s + 1) * CHIP, :LANES]
            part = part - level * jnp.sum(part, axis=0, keepdims=True)
            other = section[s * CHIP : (s + 1) * CHIP, LANES:]
            far = dot(forward_ref[...], jnp.concatenate([part, other], axis=1).astype(BF16))
            block, at = near_of[s]
            near = recv_ref[block, pl.ds(at, CHIP), :].astype(F32)
            turned = pltpu.roll(near, CHIP, 1) * turn_sign
            top, low_rows = near[:half], near[half:]
            top_turned, low_turned = turned[:half], turned[half:]
            p, q = far[:half, :LANES], far[:half, LANES:]
            p_low, q_low = far[half:, :LANES], far[half:, LANES:]
            first = top * p + top_turned * q
            second = low_rows * p_low + low_turned * q_low
            upper = first + second
            lower = (low_rows * p + low_turned * q) - (top * p_low + top_turned * q_low)
            upper = jnp.concatenate([jnp.where(top_row, first[:8], upper[:8]), upper[8:]], axis=0)
            lower = jnp.concatenate([jnp.where(top_row, second[:8], lower[:8]), lower[8:]], axis=0)
            cross = jnp.concatenate([upper, lower], axis=0)
            crosses.append(cross)
            cross_ref[s * CHIP : (s + 1) * CHIP, :] = cross.astype(BF16)
        wide = dot(cross_ref[...], across_ref[...])
        for s in range(0, BATCH, 2):
            pair = [cross_ref[r * CHIP : (r + 1) * CHIP, :] for r in (s, s + 1)]
            tall = dot(form_ref[...], jnp.concatenate(pair, axis=1))
            for r in range(2):
                cross = crosses[s + r]
                power = cross * cross
                tall_r = cross * tall[:, r * LANES : (r + 1) * LANES]
                wide_r = cross * wide[(s + r) * CHIP : (s + r + 1) * CHIP]
                at = pl.ds(rows_of[s + r], 1)
                energy_ref[at, :] = 0.5 * (
                    jnp.sum(power, axis=0, keepdims=True)
                    + power[:1] + corner * power[half : half + 1]
                )
                tall_ref[at, :] = jnp.sum(tall_r, axis=0, keepdims=True)
                wide_ref[at, :] = 0.5 * (jnp.sum(wide_r, axis=0, keepdims=True) + wide_r[:1])
        return carry

    lax.fori_loop(0, (count + BATCH - 1) // BATCH, one_batch, 0)

    lane8 = lax.broadcasted_iota(jnp.int32, (8, LANES), 1)
    row8 = lax.broadcasted_iota(jnp.int32, (8, LANES), 0)
    weights = jnp.where((row8 == 1) | ((lane8 % half == 0) & (lane8 < CHIP)), 1.0, 0.5)
    even = lane // half % 2 == 0
    stack = []
    for ref in (energy_ref, tall_ref, wide_ref):
        value = ref[:CHIP, :]
        stack += [jnp.where(even, value, 0.0), jnp.where(even, 0.0, value)]
    found = dot_nt(weights, jnp.concatenate(stack, axis=0), HIGH)
    norm = found[0:1, :LANES] + 1e-6
    tall = found[0:1, LANES : 2 * LANES] / norm
    wide = found[1:2, 2 * LANES :] / norm
    whole = whole_ref[:CHIP, :].astype(F32).astype(BF16)
    choose = (lane8 == row8).astype(F32).astype(BF16)
    fact = dot_nt(choose, jnp.concatenate([whole, whole], axis=0))
    live = fact[0:1] > 0.5
    down = jnp.where(live, jnp.where(low, fact[3:4], fact[5:6]) + tall, 0.0)
    across = jnp.where(live, jnp.where(low, fact[4:5], fact[6:7]) + wide, 0.0)
    row = lax.broadcasted_iota(jnp.int32, (LANES, LANES), 0).astype(F32)
    base = (lax.rem(lax.axis_index("date"), LANES // dates) * dates).astype(F32)
    chosen = (row == fact[1:2] + base).astype(F32)
    value = jnp.where(row8 < 6, down, across)
    value = jnp.where((row8 >= 4) & ((row8 % 2 == 0) == (lane8 < CHIP)), value, 0.0)
    result = dot_nt(value, chosen, HIGH)
    result = jnp.where(row8 == 0, down, result)
    result = jnp.where(row8 == 1, across, result)
    result = jnp.where(row8 == 2, fact[2:3], result)
    for block in range(blocks):
        out_ref[block] = result


def series_kernel(
    own_ref, result_ref, inverse_ref, turned_ref, offsets_ref, series_ref
):
    blocks = result_ref.shape[0] // 8
    slots = own_ref.shape[0]
    dates = inverse_ref.shape[2]
    ones = jnp.ones((8, LANES), F32)
    me = lax.axis_index("date").astype(F32)
    own = own_ref[...]
    partner = lax.broadcasted_iota(jnp.int32, (slots, blocks), 1).astype(F32)
    partner = (own[:, 0:1] == partner).astype(F32)
    lane = lax.broadcasted_iota(jnp.int32, (slots, LANES), 1)
    mine = lane.astype(F32) - me == own[:, 1:2] + jnp.where(lane < CHIP, 0.0, float(CHIP))
    mine = mine & (own[:, 1:2] >= 0.0)
    for axis in range(2):
        rows = result_ref[pl.ds(axis, blocks, stride=8), :]
        value = jnp.where(mine, dot(partner, rows, HIGH), 0.0)
        for chip in range(2):
            half = jnp.where(lane < CHIP if chip == 0 else lane >= CHIP, value, 0.0)
            offsets_ref[axis, chip : chip + 1, :] = dot_nt(ones, half, HIGH)[0:1, :]
    sums = [jnp.zeros((8, LANES), F32) for _ in range(dates)]
    per = LANES // dates
    groups = [jnp.zeros((8, LANES), F32) for _ in range(blocks // per)]
    for block in range(blocks):
        value = result_ref[block * 8 : block * 8 + 8, :]
        first = jnp.broadcast_to(value[2:3], (8, LANES))
        for date in range(dates):
            sums[date] = sums[date] + jnp.where(first == date, value, 0.0)
        groups[block // per] = groups[block // per] + value
    low = lax.broadcasted_iota(jnp.int32, (dates, LANES), 1) < CHIP
    for axis in range(2):
        own = jnp.zeros((dates, LANES), F32)
        for date in range(dates):
            own = own + turned_ref[axis, date] * sums[date][axis : axis + 1]
        for chip in range(2):
            total = jnp.where(low if chip == 0 else ~low, -own, 0.0)
            at = 4 + 2 * axis + chip
            for g, group in enumerate(groups):
                total = total + inverse_ref[axis, chip, :, g * LANES : (g + 1) * LANES] * group[at : at + 1]
            series_ref[axis, chip : chip + 1, :] = dot_nt(ones, total, HIGH)[0:1, :]


def body(images, inverse_blocks, pair_first, pair_block, pair_second, pair_count, shifts, anchors):
    blocks = lax.axis_size("date")
    strips = lax.axis_size("strip")
    dates, length, columns = images.shape
    slots = pair_first.shape[0]
    hbm = pl.BlockSpec(memory_space=pltpu.HBM)
    vmem = pl.BlockSpec(memory_space=pltpu.VMEM)
    params = pltpu.CompilerParams(vmem_limit_bytes=48 * 2**20)
    ends = strips - 1
    above = lax.ppermute(
        images[:, length - SMAX :, :], "strip", [(i, i + 1) for i in range(ends)]
    )
    below = lax.ppermute(images[:, :SMAX, :], "strip", [(i + 1, i) for i in range(ends)])
    turned = inverse_blocks.reshape(2, 2, dates, blocks, dates).transpose(0, 4, 2, 1, 3)
    turned = jnp.concatenate([turned, turned], axis=4)
    turned = jnp.pad(turned, ((0, 0),) * 4 + ((0, CHIP - 2 * blocks),))
    turned = turned.reshape(2, dates, dates, LANES)
    near_table, far_table, forward, form, across = [jnp.asarray(t) for t in make_tables()]
    send, own = pl.pallas_call(
        pack_kernel,
        out_shape=(
            jax.ShapeDtypeStruct((blocks, 2 * length + 8, columns), BF16),
            jax.ShapeDtypeStruct((slots, columns), F32),
        ),
        in_specs=[hbm] * 7 + [vmem] * 2,
        out_specs=(vmem, vmem),
        scratch_shapes=[
            pltpu.VMEM(images.shape, BF16),
            pltpu.SMEM((slots,), jnp.int32),
            pltpu.SMEM((slots,), jnp.int32),
            pltpu.SMEM((slots,), jnp.int32),
            pltpu.SMEM((1,), jnp.int32),
            pltpu.SMEM((2, 2, slots), jnp.int32),
            pltpu.SMEM((2,), jnp.int32),
            pltpu.VMEM((dates, length, columns), BF16),
            pltpu.VMEM((blocks * 8, columns), F32),
            pltpu.SMEM((blocks,), jnp.int32),
            pltpu.SemaphoreType.DMA((7,)),
        ],
        compiler_params=pltpu.CompilerParams(vmem_limit_bytes=60 * 2**20),
    )(
        pair_first, pair_block[:, 0], pair_second, pair_count,
        jnp.transpose(shifts, (1, 2, 0)), anchors, images, near_table, forward,
    )
    recv = lax.all_to_all(send, "date", split_axis=0, concat_axis=0, tiled=True)
    recv, turned = lax.optimization_barrier((recv, turned))
    result = pl.pallas_call(
        match_kernel,
        out_shape=jax.ShapeDtypeStruct((blocks, 8, columns), F32),
        in_specs=[vmem] * 8,
        out_specs=vmem,
        scratch_shapes=[
            pltpu.VMEM((dates, length + 2 * SMAX, columns), F32),
            pltpu.VMEM((blocks * 8, columns), F32),
            pltpu.VMEM((CHIP + 8, columns), jnp.int32),
            pltpu.SMEM((CHIP + 8, columns), jnp.int32),
            pltpu.SMEM((CHIP + BATCH,), jnp.int32),
            pltpu.VMEM((BATCH * length, columns), BF16),
            pltpu.VMEM((BATCH * length, columns), BF16),
            pltpu.VMEM((CHIP + 8, columns), F32),
            pltpu.VMEM((CHIP + 8, columns), F32),
            pltpu.VMEM((CHIP + 8, columns), F32),
            pltpu.SemaphoreType.DMA,
        ],
        compiler_params=params,
    )(recv, images, above, below, far_table, forward, form, across)
    result = lax.all_to_all(result, "date", split_axis=0, concat_axis=0, tiled=True)
    offsets, series = pl.pallas_call(
        series_kernel,
        out_shape=(
            jax.ShapeDtypeStruct((2, 2, slots), F32),
            jax.ShapeDtypeStruct((2, 2, dates), F32),
        ),
        in_specs=[vmem] * 4,
        out_specs=(vmem, vmem),
        compiler_params=params,
    )(own, result.reshape(blocks * 8, columns), inverse_blocks, turned)
    return jnp.transpose(offsets, (2, 0, 1)), series


def solution(mesh):
    return jax.shard_map(
        body,
        mesh=mesh,
        in_specs=(
            P("date", "strip", None),
            P(None, "strip", "date", None),
            P("date"),
            P("date", None),
            P("date"),
            P("date"),
            P("date", None, "strip"),
            P("strip"),
        ),
        out_specs=(P("date", None, "strip"), P(None, "strip", "date")),
        check_vma=False,
    )
```

time: 88.9 us -> 67.8 us (0.76)
  blocking collectives: 0 us -> 16.8 us
  starting transfers between devices: 29.2 us -> 14.3 us
  waiting for transfers between devices: 34 us -> 21.2 us
  Pallas kernels: 16.6 us -> 9.29 us
  local copies, waits for them, and re-layouts: 6.89 us -> 2.91 us
  other arithmetic: 0.23 us -> 1.56 us
    all_to_all x0 -> x1, blocking collectives: none -> 16.8 us  [body(): lax.all_to_all(result, 'date', split_axis=0, concat_axis=0, tiled=True)]
    all_to_all x1 -> x0, starting transfers between devices: 14.8 us -> none  [body(): lax.all_to_all(result, 'date', split_axis=0, concat_axis=0, tiled=True)]
    all_to_all x1 -> x0, waiting for transfers between devices: 8.37 us -> none  [body(): lax.all_to_all(result, 'date', split_axis=0, concat_axis=0, tiled=True)]
    pallas_call x1, Pallas kernels: 11.5 us -> 4.37 us  [body(): pl.pallas_call(match_kernel, out_shape=jax.ShapeDtypeStruct((blocks, 8, c...]
    unnamed x24 -> x14, local copies, waits for them, and re-layouts: 4.45 us -> 0.03 us
    ppermute x1, waiting for transfers between devices: 2.81 us -> 0.01 us  [body(): lax.ppermute(images[:, length - SMAX:, :], 'strip', [(i, i + 1) for i in...]
    all_to_all x1, waiting for transfers between devices: 22.9 us -> 21.2 us  [body(): recv = lax.all_to_all(send, 'date', split_axis=0, concat_axis=0, tiled=True)]
    concatenate x1, other arithmetic: 0.23 us -> 1.56 us  [body(): turned = jnp.concatenate([turned, turned], axis=4)]
  transfers between devices with their start and end apart: 4 -> 3, of which waited for: 3 -> 1; matrix products, arithmetic and copies ran while one was open for 2% -> 7% of each run, Pallas kernels for 0% -> 0%
where the time goes in v2:
time: 67.8 us; the launch traced here: 67.5 us
  waiting for transfers between devices  21.2 us (31%)
  blocking collectives  16.8 us (25%)
  starting transfers between devices  14.3 us (21%)
  Pallas kernels  9.29 us (14%)
  local copies, waits for them, and re-layouts  2.91 us (4%)
  other arithmetic  1.56 us (2%)
  between operations  1.47 us (2%)
    all_to_all x1, waiting for transfers between devices, body(): recv = lax.all_to_all(send, 'date', split_axis=0, concat_axis=0, tiled=True)  21.2 us
    all_to_all x1, blocking collectives, body(): lax.all_to_all(result, 'date', split_axis=0, concat_axis=0, tiled=True)  16.8 us
    all_to_all x1, starting transfers between devices, body(): recv = lax.all_to_all(send, 'date', split_axis=0, concat_axis=0, tiled=True)  9.96 us
    pallas_call x1, Pallas kernels, body(): pl.pallas_call(match_kernel, out_shape=jax.ShapeDtypeStruct((blocks, 8, c...  4.37 us
    pallas_call x1, Pallas kernels, body(): pl.pallas_call(pack_kernel, out_shape=(jax.ShapeDtypeStruct((blocks, 2 *...  3.56 us
    ppermute x1, starting transfers between devices, body(): lax.ppermute(images[:, length - SMAX:, :], 'strip', [(i, i + 1) for i in...  2.4 us
    concatenate x1, local copies, waits for them, and re-layouts, body(): turned = jnp.concatenate([turned, turned], axis=4)  2.22 us
    ppermute x1, starting transfers between devices, body(): lax.ppermute(images[:, :SMAX, :], 'strip', [(i + 1, i) for i in range(end...  1.92 us
  transfers between devices with their start and end apart: 3, of which 1 were waited for; matrix products, arithmetic and copies ran while one was open for 7% of the time, Pallas kernels for 0%

profile of v2, /device:TPU:448, one launch (start us, length us, event | category | flops | bytes accessed | tf_op | source)
XLA Modules:
  0.0 67.5 jit_solution(11671125328194954890)
XLA Ops:
  0.6 0.0 copy-start
  0.6 0.0 copy-start.1
  1.3 3.6 %shard_map.140 = (bf16[32,136,128]{2,1,0:T(8,128)(2,1)}, f32[32,128]{1,0:T(8,128)}) custom-call(s32[32]{0:T(128)} %first_hbm.1, s32[32]{0:T(128)} %bitcast.10, s32[32]{0:T(128)} %second_hbm.1, s32[1]{0:T(128)S(6)} %copy.21.count_hbm, s32[2,2,32]{2,1,0:T(2,128)} %bitcast.9, s32[2]{0:T(128)} %anchors_hbm.1, bf16[16,64,128]{2,1,0:T(8,128)(2,1)} %images_ref.1, ...), custom_call_target="tpu_custom_call" | custom-call | tf_op jit(solution)/shard_map/pallas_call | solution.py:330
  4.9 10.0 %all-to-all-start = ((bf16[32,136,128]{2,1,0:T(8,128)(2,1)}), bf16[32,136,128]{2,1,0:T(8,128)(2,1)S(1)}, u32[]{:S(2)}, u32[]{:S(2)}) async-start(bf16[32,136,128]{2,1,0:T(8,128)(2,1)} %get-tuple-element.9), calls=%async_computation | async-start | bytes 2228224 | tf_op jit(solution)/shard_map/all_to_all | solution.py:356
  14.9 0.0 copy-done
  14.9 1.9 %collective-permute-start.1 = (bf16[16,8,128]{2,1,0:T(8,128)(2,1)S(1)}, bf16[16,8,128]{2,1,0:T(8,128)(2,1)S(1)}, u32[]{:S(2)}, u32[]{:S(2)}) collective-permute-start(bf16[16,8,128]{2,1,0:T(8,128)(2,1)S(1)} %get-tuple-element.14), channel_id=1, source_target_pairs={{32,0},{64,32},{96,64},{128,96},{160,128},{192,160},{224,192},{256... | collective-permute-start | bytes 98312 | tf_op jit(solution)/shard_map/ppermute | solution.py:324
  16.8 2.4 %collective-permute-start = (bf16[16,8,128]{2,1,0:T(8,128)(2,1)S(1)}, bf16[16,8,128]{2,1,0:T(8,128)(2,1)S(1)}, u32[]{:S(2)}, u32[]{:S(2)}) collective-permute-start(bf16[16,8,128]{2,1,0:T(8,128)(2,1)S(1)} %get-tuple-element.15), channel_id=1, source_target_pairs={{0,32},{32,64},{64,96},{96,128},{128,160},{160,192},{192,224},{224... | collective-permute-start | bytes 98312 | tf_op jit(solution)/shard_map/ppermute | solution.py:321
  19.3 0.0 copy-done.1
  19.3 0.4 reshape.13
  19.6 1.6 %pad_maximum_fusion = f32[2,16,16,2,64]{1,4,2,3,0:T(8,128)} fusion(f32[2,16,16,2,32]{1,4,2,3,0:T(8,128)S(1)} %bitcast.8), kind=kLoop, calls=%fused_computation | loop fusion | flops 65536 | bytes 393216 | tf_op jit(solution)/shard_map/concatenate | solution.py:326
  21.2 0.0 copy-start.2
  21.2 0.0 copy-start.3
  21.2 0.0 copy-start.4
  21.2 0.0 copy-start.6
  21.2 0.0 copy-start.5
  21.2 2.2 %copy.20 = f32[2,16,16,2,64]{4,3,2,1,0:T(2,128)S(1)} copy(f32[2,16,16,2,64]{1,4,2,3,0:T(8,128)} %pad_maximum_fusion) | data formatting | bytes 524288 | tf_op jit(solution)/shard_map/concatenate | solution.py:326
  23.4 0.3 reshape.14.turned_ref
  23.7 21.2 %all-to-all-done.recv_ref = bf16[32,136,128]{2,1,0:T(8,128)(2,1)S(1)} async-done(((bf16[32,136,128]{2,1,0:T(8,128)(2,1)}), bf16[32,136,128]{2,1,0:T(8,128)(2,1)S(1)}, u32[]{:S(2)}, u32[]{:S(2)}) %all-to-all-start) | async-done | bytes 1114144 | tf_op jit(solution)/shard_map/all_to_all | solution.py:356
  44.9 0.0 collective-permute-done.1.below_ref
  44.9 0.0 collective-permute-done.above_ref
  44.9 0.0 copy-done.2
  44.9 0.0 copy-done.3
  44.9 0.0 copy-done.4
  45.0 0.0 copy-done.6
  45.0 4.4 %shard_map.141 = f32[32,8,128]{2,1,0:T(8,128)S(1)} custom-call(bf16[32,136,128]{2,1,0:T(8,128)(2,1)S(1)} %all-to-all-done.recv_ref, bf16[16,64,128]{2,1,0:T(8,128)(2,1)S(1)} %copy-done, bf16[16,8,128]{2,1,0:T(8,128)(2,1)S(1)} %collective-permute-done.above_ref, bf16[16,8,128]{2,1,0:T(8,128)(2,1)S(1)} %collective-permute-done.1.below_ref, ...), custom_call_target="tpu_custom_call" | custom-call | tf_op jit(solution)/shard_map/pallas_call | solution.py:358
  49.3 16.8 %all_to_all.10 = f32[32,8,128]{2,1,0:T(8,128)S(1)} all-to-all(f32[32,8,128]{2,1,0:T(8,128)S(1)} %shard_map.141), channel_id=1, replica_groups=mesh['strip'=16,'date'=32] {'date'}, dimensions={0} | all-to-all | bytes 262144 | tf_op jit(solution)/shard_map/all_to_all | solution.py:378
  66.1 0.0 copy-done.5
  66.1 1.4 %shard_map.142 = (f32[2,2,32]{2,1,0:T(2,128)}, f32[2,2,16]{2,1,0:T(2,128)}) custom-call(f32[32,128]{1,0:T(8,128)S(1)} %copy-done.5, f32[256,128]{1,0:T(8,128)S(1)} %bitcast.7, f32[2,2,16,512]{3,2,1,0:T(8,128)S(1)} %copy-done.1, f32[2,16,16,128]{3,2,1,0:T(8,128)S(1)} %reshape.14.turned_ref), custom_call_target="tpu_custom_call" | custom-call | tf_op jit(solution)/shard_map/pallas_call | solution.py:379
  (1 shorter events, 0.0 us)
Async XLA Ops:
  0.6 14.3 %copy-start = (bf16[16,64,128]{2,1,0:T(8,128)(2,1)S(1)}, bf16[16,64,128]{2,1,0:T(8,128)(2,1)}, u32[]{:S(2)}) copy-start(bf16[16,64,128]{2,1,0:T(8,128)(2,1)} %images_ref.1) | copy-start | bytes 786436
  0.6 18.6 %copy-start.1 = (f32[2,2,16,512]{3,2,1,0:T(8,128)S(1)}, f32[2,2,16,512]{3,2,1,0:T(8,128)}, u32[]{:S(2)}) copy-start(f32[2,2,16,512]{3,2,1,0:T(8,128)} %inverse_ref.1) | copy-start | bytes 393220
  4.9 40.0 %all-to-all-start = ((bf16[32,136,128]{2,1,0:T(8,128)(2,1)}), bf16[32,136,128]{2,1,0:T(8,128)(2,1)S(1)}, u32[]{:S(2)}, u32[]{:S(2)}) async-start(bf16[32,136,128]{2,1,0:T(8,128)(2,1)} %get-tuple-element.9), calls=%async_computation | async-start | bytes 2228224 | tf_op jit(solution)/shard_map/all_to_all | solution.py:356
  14.9 30.0 %collective-permute-start.1 = (bf16[16,8,128]{2,1,0:T(8,128)(2,1)S(1)}, bf16[16,8,128]{2,1,0:T(8,128)(2,1)S(1)}, u32[]{:S(2)}, u32[]{:S(2)}) collective-permute-start(bf16[16,8,128]{2,1,0:T(8,128)(2,1)S(1)} %get-tuple-element.14), channel_id=1, source_target_pairs={{32,0},{64,32},{96,64},{128,96},{160,128},{192,160},{224,192},{256... | collective-permute-start | bytes 98312 | tf_op jit(solution)/shard_map/ppermute | solution.py:324
  16.8 28.1 %collective-permute-start = (bf16[16,8,128]{2,1,0:T(8,128)(2,1)S(1)}, bf16[16,8,128]{2,1,0:T(8,128)(2,1)S(1)}, u32[]{:S(2)}, u32[]{:S(2)}) collective-permute-start(bf16[16,8,128]{2,1,0:T(8,128)(2,1)S(1)} %get-tuple-element.15), channel_id=1, source_target_pairs={{0,32},{32,64},{64,96},{96,128},{128,160},{160,192},{192,224},{224... | collective-permute-start | bytes 98312 | tf_op jit(solution)/shard_map/ppermute | solution.py:321
  21.2 23.7 %copy-start.2 = (bf16[128,256]{1,0:T(8,128)(2,1)S(1)}, bf16[128,256]{1,0:T(8,128)(2,1)}, u32[]{:S(2)}) copy-start(bf16[128,256]{1,0:T(8,128)(2,1)} %constant.12.clone.table_ref) | copy-start | bytes 196612
  21.2 23.7 %copy-start.3 = (bf16[64,64]{1,0:T(8,128)(2,1)S(1)}, bf16[64,64]{1,0:T(8,128)(2,1)}, u32[]{:S(2)}) copy-start(bf16[64,64]{1,0:T(8,128)(2,1)} %constant.13.clone.forward_ref) | copy-start | bytes 24580
  21.2 23.8 %copy-start.4 = (bf16[128,128]{1,0:T(8,128)(2,1)S(1)}, bf16[128,128]{1,0:T(8,128)(2,1)}, u32[]{:S(2)}) copy-start(bf16[128,128]{1,0:T(8,128)(2,1)} %constant.15.clone.across_ref) | copy-start | bytes 98308
  21.2 23.8 %copy-start.6 = (bf16[64,64]{1,0:T(8,128)(2,1)S(1)}, bf16[64,64]{1,0:T(8,128)(2,1)}, u32[]{:S(2)}) copy-start(bf16[64,64]{1,0:T(8,128)(2,1)} %constant.14.clone.form_ref) | copy-start | bytes 24580
  21.2 44.9 %copy-start.5 = (f32[32,128]{1,0:T(8,128)S(1)}, f32[32,128]{1,0:T(8,128)}, u32[]{:S(2)}) copy-start(f32[32,128]{1,0:T(8,128)} %get-tuple-element.8.own_ref) | copy-start | bytes 49156

commit v3 on v2

--- a/solution.py
+++ b/solution.py
@@ -12,8 +12,7 @@
 SMAX = 8
 CHIP = 64
 LANES = 128
-BATCH = 8
-HIGH = lax.Precision.HIGHEST
+BATCH = 16
 F32 = jnp.float32
 BF16 = jnp.bfloat16
 
@@ -48,16 +47,21 @@
     return tuple(a.astype(ml_dtypes.bfloat16) for a in tables)
 
 
-def dot(a, b, precision=None):
-    return lax.dot_general(
-        a, b, (((1,), (0,)), ((), ())), precision=precision, preferred_element_type=F32
-    )
-
-
-def dot_nt(a, b, precision=None):
-    return lax.dot_general(
-        a, b, (((1,), (1,)), ((), ())), precision=precision, preferred_element_type=F32
-    )
+def dot(a, b):
+    return lax.dot_general(a, b, (((1,), (0,)), ((), ())), preferred_element_type=F32)
+
+
+def dot_nt(a, b):
+    return lax.dot_general(a, b, (((1,), (1,)), ((), ())), preferred_element_type=F32)
+
+
+def parts_of(value, count):
+    parts = []
+    for _ in range(count):
+        part = value.astype(BF16)
+        parts.append(part)
+        value = value - part.astype(F32)
+    return parts
 
 
 def level_lanes():
@@ -70,7 +74,7 @@
     table_ref, forward_ref,
     send_ref, own_ref, images_ref,
     first_ref, block_ref, second_ref, count_ref, shifts_ref, anchors_ref,
-    near_ref, facts_ref, tally_ref, sems,
+    near_ref, facts_ref, tally_ref, where_ref, sems,
 ):
     dates = images_ref.shape[0]
     blocks = send_ref.shape[0]
@@ -90,15 +94,34 @@
     facts_ref[...] = jnp.zeros(facts_ref.shape, F32)
     for block in range(blocks):
         tally_ref[block] = 0
+    for copy in copies[:-1]:
+        copy.wait()
+    place = lax.broadcasted_iota(jnp.int32, (1, LANES), 1)
+    for slot in range(slots):
+        block = block_ref[slot]
+        rank = tally_ref[block]
+        tally_ref[block] = rank + 1
+        where_ref[slot] = rank
+        live = jnp.where(slot < count_ref[0], 1, 0)
+        values = [live, second_ref[slot]]
+        for chip in range(2):
+            start = shifts_ref[1, chip, slot] + anchors_ref[chip] - chip * CHIP
+            values += [shifts_ref[0, chip, slot], start]
+        values += [first_ref[slot], shifts_ref[1, 0, slot], shifts_ref[1, 1, slot]]
+        fact = jnp.zeros((1, LANES), jnp.int32)
+        for index, value in enumerate(values):
+            fact = jnp.where(place == index, value, fact)
+        facts_ref[pl.ds(block * 8 + rank, 1), :] = fact.astype(F32)
+        own = jnp.where(place == 0, block, jnp.where(live > 0, rank * blocks, -1))
+        own_ref[slot : slot + 1, :] = own.astype(F32)
     row = lax.broadcasted_iota(jnp.int32, (LANES, LANES), 0)
     lane = lax.broadcasted_iota(jnp.int32, (LANES, LANES), 1)
-    for copy in copies:
-        copy.wait()
     column = lane + jnp.where(lane < CHIP, anchors_ref[0], anchors_ref[1] - CHIP)
     pick = (row == column).astype(F32).astype(BF16)
     table = dot(pick, table_ref[...]).astype(BF16)
+    level = level_lanes()
+    copies[-1].wait()
     section = dot(images_ref[...].reshape(dates * CHIP, LANES), table)
-    level = level_lanes()
     parts = []
     for date in range(dates):
         part = section[date * CHIP : (date + 1) * CHIP]
@@ -107,26 +130,9 @@
         pair = dot(forward_ref[...], jnp.concatenate(parts[date : date + 2], axis=1)).astype(BF16)
         near_ref[date] = pair[:, :LANES]
         near_ref[date + 1] = pair[:, LANES:]
-    place = lax.broadcasted_iota(jnp.int32, (1, LANES), 1)
     for slot in range(slots):
-        block = block_ref[slot]
-        rank = tally_ref[block]
-        tally_ref[block] = rank + 1
-        live = jnp.where(slot < count_ref[0], 1, 0)
-        first = first_ref[slot]
-        at = pl.multiple_of(rank * CHIP, CHIP)
-        send_ref[block, pl.ds(at, CHIP), :] = near_ref[first]
-        fact = jnp.where(place == 0, live, 0)
-        values = [second_ref[slot], first]
-        for chip in range(2):
-            values += [shifts_ref[0, chip, slot], shifts_ref[1, chip, slot]]
-        for chip in range(2):
-            values += [shifts_ref[1, chip, slot] + anchors_ref[chip] - chip * CHIP]
-        for index, value in enumerate(values):
-            fact = jnp.where(place == index + 1, value, fact)
-        facts_ref[pl.ds(block * 8 + rank, 1), :] = fact.astype(F32)
-        own = jnp.where(place == 0, block, jnp.where(live > 0, rank * blocks, -1))
-        own_ref[slot : slot + 1, :] = own.astype(F32)
+        at = pl.multiple_of(where_ref[slot] * CHIP, CHIP)
+        send_ref[block_ref[slot], pl.ds(at, CHIP), :] = near_ref[first_ref[slot]]
     send_ref[:, 2 * CHIP : 2 * CHIP + 8, :] = (
         facts_ref[...].reshape(blocks, 8, LANES).astype(BF16)
     )
@@ -142,11 +148,14 @@
     dates = images_ref.shape[0]
     half = CHIP // 2
     facts_ref[...] = recv_ref[:, 2 * CHIP : 2 * CHIP + 8, :].astype(F32).reshape(blocks * 8, LANES)
-    whole_ref[...] = jnp.zeros(whole_ref.shape, jnp.int32)
-    for rank in range(2):
-        whole_ref[rank * blocks : (rank + 1) * blocks, :] = facts_ref[
-            pl.ds(rank, blocks, stride=8), :
-        ].astype(jnp.int32)
+    whole = [facts_ref[pl.ds(rank, blocks, stride=8), :].astype(BF16) for rank in range(2)]
+    if blocks < CHIP // 2:
+        whole.append(jnp.zeros((CHIP - 2 * blocks, LANES), BF16))
+    lane16 = lax.broadcasted_iota(jnp.int32, (16, LANES), 1)
+    row16 = lax.broadcasted_iota(jnp.int32, (16, LANES), 0)
+    choose = (lane16 == row16).astype(F32).astype(BF16)
+    fact = dot_nt(choose, jnp.concatenate(whole + whole, axis=0))
+    whole_ref[...] = fact[:8].astype(jnp.int32)
     copy = pltpu.make_async_copy(whole_ref, scalar_ref, copy_sem)
     copy.start()
     framed_ref[:, :SMAX, :] = above_ref[...].astype(F32)
@@ -156,12 +165,11 @@
         ref[...] = jnp.zeros(ref.shape, F32)
     copy.wait()
 
-    def note(slot, count):
+    count = 0
+    for slot in range(2 * blocks):
         list_ref[count] = slot
-        return count + scalar_ref[slot, 0]
-
-    count = lax.fori_loop(0, 2 * blocks, note, 0)
-    spare = 2 * CHIP // 2
+        count = count + scalar_ref[0, slot]
+    spare = CHIP
     for extra in range(BATCH):
         list_ref[count + extra] = spare
     lane = lax.broadcasted_iota(jnp.int32, (1, LANES), 1)
@@ -180,12 +188,12 @@
             source = jnp.where(slot == spare, 0, slot)
             rank = jnp.where(source >= blocks, 1, 0)
             near_of.append((source - rank * blocks, pl.multiple_of(rank * CHIP, CHIP)))
-            second = scalar_ref[slot, 1]
+            second = scalar_ref[1, source]
             pieces = []
             starts = []
             for chip in range(2):
-                down = scalar_ref[slot, 3 + 2 * chip] + SMAX
-                start = scalar_ref[slot, 7 + chip]
+                down = scalar_ref[2 + 2 * chip, source] + SMAX
+                start = scalar_ref[3 + 2 * chip, source]
                 piece = framed_ref[second, pl.ds(down, CHIP), :]
                 pieces.append(pltpu.roll(piece, lax.rem(LANES - start, LANES), 1))
                 starts.append(start)
@@ -244,25 +252,24 @@
     for ref in (energy_ref, tall_ref, wide_ref):
         value = ref[:CHIP, :]
         stack += [jnp.where(even, value, 0.0), jnp.where(even, 0.0, value)]
-    found = dot_nt(weights, jnp.concatenate(stack, axis=0), HIGH)
+    weights = weights.astype(BF16)
+    found = sum(dot_nt(weights, part) for part in parts_of(jnp.concatenate(stack, axis=0), 3))
     norm = found[0:1, :LANES] + 1e-6
     tall = found[0:1, LANES : 2 * LANES] / norm
     wide = found[1:2, 2 * LANES :] / norm
-    whole = whole_ref[:CHIP, :].astype(F32).astype(BF16)
-    choose = (lane8 == row8).astype(F32).astype(BF16)
-    fact = dot_nt(choose, jnp.concatenate([whole, whole], axis=0))
     live = fact[0:1] > 0.5
-    down = jnp.where(live, jnp.where(low, fact[3:4], fact[5:6]) + tall, 0.0)
-    across = jnp.where(live, jnp.where(low, fact[4:5], fact[6:7]) + wide, 0.0)
+    down = jnp.where(live, jnp.where(low, fact[2:3], fact[4:5]) + tall, 0.0)
+    across = jnp.where(live, jnp.where(low, fact[7:8], fact[8:9]) + wide, 0.0)
     row = lax.broadcasted_iota(jnp.int32, (LANES, LANES), 0).astype(F32)
     base = (lax.rem(lax.axis_index("date"), LANES // dates) * dates).astype(F32)
-    chosen = (row == fact[1:2] + base).astype(F32)
+    chosen = (row == fact[1:2] + base).astype(F32).astype(BF16)
     value = jnp.where(row8 < 6, down, across)
     value = jnp.where((row8 >= 4) & ((row8 % 2 == 0) == (lane8 < CHIP)), value, 0.0)
-    result = dot_nt(value, chosen, HIGH)
+    result = dot_nt(jnp.concatenate(parts_of(value, 3), axis=0), chosen)
+    result = result[:8] + result[8:16] + result[16:24]
     result = jnp.where(row8 == 0, down, result)
     result = jnp.where(row8 == 1, across, result)
-    result = jnp.where(row8 == 2, fact[2:3], result)
+    result = jnp.where(row8 == 2, fact[6:7], result)
     for block in range(blocks):
         out_ref[block] = result
 
@@ -273,20 +280,22 @@
     blocks = result_ref.shape[0] // 8
     slots = own_ref.shape[0]
     dates = inverse_ref.shape[2]
-    ones = jnp.ones((8, LANES), F32)
+    ones = jnp.ones((8, LANES), F32).astype(BF16)
     me = lax.axis_index("date").astype(F32)
     own = own_ref[...]
     partner = lax.broadcasted_iota(jnp.int32, (slots, blocks), 1).astype(F32)
-    partner = (own[:, 0:1] == partner).astype(F32)
+    partner = (own[:, 0:1] == partner).astype(F32).astype(BF16)
     lane = lax.broadcasted_iota(jnp.int32, (slots, LANES), 1)
     mine = lane.astype(F32) - me == own[:, 1:2] + jnp.where(lane < CHIP, 0.0, float(CHIP))
     mine = mine & (own[:, 1:2] >= 0.0)
     for axis in range(2):
         rows = result_ref[pl.ds(axis, blocks, stride=8), :]
-        value = jnp.where(mine, dot(partner, rows, HIGH), 0.0)
+        value = sum(dot(partner, part) for part in parts_of(rows, 3))
+        value = jnp.where(mine, value, 0.0)
         for chip in range(2):
             half = jnp.where(lane < CHIP if chip == 0 else lane >= CHIP, value, 0.0)
-            offsets_ref[axis, chip : chip + 1, :] = dot_nt(ones, half, HIGH)[0:1, :]
+            half = sum(dot_nt(ones, part) for part in parts_of(half, 3))
+            offsets_ref[axis, chip : chip + 1, :] = half[0:1, :]
     sums = [jnp.zeros((8, LANES), F32) for _ in range(dates)]
     per = LANES // dates
     groups = [jnp.zeros((8, LANES), F32) for _ in range(blocks // per)]
@@ -306,7 +315,8 @@
             at = 4 + 2 * axis + chip
             for g, group in enumerate(groups):
                 total = total + inverse_ref[axis, chip, :, g * LANES : (g + 1) * LANES] * group[at : at + 1]
-            series_ref[axis, chip : chip + 1, :] = dot_nt(ones, total, HIGH)[0:1, :]
+            total = sum(dot_nt(ones, part) for part in parts_of(total, 3))
+            series_ref[axis, chip : chip + 1, :] = total[0:1, :]
 
 
 def body(images, inverse_blocks, pair_first, pair_block, pair_second, pair_count, shifts, anchors):
@@ -346,6 +356,7 @@
             pltpu.VMEM((dates, length, columns), BF16),
             pltpu.VMEM((blocks * 8, columns), F32),
             pltpu.SMEM((blocks,), jnp.int32),
+            pltpu.SMEM((slots,), jnp.int32),
             pltpu.SemaphoreType.DMA((7,)),
         ],
         compiler_params=pltpu.CompilerParams(vmem_limit_bytes=60 * 2**20),
@@ -363,8 +374,8 @@
         scratch_shapes=[
             pltpu.VMEM((dates, length + 2 * SMAX, columns), F32),
             pltpu.VMEM((blocks * 8, columns), F32),
-            pltpu.VMEM((CHIP + 8, columns), jnp.int32),
-            pltpu.SMEM((CHIP + 8, columns), jnp.int32),
+            pltpu.VMEM((8, columns), jnp.int32),
+            pltpu.SMEM((8, columns), jnp.int32),
             pltpu.SMEM((CHIP + BATCH,), jnp.int32),
             pltpu.VMEM((BATCH * length, columns), BF16),
             pltpu.VMEM((BATCH * length, columns), BF16),

time: 67.8 us -> 65.2 us (0.962)
  Pallas kernels: 9.29 us -> 7.68 us
  blocking collectives: 16.8 us -> 15.8 us
    pallas_call x1, Pallas kernels: 4.37 us -> 3.02 us  [body(): pl.pallas_call(match_kernel, out_shape=jax.ShapeDtypeStruct((blocks, 8, c...]
    all_to_all x1, blocking collectives: 16.8 us -> 15.8 us  [body(): lax.all_to_all(result, 'date', split_axis=0, concat_axis=0, tiled=True)]
where the time goes in v3:
time: 65.2 us; the launch traced here: 64.9 us
  waiting for transfers between devices  21.2 us (33%)
  blocking collectives  15.8 us (24%)
  starting transfers between devices  14.3 us (22%)
  Pallas kernels  7.68 us (12%)
  local copies, waits for them, and re-layouts  2.91 us (4%)
  other arithmetic  1.56 us (2%)
  between operations  1.47 us (2%)
    all_to_all x1, waiting for transfers between devices, body(): recv = lax.all_to_all(send, 'date', split_axis=0, concat_axis=0, tiled=True)  21.2 us
    all_to_all x1, blocking collectives, body(): lax.all_to_all(result, 'date', split_axis=0, concat_axis=0, tiled=True)  15.8 us
    all_to_all x1, starting transfers between devices, body(): recv = lax.all_to_all(send, 'date', split_axis=0, concat_axis=0, tiled=True)  9.96 us
    pallas_call x1, Pallas kernels, body(): pl.pallas_call(pack_kernel, out_shape=(jax.ShapeDtypeStruct((blocks, 2 *...  3.4 us
    pallas_call x1, Pallas kernels, body(): pl.pallas_call(match_kernel, out_shape=jax.ShapeDtypeStruct((blocks, 8, c...  3.02 us
    ppermute x1, starting transfers between devices, body(): lax.ppermute(images[:, length - SMAX:, :], 'strip', [(i, i + 1) for i in...  2.4 us
    concatenate x1, local copies, waits for them, and re-layouts, body(): turned = jnp.concatenate([turned, turned], axis=4)  2.22 us
    ppermute x1, starting transfers between devices, body(): lax.ppermute(images[:, :SMAX, :], 'strip', [(i + 1, i) for i in range(end...  1.92 us
  transfers between devices with their start and end apart: 3, of which 1 were waited for; matrix products, arithmetic and copies ran while one was open for 7% of the time, Pallas kernels for 0%

profile of v3, /device:TPU:448, one launch (start us, length us, event | category | flops | bytes accessed | tf_op | source)
XLA Modules:
  0.0 64.9 jit_solution(14746987390072609688)
XLA Ops:
  0.6 0.0 copy-start
  0.6 0.0 copy-start.1
  1.3 3.4 %shard_map.140 = (bf16[32,136,128]{2,1,0:T(8,128)(2,1)}, f32[32,128]{1,0:T(8,128)}) custom-call(s32[32]{0:T(128)} %first_hbm.1, s32[32]{0:T(128)} %bitcast.10, s32[32]{0:T(128)} %second_hbm.1, s32[1]{0:T(128)S(6)} %copy.21.count_hbm, s32[2,2,32]{2,1,0:T(2,128)} %bitcast.9, s32[2]{0:T(128)} %anchors_hbm.1, bf16[16,64,128]{2,1,0:T(8,128)(2,1)} %images_ref.1, ...), custom_call_target="tpu_custom_call" | custom-call | tf_op jit(solution)/shard_map/pallas_call | solution.py:340
  4.8 10.0 %all-to-all-start = ((bf16[32,136,128]{2,1,0:T(8,128)(2,1)}), bf16[32,136,128]{2,1,0:T(8,128)(2,1)S(1)}, u32[]{:S(2)}, u32[]{:S(2)}) async-start(bf16[32,136,128]{2,1,0:T(8,128)(2,1)} %get-tuple-element.9), calls=%async_computation | async-start | bytes 2228224 | tf_op jit(solution)/shard_map/all_to_all | solution.py:367
  14.7 0.0 copy-done
  14.8 1.9 %collective-permute-start.1 = (bf16[16,8,128]{2,1,0:T(8,128)(2,1)S(1)}, bf16[16,8,128]{2,1,0:T(8,128)(2,1)S(1)}, u32[]{:S(2)}, u32[]{:S(2)}) collective-permute-start(bf16[16,8,128]{2,1,0:T(8,128)(2,1)S(1)} %get-tuple-element.14), channel_id=1, source_target_pairs={{32,0},{64,32},{96,64},{128,96},{160,128},{192,160},{224,192},{256... | collective-permute-start | bytes 98312 | tf_op jit(solution)/shard_map/ppermute | solution.py:334
  16.7 2.4 %collective-permute-start = (bf16[16,8,128]{2,1,0:T(8,128)(2,1)S(1)}, bf16[16,8,128]{2,1,0:T(8,128)(2,1)S(1)}, u32[]{:S(2)}, u32[]{:S(2)}) collective-permute-start(bf16[16,8,128]{2,1,0:T(8,128)(2,1)S(1)} %get-tuple-element.15), channel_id=1, source_target_pairs={{0,32},{32,64},{64,96},{96,128},{128,160},{160,192},{192,224},{224... | collective-permute-start | bytes 98312 | tf_op jit(solution)/shard_map/ppermute | solution.py:331
  19.1 0.0 copy-done.1
  19.1 0.4 reshape.13
  19.5 1.6 %pad_maximum_fusion = f32[2,16,16,2,64]{1,4,2,3,0:T(8,128)} fusion(f32[2,16,16,2,32]{1,4,2,3,0:T(8,128)S(1)} %bitcast.8), kind=kLoop, calls=%fused_computation | loop fusion | flops 65536 | bytes 393216 | tf_op jit(solution)/shard_map/concatenate | solution.py:336
  21.0 0.0 copy-start.2
  21.0 0.0 copy-start.3
  21.0 0.0 copy-start.4
  21.0 0.0 copy-start.6
  21.0 0.0 copy-start.5
  21.0 2.2 %copy.20 = f32[2,16,16,2,64]{4,3,2,1,0:T(2,128)S(1)} copy(f32[2,16,16,2,64]{1,4,2,3,0:T(8,128)} %pad_maximum_fusion) | data formatting | bytes 524288 | tf_op jit(solution)/shard_map/concatenate | solution.py:336
  23.3 0.3 reshape.14.turned_ref
  23.6 21.2 %all-to-all-done.recv_ref = bf16[32,136,128]{2,1,0:T(8,128)(2,1)S(1)} async-done(((bf16[32,136,128]{2,1,0:T(8,128)(2,1)}), bf16[32,136,128]{2,1,0:T(8,128)(2,1)S(1)}, u32[]{:S(2)}, u32[]{:S(2)}) %all-to-all-start) | async-done | bytes 1114144 | tf_op jit(solution)/shard_map/all_to_all | solution.py:367
  44.8 0.0 collective-permute-done.1.below_ref
  44.8 0.0 collective-permute-done.above_ref
  44.8 0.0 copy-done.2
  44.8 0.0 copy-done.3
  44.8 0.0 copy-done.4
  44.8 0.0 copy-done.6
  44.8 3.0 %shard_map.141 = f32[32,8,128]{2,1,0:T(8,128)S(1)} custom-call(bf16[32,136,128]{2,1,0:T(8,128)(2,1)S(1)} %all-to-all-done.recv_ref, bf16[16,64,128]{2,1,0:T(8,128)(2,1)S(1)} %copy-done, bf16[16,8,128]{2,1,0:T(8,128)(2,1)S(1)} %collective-permute-done.above_ref, bf16[16,8,128]{2,1,0:T(8,128)(2,1)S(1)} %collective-permute-done.1.below_ref, ...), custom_call_target="tpu_custom_call" | custom-call | tf_op jit(solution)/shard_map/pallas_call | solution.py:369
  47.8 15.8 %all_to_all.10 = f32[32,8,128]{2,1,0:T(8,128)S(1)} all-to-all(f32[32,8,128]{2,1,0:T(8,128)S(1)} %shard_map.141), channel_id=1, replica_groups=mesh['strip'=16,'date'=32] {'date'}, dimensions={0} | all-to-all | bytes 262144 | tf_op jit(solution)/shard_map/all_to_all | solution.py:389
  63.6 0.0 copy-done.5
  63.6 1.3 %shard_map.142 = (f32[2,2,32]{2,1,0:T(2,128)}, f32[2,2,16]{2,1,0:T(2,128)}) custom-call(f32[32,128]{1,0:T(8,128)S(1)} %copy-done.5, f32[256,128]{1,0:T(8,128)S(1)} %bitcast.7, f32[2,2,16,512]{3,2,1,0:T(8,128)S(1)} %copy-done.1, f32[2,16,16,128]{3,2,1,0:T(8,128)S(1)} %reshape.14.turned_ref), custom_call_target="tpu_custom_call" | custom-call | tf_op jit(solution)/shard_map/pallas_call | solution.py:390
  (1 shorter events, 0.0 us)
Async XLA Ops:
  0.6 14.1 %copy-start = (bf16[16,64,128]{2,1,0:T(8,128)(2,1)S(1)}, bf16[16,64,128]{2,1,0:T(8,128)(2,1)}, u32[]{:S(2)}) copy-start(bf16[16,64,128]{2,1,0:T(8,128)(2,1)} %images_ref.1) | copy-start | bytes 786436
  0.6 18.5 %copy-start.1 = (f32[2,2,16,512]{3,2,1,0:T(8,128)S(1)}, f32[2,2,16,512]{3,2,1,0:T(8,128)}, u32[]{:S(2)}) copy-start(f32[2,2,16,512]{3,2,1,0:T(8,128)} %inverse_ref.1) | copy-start | bytes 393220
  4.8 40.0 %all-to-all-start = ((bf16[32,136,128]{2,1,0:T(8,128)(2,1)}), bf16[32,136,128]{2,1,0:T(8,128)(2,1)S(1)}, u32[]{:S(2)}, u32[]{:S(2)}) async-start(bf16[32,136,128]{2,1,0:T(8,128)(2,1)} %get-tuple-element.9), calls=%async_computation | async-start | bytes 2228224 | tf_op jit(solution)/shard_map/all_to_all | solution.py:367
  14.8 30.0 %collective-permute-start.1 = (bf16[16,8,128]{2,1,0:T(8,128)(2,1)S(1)}, bf16[16,8,128]{2,1,0:T(8,128)(2,1)S(1)}, u32[]{:S(2)}, u32[]{:S(2)}) collective-permute-start(bf16[16,8,128]{2,1,0:T(8,128)(2,1)S(1)} %get-tuple-element.14), channel_id=1, source_target_pairs={{32,0},{64,32},{96,64},{128,96},{160,128},{192,160},{224,192},{256... | collective-permute-start | bytes 98312 | tf_op jit(solution)/shard_map/ppermute | solution.py:334
  16.7 28.1 %collective-permute-start = (bf16[16,8,128]{2,1,0:T(8,128)(2,1)S(1)}, bf16[16,8,128]{2,1,0:T(8,128)(2,1)S(1)}, u32[]{:S(2)}, u32[]{:S(2)}) collective-permute-start(bf16[16,8,128]{2,1,0:T(8,128)(2,1)S(1)} %get-tuple-element.15), channel_id=1, source_target_pairs={{0,32},{32,64},{64,96},{96,128},{128,160},{160,192},{192,224},{224... | collective-permute-start | bytes 98312 | tf_op jit(solution)/shard_map/ppermute | solution.py:331
  21.0 23.8 %copy-start.2 = (bf16[128,256]{1,0:T(8,128)(2,1)S(1)}, bf16[128,256]{1,0:T(8,128)(2,1)}, u32[]{:S(2)}) copy-start(bf16[128,256]{1,0:T(8,128)(2,1)} %constant.12.clone.table_ref) | copy-start | bytes 196612
  21.0 23.8 %copy-start.3 = (bf16[64,64]{1,0:T(8,128)(2,1)S(1)}, bf16[64,64]{1,0:T(8,128)(2,1)}, u32[]{:S(2)}) copy-start(bf16[64,64]{1,0:T(8,128)(2,1)} %constant.13.clone.forward_ref) | copy-start | bytes 24580
  21.0 23.8 %copy-start.4 = (bf16[128,128]{1,0:T(8,128)(2,1)S(1)}, bf16[128,128]{1,0:T(8,128)(2,1)}, u32[]{:S(2)}) copy-start(bf16[128,128]{1,0:T(8,128)(2,1)} %constant.15.clone.across_ref) | copy-start | bytes 98308
  21.0 23.8 %copy-start.6 = (bf16[64,64]{1,0:T(8,128)(2,1)S(1)}, bf16[64,64]{1,0:T(8,128)(2,1)}, u32[]{:S(2)}) copy-start(bf16[64,64]{1,0:T(8,128)(2,1)} %constant.14.clone.form_ref) | copy-start | bytes 24580
  21.0 42.6 %copy-start.5 = (f32[32,128]{1,0:T(8,128)S(1)}, f32[32,128]{1,0:T(8,128)}, u32[]{:S(2)}) copy-start(f32[32,128]{1,0:T(8,128)} %get-tuple-element.8.own_ref) | copy-start | bytes 49156

commit v4 on v3

--- a/solution.py
+++ b/solution.py
@@ -260,27 +260,27 @@
     live = fact[0:1] > 0.5
     down = jnp.where(live, jnp.where(low, fact[2:3], fact[4:5]) + tall, 0.0)
     across = jnp.where(live, jnp.where(low, fact[7:8], fact[8:9]) + wide, 0.0)
-    row = lax.broadcasted_iota(jnp.int32, (LANES, LANES), 0).astype(F32)
-    base = (lax.rem(lax.axis_index("date"), LANES // dates) * dates).astype(F32)
-    chosen = (row == fact[1:2] + base).astype(F32).astype(BF16)
-    value = jnp.where(row8 < 6, down, across)
-    value = jnp.where((row8 >= 4) & ((row8 % 2 == 0) == (lane8 < CHIP)), value, 0.0)
-    result = dot_nt(jnp.concatenate(parts_of(value, 3), axis=0), chosen)
-    result = result[:8] + result[8:16] + result[16:24]
-    result = jnp.where(row8 == 0, down, result)
-    result = jnp.where(row8 == 1, across, result)
-    result = jnp.where(row8 == 2, fact[6:7], result)
+    row = lax.broadcasted_iota(jnp.int32, (LANES, LANES), 0)
+    row = jnp.where(row < CHIP, -1, row % dates).astype(F32)
+    chosen = (row == fact[1:2]).astype(F32).astype(BF16)
+    value = jnp.where(row8 < 2, down, across)
+    value = jnp.where((row8 < 4) & ((row8 % 2 == 0) == (lane8 < CHIP)), value, 0.0)
+    sums = dot_nt(jnp.concatenate(parts_of(value, 3), axis=0), chosen)
+    sums = sums[:8] + sums[8:16] + sums[16:24]
+    sums = jnp.where((lane8 - CHIP) // dates == row8, sums, 0.0)
+    sums = jnp.sum(sums, axis=0, keepdims=True)
+    sums = jnp.where(low, fact[6:7], sums)
+    result = jnp.where(row8 == 0, down, jnp.where(row8 == 1, across, sums))
     for block in range(blocks):
-        out_ref[block] = result
+        out_ref[block] = result[:4]
 
 
 def series_kernel(
-    own_ref, result_ref, inverse_ref, turned_ref, offsets_ref, series_ref
+    own_ref, result_ref, firsts_ref, seconds_ref, offsets_ref, series_ref
 ):
-    blocks = result_ref.shape[0] // 8
+    blocks = result_ref.shape[0] // 4
     slots = own_ref.shape[0]
-    dates = inverse_ref.shape[2]
-    ones = jnp.ones((8, LANES), F32).astype(BF16)
+    dates = seconds_ref.shape[0]
     me = lax.axis_index("date").astype(F32)
     own = own_ref[...]
     partner = lax.broadcasted_iota(jnp.int32, (slots, blocks), 1).astype(F32)
@@ -288,35 +288,30 @@
     lane = lax.broadcasted_iota(jnp.int32, (slots, LANES), 1)
     mine = lane.astype(F32) - me == own[:, 1:2] + jnp.where(lane < CHIP, 0.0, float(CHIP))
     mine = mine & (own[:, 1:2] >= 0.0)
+    facts = result_ref[pl.ds(2, blocks, stride=4), :]
+    low = lax.broadcasted_iota(jnp.int32, (blocks, LANES), 1) < CHIP
+    first = jnp.where(low, facts, pltpu.roll(facts, CHIP, 1))
+    lane8 = lax.broadcasted_iota(jnp.int32, (8, LANES), 1)
+    row8 = lax.broadcasted_iota(jnp.int32, (8, LANES), 0)
+    chips = (lane8 // CHIP == row8).astype(F32).astype(BF16)
+    pieces = ((lane8 - CHIP) // dates == row8).astype(F32).astype(BF16)
+    total = jnp.concatenate(
+        [jnp.sum(seconds_ref[date] * facts, axis=0, keepdims=True) for date in range(dates)],
+        axis=0,
+    )
+    gained = sum(dot_nt(pieces, part) for part in parts_of(total, 3))
     for axis in range(2):
-        rows = result_ref[pl.ds(axis, blocks, stride=8), :]
+        rows = result_ref[pl.ds(axis, blocks, stride=4), :]
         value = sum(dot(partner, part) for part in parts_of(rows, 3))
         value = jnp.where(mine, value, 0.0)
-        for chip in range(2):
-            half = jnp.where(lane < CHIP if chip == 0 else lane >= CHIP, value, 0.0)
-            half = sum(dot_nt(ones, part) for part in parts_of(half, 3))
-            offsets_ref[axis, chip : chip + 1, :] = half[0:1, :]
-    sums = [jnp.zeros((8, LANES), F32) for _ in range(dates)]
-    per = LANES // dates
-    groups = [jnp.zeros((8, LANES), F32) for _ in range(blocks // per)]
-    for block in range(blocks):
-        value = result_ref[block * 8 : block * 8 + 8, :]
-        first = jnp.broadcast_to(value[2:3], (8, LANES))
+        value = sum(dot_nt(chips, part) for part in parts_of(value, 3))
+        offsets_ref[axis] = value[:2]
+        total = jnp.zeros((dates, LANES), F32)
         for date in range(dates):
-            sums[date] = sums[date] + jnp.where(first == date, value, 0.0)
-        groups[block // per] = groups[block // per] + value
-    low = lax.broadcasted_iota(jnp.int32, (dates, LANES), 1) < CHIP
-    for axis in range(2):
-        own = jnp.zeros((dates, LANES), F32)
-        for date in range(dates):
-            own = own + turned_ref[axis, date] * sums[date][axis : axis + 1]
-        for chip in range(2):
-            total = jnp.where(low if chip == 0 else ~low, -own, 0.0)
-            at = 4 + 2 * axis + chip
-            for g, group in enumerate(groups):
-                total = total + inverse_ref[axis, chip, :, g * LANES : (g + 1) * LANES] * group[at : at + 1]
-            total = sum(dot_nt(ones, part) for part in parts_of(total, 3))
-            series_ref[axis, chip : chip + 1, :] = total[0:1, :]
+            here = jnp.sum(jnp.where(first == date, rows, 0.0), axis=0, keepdims=True)
+            total = total + firsts_ref[axis, date] * here
+        lost = sum(dot_nt(chips, part) for part in parts_of(total, 3))
+        series_ref[axis] = gained[2 * axis : 2 * axis + 2] - lost[:2]
 
 
 def body(images, inverse_blocks, pair_first, pair_block, pair_second, pair_count, shifts, anchors):
@@ -335,7 +330,9 @@
     turned = inverse_blocks.reshape(2, 2, dates, blocks, dates).transpose(0, 4, 2, 1, 3)
     turned = jnp.concatenate([turned, turned], axis=4)
     turned = jnp.pad(turned, ((0, 0),) * 4 + ((0, CHIP - 2 * blocks),))
-    turned = turned.reshape(2, dates, dates, LANES)
+    firsts = turned.reshape(2, dates, dates, LANES)
+    seconds = inverse_blocks.reshape(2, 2, dates, blocks, dates).transpose(2, 3, 0, 1, 4)
+    seconds = jnp.pad(seconds.reshape(dates, blocks, 4 * dates), ((0, 0), (0, 0), (CHIP, 0)))
     near_table, far_table, forward, form, across = [jnp.asarray(t) for t in make_tables()]
     send, own = pl.pallas_call(
         pack_kernel,
@@ -365,10 +362,10 @@
         jnp.transpose(shifts, (1, 2, 0)), anchors, images, near_table, forward,
     )
     recv = lax.all_to_all(send, "date", split_axis=0, concat_axis=0, tiled=True)
-    recv, turned = lax.optimization_barrier((recv, turned))
+    recv, firsts, seconds = lax.optimization_barrier((recv, firsts, seconds))
     result = pl.pallas_call(
         match_kernel,
-        out_shape=jax.ShapeDtypeStruct((blocks, 8, columns), F32),
+        out_shape=jax.ShapeDtypeStruct((blocks, 4, columns), F32),
         in_specs=[vmem] * 8,
         out_specs=vmem,
         scratch_shapes=[
@@ -396,7 +393,7 @@
         in_specs=[vmem] * 4,
         out_specs=(vmem, vmem),
         compiler_params=params,
-    )(own, result.reshape(blocks * 8, columns), inverse_blocks, turned)
+    )(own, result.reshape(blocks * 4, columns), firsts, seconds)
     return jnp.transpose(offsets, (2, 0, 1)), series
 
 

time: 65.2 us -> 64.9 us (level)
  waiting for transfers between devices: 21.2 us -> 19.3 us
  starting transfers between devices: 14.3 us -> 15.5 us
    all_to_all x1, waiting for transfers between devices: 21.2 us -> 19.3 us  [body(): recv = lax.all_to_all(send, 'date', split_axis=0, concat_axis=0, tiled=True)]
    ppermute x1, starting transfers between devices: 1.92 us -> 3.64 us  [body(): lax.ppermute(images[:, :SMAX, :], 'strip', [(i + 1, i) for i in range(end...]
  transfers between devices with their start and end apart: 3 -> 3, of which waited for: 1 -> 1; matrix products, arithmetic and copies ran while one was open for 7% -> 8% of each run, Pallas kernels for 0% -> 0%
where the time goes in v4:
time: 64.9 us; the launch traced here: 64.5 us
  waiting for transfers between devices  19.3 us (30%)
  blocking collectives  15.6 us (24%)
  starting transfers between devices  15.5 us (24%)
  Pallas kernels  7.43 us (11%)
  local copies, waits for them, and re-layouts  3.52 us (5%)
  other arithmetic  1.56 us (2%)
  between operations  1.51 us (2%)
    all_to_all x1, waiting for transfers between devices, body(): recv = lax.all_to_all(send, 'date', split_axis=0, concat_axis=0, tiled=True)  19.3 us
    all_to_all x1, blocking collectives, body(): lax.all_to_all(result, 'date', split_axis=0, concat_axis=0, tiled=True)  15.6 us
    all_to_all x1, starting transfers between devices, body(): recv = lax.all_to_all(send, 'date', split_axis=0, concat_axis=0, tiled=True)  9.96 us
    ppermute x1, starting transfers between devices, body(): lax.ppermute(images[:, :SMAX, :], 'strip', [(i + 1, i) for i in range(end...  3.64 us
    pallas_call x1, Pallas kernels, body(): pl.pallas_call(pack_kernel, out_shape=(jax.ShapeDtypeStruct((blocks, 2 *...  3.4 us
    pallas_call x1, Pallas kernels, body(): pl.pallas_call(match_kernel, out_shape=jax.ShapeDtypeStruct((blocks, 4, c...  3.03 us
    concatenate x1, local copies, waits for them, and re-layouts, body(): turned = jnp.concatenate([turned, turned], axis=4)  2.16 us
    ppermute x1, starting transfers between devices, body(): lax.ppermute(images[:, length - SMAX:, :], 'strip', [(i, i + 1) for i in...  1.92 us
  transfers between devices with their start and end apart: 3, of which 1 were waited for; matrix products, arithmetic and copies ran while one was open for 8% of the time, Pallas kernels for 0%

profile of v4, /device:TPU:448, one launch (start us, length us, event | category | flops | bytes accessed | tf_op | source)
XLA Modules:
  0.0 64.5 jit_solution(14064795917511748421)
XLA Ops:
  0.6 0.0 copy-start
  0.6 0.0 copy-start.6
  1.3 3.4 %shard_map.140 = (bf16[32,136,128]{2,1,0:T(8,128)(2,1)}, f32[32,128]{1,0:T(8,128)}) custom-call(s32[32]{0:T(128)} %first_hbm.1, s32[32]{0:T(128)} %bitcast.14, s32[32]{0:T(128)} %second_hbm.1, s32[1]{0:T(128)S(6)} %copy.28.count_hbm, s32[2,2,32]{2,1,0:T(2,128)} %bitcast.13, s32[2]{0:T(128)} %anchors_hbm.1, bf16[16,64,128]{2,1,0:T(8,128)(2,1)} %images_ref.1, ...), custom_call_target="tpu_custom_call" | custom-call | tf_op jit(solution)/shard_map/pallas_call | solution.py:337
  4.8 10.0 %all-to-all-start = ((bf16[32,136,128]{2,1,0:T(8,128)(2,1)}), bf16[32,136,128]{2,1,0:T(8,128)(2,1)S(1)}, u32[]{:S(2)}, u32[]{:S(2)}) async-start(bf16[32,136,128]{2,1,0:T(8,128)(2,1)} %get-tuple-element.10), calls=%async_computation | async-start | bytes 2228224 | tf_op jit(solution)/shard_map/all_to_all | solution.py:364
  14.7 0.0 copy-done
  14.8 1.9 %collective-permute-start = (bf16[16,8,128]{2,1,0:T(8,128)(2,1)S(1)}, bf16[16,8,128]{2,1,0:T(8,128)(2,1)S(1)}, u32[]{:S(2)}, u32[]{:S(2)}) collective-permute-start(bf16[16,8,128]{2,1,0:T(8,128)(2,1)S(1)} %get-tuple-element.17), channel_id=1, source_target_pairs={{0,32},{32,64},{64,96},{96,128},{128,160},{160,192},{192,224},{224... | collective-permute-start | bytes 98312 | tf_op jit(solution)/shard_map/ppermute | solution.py:326
  16.7 3.6 %collective-permute-start.1 = (bf16[16,8,128]{2,1,0:T(8,128)(2,1)S(1)}, bf16[16,8,128]{2,1,0:T(8,128)(2,1)S(1)}, u32[]{:S(2)}, u32[]{:S(2)}) collective-permute-start(bf16[16,8,128]{2,1,0:T(8,128)(2,1)S(1)} %get-tuple-element.16), channel_id=1, source_target_pairs={{32,0},{64,32},{96,64},{128,96},{160,128},{192,160},{224,192},{256... | collective-permute-start | bytes 98312 | tf_op jit(solution)/shard_map/ppermute | solution.py:329
  20.3 0.0 copy-done.6
  20.3 0.4 reshape.17
  20.7 1.6 %pad_maximum_fusion = f32[2,16,16,2,64]{1,4,2,3,0:T(8,128)} fusion(f32[2,16,16,2,32]{1,4,2,3,0:T(8,128)S(1)} %bitcast.10), kind=kLoop, calls=%fused_computation | loop fusion | flops 65536 | bytes 393216 | tf_op jit(solution)/shard_map/concatenate | solution.py:331
  22.3 2.2 %copy.25 = f32[2,16,16,2,64]{4,3,2,1,0:T(2,128)S(1)} copy(f32[2,16,16,2,64]{1,4,2,3,0:T(8,128)} %pad_maximum_fusion) | data formatting | bytes 524288 | tf_op jit(solution)/shard_map/concatenate | solution.py:331
  24.4 0.0 copy-start.1
  24.4 0.0 copy-start.2
  24.5 0.0 copy-start.3
  24.5 0.0 copy-start.4
  24.5 0.3 reshape.18.firsts_ref
  24.8 0.0 copy-start.5
  24.8 0.3 copy.26
  25.1 0.2 copy.27
  25.3 0.1 pad.4.seconds_ref
  25.5 19.3 %all-to-all-done.recv_ref = bf16[32,136,128]{2,1,0:T(8,128)(2,1)S(1)} async-done(((bf16[32,136,128]{2,1,0:T(8,128)(2,1)}), bf16[32,136,128]{2,1,0:T(8,128)(2,1)S(1)}, u32[]{:S(2)}, u32[]{:S(2)}) %all-to-all-start) | async-done | bytes 1114144 | tf_op jit(solution)/shard_map/all_to_all | solution.py:364
  44.8 0.0 collective-permute-done.above_ref
  44.8 0.0 collective-permute-done.1.below_ref
  44.8 0.0 copy-done.1
  44.8 0.0 copy-done.2
  44.8 0.0 copy-done.3
  44.8 0.0 copy-done.4
  44.8 3.0 %shard_map.141 = f32[32,4,128]{2,1,0:T(4,128)S(1)} custom-call(bf16[32,136,128]{2,1,0:T(8,128)(2,1)S(1)} %all-to-all-done.recv_ref, bf16[16,64,128]{2,1,0:T(8,128)(2,1)S(1)} %copy-done, bf16[16,8,128]{2,1,0:T(8,128)(2,1)S(1)} %collective-permute-done.above_ref, bf16[16,8,128]{2,1,0:T(8,128)(2,1)S(1)} %collective-permute-done.1.below_ref, ...), custom_call_target="tpu_custom_call" | custom-call | tf_op jit(solution)/shard_map/pallas_call | solution.py:366
  47.9 15.6 %all_to_all.10 = f32[32,4,128]{2,1,0:T(4,128)S(1)} all-to-all(f32[32,4,128]{2,1,0:T(4,128)S(1)} %shard_map.141), channel_id=1, replica_groups=mesh['strip'=16,'date'=32] {'date'}, dimensions={0} | all-to-all | bytes 131072 | tf_op jit(solution)/shard_map/all_to_all | solution.py:386
  63.5 0.0 copy-done.5
  63.5 1.0 %shard_map.142 = (f32[2,2,32]{2,1,0:T(2,128)}, f32[2,2,16]{2,1,0:T(2,128)}) custom-call(f32[32,128]{1,0:T(8,128)S(1)} %copy-done.5, f32[128,128]{1,0:T(8,128)S(1)} %bitcast.9, f32[2,16,16,128]{3,2,1,0:T(8,128)S(1)} %reshape.18.firsts_ref, f32[16,32,128]{2,1,0:T(8,128)S(1)} %pad.4.seconds_ref), custom_call_target="tpu_custom_call" | custom-call | tf_op jit(solution)/shard_map/pallas_call | solution.py:387
  (1 shorter events, 0.0 us)
Async XLA Ops:
  0.6 14.1 %copy-start = (bf16[16,64,128]{2,1,0:T(8,128)(2,1)S(1)}, bf16[16,64,128]{2,1,0:T(8,128)(2,1)}, u32[]{:S(2)}) copy-start(bf16[16,64,128]{2,1,0:T(8,128)(2,1)} %images_ref.1) | copy-start | bytes 786436
  0.6 19.7 %copy-start.6 = (f32[2,2,16,512]{3,2,1,0:T(8,128)S(1)}, f32[2,2,16,512]{3,2,1,0:T(8,128)}, u32[]{:S(2)}) copy-start(f32[2,2,16,512]{3,2,1,0:T(8,128)} %param.14) | copy-start | bytes 393220
  4.8 40.0 %all-to-all-start = ((bf16[32,136,128]{2,1,0:T(8,128)(2,1)}), bf16[32,136,128]{2,1,0:T(8,128)(2,1)S(1)}, u32[]{:S(2)}, u32[]{:S(2)}) async-start(bf16[32,136,128]{2,1,0:T(8,128)(2,1)} %get-tuple-element.10), calls=%async_computation | async-start | bytes 2228224 | tf_op jit(solution)/shard_map/all_to_all | solution.py:364
  14.8 30.0 %collective-permute-start = (bf16[16,8,128]{2,1,0:T(8,128)(2,1)S(1)}, bf16[16,8,128]{2,1,0:T(8,128)(2,1)S(1)}, u32[]{:S(2)}, u32[]{:S(2)}) collective-permute-start(bf16[16,8,128]{2,1,0:T(8,128)(2,1)S(1)} %get-tuple-element.17), channel_id=1, source_target_pairs={{0,32},{32,64},{64,96},{96,128},{128,160},{160,192},{192,224},{224... | collective-permute-start | bytes 98312 | tf_op jit(solution)/shard_map/ppermute | solution.py:326
  16.7 28.1 %collective-permute-start.1 = (bf16[16,8,128]{2,1,0:T(8,128)(2,1)S(1)}, bf16[16,8,128]{2,1,0:T(8,128)(2,1)S(1)}, u32[]{:S(2)}, u32[]{:S(2)}) collective-permute-start(bf16[16,8,128]{2,1,0:T(8,128)(2,1)S(1)} %get-tuple-element.16), channel_id=1, source_target_pairs={{32,0},{64,32},{96,64},{128,96},{160,128},{192,160},{224,192},{256... | collective-permute-start | bytes 98312 | tf_op jit(solution)/shard_map/ppermute | solution.py:329
  24.4 20.3 %copy-start.1 = (bf16[64,64]{1,0:T(8,128)(2,1)S(1)}, bf16[64,64]{1,0:T(8,128)(2,1)}, u32[]{:S(2)}) copy-start(bf16[64,64]{1,0:T(8,128)(2,1)} %constant.15.clone.forward_ref) | copy-start | bytes 24580
  24.4 20.3 %copy-start.2 = (bf16[128,256]{1,0:T(8,128)(2,1)S(1)}, bf16[128,256]{1,0:T(8,128)(2,1)}, u32[]{:S(2)}) copy-start(bf16[128,256]{1,0:T(8,128)(2,1)} %constant.14.clone.table_ref) | copy-start | bytes 196612
  24.5 20.3 %copy-start.3 = (bf16[128,128]{1,0:T(8,128)(2,1)S(1)}, bf16[128,128]{1,0:T(8,128)(2,1)}, u32[]{:S(2)}) copy-start(bf16[128,128]{1,0:T(8,128)(2,1)} %constant.17.clone.across_ref) | copy-start | bytes 98308
  24.5 20.3 %copy-start.4 = (bf16[64,64]{1,0:T(8,128)(2,1)S(1)}, bf16[64,64]{1,0:T(8,128)(2,1)}, u32[]{:S(2)}) copy-start(bf16[64,64]{1,0:T(8,128)(2,1)} %constant.16.clone.form_ref) | copy-start | bytes 24580
  24.8 38.7 %copy-start.5 = (f32[32,128]{1,0:T(8,128)S(1)}, f32[32,128]{1,0:T(8,128)}, u32[]{:S(2)}) copy-start(f32[32,128]{1,0:T(8,128)} %get-tuple-element.9.own_ref) | copy-start | bytes 49156

commit v5 on v4

--- a/solution.py
+++ b/solution.py
@@ -12,7 +12,7 @@
 SMAX = 8
 CHIP = 64
 LANES = 128
-BATCH = 16
+BATCH = 32
 F32 = jnp.float32
 BF16 = jnp.bfloat16
 
@@ -71,8 +71,8 @@
 
 def pack_kernel(
     first_hbm, block_hbm, second_hbm, count_hbm, shifts_hbm, anchors_hbm, images_hbm,
-    table_ref, forward_ref,
-    send_ref, own_ref, images_ref,
+    table_hbm, forward_hbm,
+    send_ref, own_ref, images_ref, table_ref, forward_ref,
     first_ref, block_ref, second_ref, count_ref, shifts_ref, anchors_ref,
     near_ref, facts_ref, tally_ref, where_ref, sems,
 ):
@@ -85,7 +85,7 @@
             (
                 (anchors_hbm, anchors_ref), (first_hbm, first_ref), (block_hbm, block_ref),
                 (second_hbm, second_ref), (count_hbm, count_ref), (shifts_hbm, shifts_ref),
-                (images_hbm, images_ref),
+                (table_hbm, table_ref), (forward_hbm, forward_ref), (images_hbm, images_ref),
             )
         )
     ]
@@ -94,7 +94,7 @@
     facts_ref[...] = jnp.zeros(facts_ref.shape, F32)
     for block in range(blocks):
         tally_ref[block] = 0
-    for copy in copies[:-1]:
+    for copy in copies[:6]:
         copy.wait()
     place = lax.broadcasted_iota(jnp.int32, (1, LANES), 1)
     for slot in range(slots):
@@ -118,6 +118,8 @@
     lane = lax.broadcasted_iota(jnp.int32, (LANES, LANES), 1)
     column = lane + jnp.where(lane < CHIP, anchors_ref[0], anchors_ref[1] - CHIP)
     pick = (row == column).astype(F32).astype(BF16)
+    for copy in copies[6:8]:
+        copy.wait()
     table = dot(pick, table_ref[...]).astype(BF16)
     level = level_lanes()
     copies[-1].wait()
@@ -340,10 +342,12 @@
             jax.ShapeDtypeStruct((blocks, 2 * length + 8, columns), BF16),
             jax.ShapeDtypeStruct((slots, columns), F32),
         ),
-        in_specs=[hbm] * 7 + [vmem] * 2,
+        in_specs=[hbm] * 9,
         out_specs=(vmem, vmem),
         scratch_shapes=[
             pltpu.VMEM(images.shape, BF16),
+            pltpu.VMEM(near_table.shape, BF16),
+            pltpu.VMEM(forward.shape, BF16),
             pltpu.SMEM((slots,), jnp.int32),
             pltpu.SMEM((slots,), jnp.int32),
             pltpu.SMEM((slots,), jnp.int32),
@@ -354,7 +358,7 @@
             pltpu.VMEM((blocks * 8, columns), F32),
             pltpu.SMEM((blocks,), jnp.int32),
             pltpu.SMEM((slots,), jnp.int32),
-            pltpu.SemaphoreType.DMA((7,)),
+            pltpu.SemaphoreType.DMA((9,)),
         ],
         compiler_params=pltpu.CompilerParams(vmem_limit_bytes=60 * 2**20),
     )(

time: 64.9 us -> 63.9 us (0.985)
  Pallas kernels: 7.43 us -> 6.49 us
    pallas_call x1, Pallas kernels: 3.4 us -> 2.72 us  [body(): pl.pallas_call(pack_kernel, out_shape=(jax.ShapeDtypeStruct((blocks, 2 *...]
where the time goes in v5:
time: 63.9 us; the launch traced here: 63.6 us
  waiting for transfers between devices  19.3 us (30%)
  blocking collectives  15.7 us (25%)
  starting transfers between devices  15.5 us (24%)
  Pallas kernels  6.49 us (10%)
  local copies, waits for them, and re-layouts  3.52 us (6%)
  other arithmetic  1.56 us (2%)
  between operations  1.51 us (2%)
    all_to_all x1, waiting for transfers between devices, body(): recv = lax.all_to_all(send, 'date', split_axis=0, concat_axis=0, tiled=True)  19.3 us
    all_to_all x1, blocking collectives, body(): lax.all_to_all(result, 'date', split_axis=0, concat_axis=0, tiled=True)  15.7 us
    all_to_all x1, starting transfers between devices, body(): recv = lax.all_to_all(send, 'date', split_axis=0, concat_axis=0, tiled=True)  9.96 us
    ppermute x1, starting transfers between devices, body(): lax.ppermute(images[:, :SMAX, :], 'strip', [(i + 1, i) for i in range(end...  3.64 us
    pallas_call x1, Pallas kernels, body(): pl.pallas_call(match_kernel, out_shape=jax.ShapeDtypeStruct((blocks, 4, c...  2.77 us
    pallas_call x1, Pallas kernels, body(): pl.pallas_call(pack_kernel, out_shape=(jax.ShapeDtypeStruct((blocks, 2 *...  2.72 us
    concatenate x1, local copies, waits for them, and re-layouts, body(): turned = jnp.concatenate([turned, turned], axis=4)  2.16 us
    ppermute x1, starting transfers between devices, body(): lax.ppermute(images[:, length - SMAX:, :], 'strip', [(i, i + 1) for i in...  1.92 us
  transfers between devices with their start and end apart: 3, of which 1 were waited for; matrix products, arithmetic and copies ran while one was open for 8% of the time, Pallas kernels for 0%

profile of v5, /device:TPU:448, one launch (start us, length us, event | category | flops | bytes accessed | tf_op | source)
XLA Modules:
  0.0 63.6 jit_solution(12721990530525557882)
XLA Ops:
  0.6 0.0 copy-start
  0.6 0.0 copy-start.6
  1.3 2.7 %shard_map.140 = (bf16[32,136,128]{2,1,0:T(8,128)(2,1)}, f32[32,128]{1,0:T(8,128)}) custom-call(s32[32]{0:T(128)} %first_hbm.1, s32[32]{0:T(128)} %bitcast.14, s32[32]{0:T(128)} %second_hbm.1, s32[1]{0:T(128)S(6)} %copy.28.count_hbm, s32[2,2,32]{2,1,0:T(2,128)} %bitcast.13, s32[2]{0:T(128)} %anchors_hbm.1, bf16[16,64,128]{2,1,0:T(8,128)(2,1)} %images_ref.1, ...), custom_call_target="tpu_custom_call" | custom-call | tf_op jit(solution)/shard_map/pallas_call | solution.py:339
  4.1 10.0 %all-to-all-start = ((bf16[32,136,128]{2,1,0:T(8,128)(2,1)}), bf16[32,136,128]{2,1,0:T(8,128)(2,1)S(1)}, u32[]{:S(2)}, u32[]{:S(2)}) async-start(bf16[32,136,128]{2,1,0:T(8,128)(2,1)} %get-tuple-element.10), calls=%async_computation | async-start | bytes 2228224 | tf_op jit(solution)/shard_map/all_to_all | solution.py:368
  14.0 0.0 copy-done
  14.1 1.9 %collective-permute-start = (bf16[16,8,128]{2,1,0:T(8,128)(2,1)S(1)}, bf16[16,8,128]{2,1,0:T(8,128)(2,1)S(1)}, u32[]{:S(2)}, u32[]{:S(2)}) collective-permute-start(bf16[16,8,128]{2,1,0:T(8,128)(2,1)S(1)} %get-tuple-element.17), channel_id=1, source_target_pairs={{0,32},{32,64},{64,96},{96,128},{128,160},{160,192},{192,224},{224... | collective-permute-start | bytes 98312 | tf_op jit(solution)/shard_map/ppermute | solution.py:328
  16.0 3.6 %collective-permute-start.1 = (bf16[16,8,128]{2,1,0:T(8,128)(2,1)S(1)}, bf16[16,8,128]{2,1,0:T(8,128)(2,1)S(1)}, u32[]{:S(2)}, u32[]{:S(2)}) collective-permute-start(bf16[16,8,128]{2,1,0:T(8,128)(2,1)S(1)} %get-tuple-element.16), channel_id=1, source_target_pairs={{32,0},{64,32},{96,64},{128,96},{160,128},{192,160},{224,192},{256... | collective-permute-start | bytes 98312 | tf_op jit(solution)/shard_map/ppermute | solution.py:331
  19.7 0.0 copy-done.6
  19.7 0.4 reshape.17
  20.0 1.6 %pad_maximum_fusion = f32[2,16,16,2,64]{1,4,2,3,0:T(8,128)} fusion(f32[2,16,16,2,32]{1,4,2,3,0:T(8,128)S(1)} %bitcast.10), kind=kLoop, calls=%fused_computation | loop fusion | flops 65536 | bytes 393216 | tf_op jit(solution)/shard_map/concatenate | solution.py:333
  21.6 2.2 %copy.25 = f32[2,16,16,2,64]{4,3,2,1,0:T(2,128)S(1)} copy(f32[2,16,16,2,64]{1,4,2,3,0:T(8,128)} %pad_maximum_fusion) | data formatting | bytes 524288 | tf_op jit(solution)/shard_map/concatenate | solution.py:333
  23.8 0.0 copy-start.1
  23.8 0.0 copy-start.2
  23.8 0.0 copy-start.3
  23.8 0.0 copy-start.4
  23.8 0.3 reshape.18.firsts_ref
  24.1 0.0 copy-start.5
  24.1 0.3 copy.26
  24.4 0.2 copy.27
  24.6 0.1 pad.4.seconds_ref
  24.8 19.3 %all-to-all-done.recv_ref = bf16[32,136,128]{2,1,0:T(8,128)(2,1)S(1)} async-done(((bf16[32,136,128]{2,1,0:T(8,128)(2,1)}), bf16[32,136,128]{2,1,0:T(8,128)(2,1)S(1)}, u32[]{:S(2)}, u32[]{:S(2)}) %all-to-all-start) | async-done | bytes 1114144 | tf_op jit(solution)/shard_map/all_to_all | solution.py:368
  44.1 0.0 collective-permute-done.above_ref
  44.1 0.0 collective-permute-done.1.below_ref
  44.1 0.0 copy-done.1
  44.1 0.0 copy-done.2
  44.1 0.0 copy-done.3
  44.1 0.0 copy-done.4
  44.1 2.8 %shard_map.141 = f32[32,4,128]{2,1,0:T(4,128)S(1)} custom-call(bf16[32,136,128]{2,1,0:T(8,128)(2,1)S(1)} %all-to-all-done.recv_ref, bf16[16,64,128]{2,1,0:T(8,128)(2,1)S(1)} %copy-done, bf16[16,8,128]{2,1,0:T(8,128)(2,1)S(1)} %collective-permute-done.above_ref, bf16[16,8,128]{2,1,0:T(8,128)(2,1)S(1)} %collective-permute-done.1.below_ref, ...), custom_call_target="tpu_custom_call" | custom-call | tf_op jit(solution)/shard_map/pallas_call | solution.py:370
  46.9 15.7 %all_to_all.10 = f32[32,4,128]{2,1,0:T(4,128)S(1)} all-to-all(f32[32,4,128]{2,1,0:T(4,128)S(1)} %shard_map.141), channel_id=1, replica_groups=mesh['strip'=16,'date'=32] {'date'}, dimensions={0} | all-to-all | bytes 131072 | tf_op jit(solution)/shard_map/all_to_all | solution.py:390
  62.6 0.0 copy-done.5
  62.6 1.0 %shard_map.142 = (f32[2,2,32]{2,1,0:T(2,128)}, f32[2,2,16]{2,1,0:T(2,128)}) custom-call(f32[32,128]{1,0:T(8,128)S(1)} %copy-done.5, f32[128,128]{1,0:T(8,128)S(1)} %bitcast.9, f32[2,16,16,128]{3,2,1,0:T(8,128)S(1)} %reshape.18.firsts_ref, f32[16,32,128]{2,1,0:T(8,128)S(1)} %pad.4.seconds_ref), custom_call_target="tpu_custom_call" | custom-call | tf_op jit(solution)/shard_map/pallas_call | solution.py:391
  (1 shorter events, 0.0 us)
Async XLA Ops:
  0.6 13.4 %copy-start = (bf16[16,64,128]{2,1,0:T(8,128)(2,1)S(1)}, bf16[16,64,128]{2,1,0:T(8,128)(2,1)}, u32[]{:S(2)}) copy-start(bf16[16,64,128]{2,1,0:T(8,128)(2,1)} %images_ref.1) | copy-start | bytes 786436
  0.6 19.0 %copy-start.6 = (f32[2,2,16,512]{3,2,1,0:T(8,128)S(1)}, f32[2,2,16,512]{3,2,1,0:T(8,128)}, u32[]{:S(2)}) copy-start(f32[2,2,16,512]{3,2,1,0:T(8,128)} %param.14) | copy-start | bytes 393220
  4.1 40.0 %all-to-all-start = ((bf16[32,136,128]{2,1,0:T(8,128)(2,1)}), bf16[32,136,128]{2,1,0:T(8,128)(2,1)S(1)}, u32[]{:S(2)}, u32[]{:S(2)}) async-start(bf16[32,136,128]{2,1,0:T(8,128)(2,1)} %get-tuple-element.10), calls=%async_computation | async-start | bytes 2228224 | tf_op jit(solution)/shard_map/all_to_all | solution.py:368
  14.1 30.0 %collective-permute-start = (bf16[16,8,128]{2,1,0:T(8,128)(2,1)S(1)}, bf16[16,8,128]{2,1,0:T(8,128)(2,1)S(1)}, u32[]{:S(2)}, u32[]{:S(2)}) collective-permute-start(bf16[16,8,128]{2,1,0:T(8,128)(2,1)S(1)} %get-tuple-element.17), channel_id=1, source_target_pairs={{0,32},{32,64},{64,96},{96,128},{128,160},{160,192},{192,224},{224... | collective-permute-start | bytes 98312 | tf_op jit(solution)/shard_map/ppermute | solution.py:328
  16.0 28.1 %collective-permute-start.1 = (bf16[16,8,128]{2,1,0:T(8,128)(2,1)S(1)}, bf16[16,8,128]{2,1,0:T(8,128)(2,1)S(1)}, u32[]{:S(2)}, u32[]{:S(2)}) collective-permute-start(bf16[16,8,128]{2,1,0:T(8,128)(2,1)S(1)} %get-tuple-element.16), channel_id=1, source_target_pairs={{32,0},{64,32},{96,64},{128,96},{160,128},{192,160},{224,192},{256... | collective-permute-start | bytes 98312 | tf_op jit(solution)/shard_map/ppermute | solution.py:331
  23.8 20.3 %copy-start.1 = (bf16[64,64]{1,0:T(8,128)(2,1)S(1)}, bf16[64,64]{1,0:T(8,128)(2,1)}, u32[]{:S(2)}) copy-start(bf16[64,64]{1,0:T(8,128)(2,1)} %constant.15.clone.forward_hbm.forward_ref) | copy-start | bytes 24580
  23.8 20.3 %copy-start.2 = (bf16[128,256]{1,0:T(8,128)(2,1)S(1)}, bf16[128,256]{1,0:T(8,128)(2,1)}, u32[]{:S(2)}) copy-start(bf16[128,256]{1,0:T(8,128)(2,1)} %constant.14.clone.table_ref) | copy-start | bytes 196612
  23.8 20.3 %copy-start.3 = (bf16[128,128]{1,0:T(8,128)(2,1)S(1)}, bf16[128,128]{1,0:T(8,128)(2,1)}, u32[]{:S(2)}) copy-start(bf16[128,128]{1,0:T(8,128)(2,1)} %constant.17.clone.across_ref) | copy-start | bytes 98308
  23.8 20.3 %copy-start.4 = (bf16[64,64]{1,0:T(8,128)(2,1)S(1)}, bf16[64,64]{1,0:T(8,128)(2,1)}, u32[]{:S(2)}) copy-start(bf16[64,64]{1,0:T(8,128)(2,1)} %constant.16.clone.form_ref) | copy-start | bytes 24580
  24.1 38.5 %copy-start.5 = (f32[32,128]{1,0:T(8,128)S(1)}, f32[32,128]{1,0:T(8,128)}, u32[]{:S(2)}) copy-start(f32[32,128]{1,0:T(8,128)} %get-tuple-element.9.own_ref) | copy-start | bytes 49156

commit v6 on v5

--- a/solution.py
+++ b/solution.py
@@ -97,21 +97,25 @@
     for copy in copies[:6]:
         copy.wait()
     place = lax.broadcasted_iota(jnp.int32, (1, LANES), 1)
+    row8 = lax.broadcasted_iota(jnp.int32, (8, LANES), 0)
+    lane8 = lax.broadcasted_iota(jnp.int32, (8, LANES), 1) % CHIP
+    me = lax.axis_index("date")
     for slot in range(slots):
         block = block_ref[slot]
         rank = tally_ref[block]
         tally_ref[block] = rank + 1
         where_ref[slot] = rank
         live = jnp.where(slot < count_ref[0], 1, 0)
-        values = [live, second_ref[slot]]
+        values = [jnp.where(live > 0, second_ref[slot] + 1, 0)]
         for chip in range(2):
             start = shifts_ref[1, chip, slot] + anchors_ref[chip] - chip * CHIP
             values += [shifts_ref[0, chip, slot], start]
         values += [first_ref[slot], shifts_ref[1, 0, slot], shifts_ref[1, 1, slot]]
-        fact = jnp.zeros((1, LANES), jnp.int32)
+        fact = jnp.zeros((8, LANES), jnp.int32)
         for index, value in enumerate(values):
-            fact = jnp.where(place == index, value, fact)
-        facts_ref[pl.ds(block * 8 + rank, 1), :] = fact.astype(F32)
+            fact = jnp.where(row8 == index, value, fact)
+        fact = jnp.where(lane8 == rank * blocks + me, fact, 0)
+        facts_ref[rank, pl.ds(pl.multiple_of(block * 8, 8), 8), :] = fact.astype(F32)
         own = jnp.where(place == 0, block, jnp.where(live > 0, rank * blocks, -1))
         own_ref[slot : slot + 1, :] = own.astype(F32)
     row = lax.broadcasted_iota(jnp.int32, (LANES, LANES), 0)
@@ -136,28 +140,23 @@
         at = pl.multiple_of(where_ref[slot] * CHIP, CHIP)
         send_ref[block_ref[slot], pl.ds(at, CHIP), :] = near_ref[first_ref[slot]]
     send_ref[:, 2 * CHIP : 2 * CHIP + 8, :] = (
-        facts_ref[...].reshape(blocks, 8, LANES).astype(BF16)
+        (facts_ref[0] + facts_ref[1]).reshape(blocks, 8, LANES).astype(BF16)
     )
 
 
 def match_kernel(
     recv_ref, images_ref, above_ref, below_ref,
     table_ref, forward_ref, form_ref, across_ref, out_ref,
-    framed_ref, facts_ref, whole_ref, scalar_ref, list_ref, data_ref, cross_ref,
+    framed_ref, whole_ref, scalar_ref, list_ref, data_ref, cross_ref,
     energy_ref, tall_ref, wide_ref, copy_sem,
 ):
     blocks = recv_ref.shape[0]
     dates = images_ref.shape[0]
     half = CHIP // 2
-    facts_ref[...] = recv_ref[:, 2 * CHIP : 2 * CHIP + 8, :].astype(F32).reshape(blocks * 8, LANES)
-    whole = [facts_ref[pl.ds(rank, blocks, stride=8), :].astype(BF16) for rank in range(2)]
-    if blocks < CHIP // 2:
-        whole.append(jnp.zeros((CHIP - 2 * blocks, LANES), BF16))
-    lane16 = lax.broadcasted_iota(jnp.int32, (16, LANES), 1)
-    row16 = lax.broadcasted_iota(jnp.int32, (16, LANES), 0)
-    choose = (lane16 == row16).astype(F32).astype(BF16)
-    fact = dot_nt(choose, jnp.concatenate(whole + whole, axis=0))
-    whole_ref[...] = fact[:8].astype(jnp.int32)
+    fact = recv_ref[0, 2 * CHIP : 2 * CHIP + 8, :].astype(F32)
+    for block in range(1, blocks):
+        fact = fact + recv_ref[block, 2 * CHIP : 2 * CHIP + 8, :].astype(F32)
+    whole_ref[...] = fact.astype(jnp.int32)
     copy = pltpu.make_async_copy(whole_ref, scalar_ref, copy_sem)
     copy.start()
     framed_ref[:, :SMAX, :] = above_ref[...].astype(F32)
@@ -170,7 +169,7 @@
     count = 0
     for slot in range(2 * blocks):
         list_ref[count] = slot
-        count = count + scalar_ref[0, slot]
+        count = count + jnp.minimum(scalar_ref[0, slot], 1)
     spare = CHIP
     for extra in range(BATCH):
         list_ref[count + extra] = spare
@@ -190,12 +189,12 @@
             source = jnp.where(slot == spare, 0, slot)
             rank = jnp.where(source >= blocks, 1, 0)
             near_of.append((source - rank * blocks, pl.multiple_of(rank * CHIP, CHIP)))
-            second = scalar_ref[1, source]
+            second = jnp.maximum(scalar_ref[0, source] - 1, 0)
             pieces = []
             starts = []
             for chip in range(2):
-                down = scalar_ref[2 + 2 * chip, source] + SMAX
-                start = scalar_ref[3 + 2 * chip, source]
+                down = scalar_ref[1 + 2 * chip, source] + SMAX
+                start = scalar_ref[2 + 2 * chip, source]
                 piece = framed_ref[second, pl.ds(down, CHIP), :]
                 pieces.append(pltpu.roll(piece, lax.rem(LANES - start, LANES), 1))
                 starts.append(start)
@@ -260,18 +259,18 @@
     tall = found[0:1, LANES : 2 * LANES] / norm
     wide = found[1:2, 2 * LANES :] / norm
     live = fact[0:1] > 0.5
-    down = jnp.where(live, jnp.where(low, fact[2:3], fact[4:5]) + tall, 0.0)
-    across = jnp.where(live, jnp.where(low, fact[7:8], fact[8:9]) + wide, 0.0)
+    down = jnp.where(live, jnp.where(low, fact[1:2], fact[3:4]) + tall, 0.0)
+    across = jnp.where(live, jnp.where(low, fact[6:7], fact[7:8]) + wide, 0.0)
     row = lax.broadcasted_iota(jnp.int32, (LANES, LANES), 0)
     row = jnp.where(row < CHIP, -1, row % dates).astype(F32)
-    chosen = (row == fact[1:2]).astype(F32).astype(BF16)
+    chosen = (row == fact[0:1] - 1.0).astype(F32).astype(BF16)
     value = jnp.where(row8 < 2, down, across)
     value = jnp.where((row8 < 4) & ((row8 % 2 == 0) == (lane8 < CHIP)), value, 0.0)
     sums = dot_nt(jnp.concatenate(parts_of(value, 3), axis=0), chosen)
     sums = sums[:8] + sums[8:16] + sums[16:24]
     sums = jnp.where((lane8 - CHIP) // dates == row8, sums, 0.0)
     sums = jnp.sum(sums, axis=0, keepdims=True)
-    sums = jnp.where(low, fact[6:7], sums)
+    sums = jnp.where(low, fact[5:6], sums)
     result = jnp.where(row8 == 0, down, jnp.where(row8 == 1, across, sums))
     for block in range(blocks):
         out_ref[block] = result[:4]
@@ -355,7 +354,7 @@
             pltpu.SMEM((2, 2, slots), jnp.int32),
             pltpu.SMEM((2,), jnp.int32),
             pltpu.VMEM((dates, length, columns), BF16),
-            pltpu.VMEM((blocks * 8, columns), F32),
+            pltpu.VMEM((2, blocks * 8, columns), F32),
             pltpu.SMEM((blocks,), jnp.int32),
             pltpu.SMEM((slots,), jnp.int32),
             pltpu.SemaphoreType.DMA((9,)),
@@ -374,7 +373,6 @@
         out_specs=vmem,
         scratch_shapes=[
             pltpu.VMEM((dates, length + 2 * SMAX, columns), F32),
-            pltpu.VMEM((blocks * 8, columns), F32),
             pltpu.VMEM((8, columns), jnp.int32),
             pltpu.SMEM((8, columns), jnp.int32),
             pltpu.SMEM((CHIP + BATCH,), jnp.int32),

time: 63.9 us -> 63.3 us (level)
  no operation moved by 1% of the time
where the time goes in v6:
time: 63.3 us
  waiting for transfers between devices  19.3 us (30%)
  starting transfers between devices  15.5 us (24%)
  blocking collectives  15.4 us (24%)
  Pallas kernels  6.42 us (10%)
  local copies, waits for them, and re-layouts  3.52 us (6%)
  other arithmetic  1.56 us (2%)
  between operations  1.51 us (2%)
    all_to_all x1, waiting for transfers between devices, body(): recv = lax.all_to_all(send, 'date', split_axis=0, concat_axis=0, tiled=True)  19.3 us
    all_to_all x1, blocking collectives, body(): lax.all_to_all(result, 'date', split_axis=0, concat_axis=0, tiled=True)  15.4 us
    all_to_all x1, starting transfers between devices, body(): recv = lax.all_to_all(send, 'date', split_axis=0, concat_axis=0, tiled=True)  9.96 us
    ppermute x1, starting transfers between devices, body(): lax.ppermute(images[:, :SMAX, :], 'strip', [(i + 1, i) for i in range(end...  3.64 us
    pallas_call x1, Pallas kernels, body(): pl.pallas_call(pack_kernel, out_shape=(jax.ShapeDtypeStruct((blocks, 2 *...  2.75 us
    pallas_call x1, Pallas kernels, body(): pl.pallas_call(match_kernel, out_shape=jax.ShapeDtypeStruct((blocks, 4, c...  2.67 us
    concatenate x1, local copies, waits for them, and re-layouts, body(): turned = jnp.concatenate([turned, turned], axis=4)  2.16 us
    ppermute x1, starting transfers between devices, body(): lax.ppermute(images[:, length - SMAX:, :], 'strip', [(i, i + 1) for i in...  1.92 us
  transfers between devices with their start and end apart: 3, of which 1 were waited for; matrix products, arithmetic and copies ran while one was open for 8% of the time, Pallas kernels for 0%

profile of v6, /device:TPU:448, one launch (start us, length us, event | category | flops | bytes accessed | tf_op | source)
XLA Modules:
  0.0 63.3 jit_solution(15541003722741910095)
XLA Ops:
  0.6 0.0 copy-start
  0.6 0.0 copy-start.6
  1.3 2.7 %shard_map.140 = (bf16[32,136,128]{2,1,0:T(8,128)(2,1)}, f32[32,128]{1,0:T(8,128)}) custom-call(s32[32]{0:T(128)} %first_hbm.1, s32[32]{0:T(128)} %bitcast.14, s32[32]{0:T(128)} %second_hbm.1, s32[1]{0:T(128)S(6)} %copy.28.count_hbm, s32[2,2,32]{2,1,0:T(2,128)} %bitcast.13, s32[2]{0:T(128)} %anchors_hbm.1, bf16[16,64,128]{2,1,0:T(8,128)(2,1)} %images_ref.1, ...), custom_call_target="tpu_custom_call" | custom-call | tf_op jit(solution)/shard_map/pallas_call | solution.py:338
  4.1 10.0 %all-to-all-start = ((bf16[32,136,128]{2,1,0:T(8,128)(2,1)}), bf16[32,136,128]{2,1,0:T(8,128)(2,1)S(1)}, u32[]{:S(2)}, u32[]{:S(2)}) async-start(bf16[32,136,128]{2,1,0:T(8,128)(2,1)} %get-tuple-element.10), calls=%async_computation | async-start | bytes 2228224 | tf_op jit(solution)/shard_map/all_to_all | solution.py:367
  14.1 0.0 copy-done
  14.1 1.9 %collective-permute-start = (bf16[16,8,128]{2,1,0:T(8,128)(2,1)S(1)}, bf16[16,8,128]{2,1,0:T(8,128)(2,1)S(1)}, u32[]{:S(2)}, u32[]{:S(2)}) collective-permute-start(bf16[16,8,128]{2,1,0:T(8,128)(2,1)S(1)} %get-tuple-element.17), channel_id=1, source_target_pairs={{0,32},{32,64},{64,96},{96,128},{128,160},{160,192},{192,224},{224... | collective-permute-start | bytes 98312 | tf_op jit(solution)/shard_map/ppermute | solution.py:327
  16.0 3.6 %collective-permute-start.1 = (bf16[16,8,128]{2,1,0:T(8,128)(2,1)S(1)}, bf16[16,8,128]{2,1,0:T(8,128)(2,1)S(1)}, u32[]{:S(2)}, u32[]{:S(2)}) collective-permute-start(bf16[16,8,128]{2,1,0:T(8,128)(2,1)S(1)} %get-tuple-element.16), channel_id=1, source_target_pairs={{32,0},{64,32},{96,64},{128,96},{160,128},{192,160},{224,192},{256... | collective-permute-start | bytes 98312 | tf_op jit(solution)/shard_map/ppermute | solution.py:330
  19.7 0.0 copy-done.6
  19.7 0.4 reshape.17
  20.1 1.6 %pad_maximum_fusion = f32[2,16,16,2,64]{1,4,2,3,0:T(8,128)} fusion(f32[2,16,16,2,32]{1,4,2,3,0:T(8,128)S(1)} %bitcast.10), kind=kLoop, calls=%fused_computation | loop fusion | flops 65536 | bytes 393216 | tf_op jit(solution)/shard_map/concatenate | solution.py:332
  21.6 2.2 %copy.25 = f32[2,16,16,2,64]{4,3,2,1,0:T(2,128)S(1)} copy(f32[2,16,16,2,64]{1,4,2,3,0:T(8,128)} %pad_maximum_fusion) | data formatting | bytes 524288 | tf_op jit(solution)/shard_map/concatenate | solution.py:332
  23.8 0.0 copy-start.1
  23.8 0.0 copy-start.2
  23.8 0.0 copy-start.3
  23.8 0.0 copy-start.4
  23.8 0.3 reshape.18.firsts_ref
  24.1 0.0 copy-start.5
  24.2 0.3 copy.26
  24.5 0.2 copy.27
  24.7 0.1 pad.4.seconds_ref
  24.8 19.3 %all-to-all-done.recv_ref = bf16[32,136,128]{2,1,0:T(8,128)(2,1)S(1)} async-done(((bf16[32,136,128]{2,1,0:T(8,128)(2,1)}), bf16[32,136,128]{2,1,0:T(8,128)(2,1)S(1)}, u32[]{:S(2)}, u32[]{:S(2)}) %all-to-all-start) | async-done | bytes 1114144 | tf_op jit(solution)/shard_map/all_to_all | solution.py:367
  44.1 0.0 collective-permute-done.above_ref
  44.1 0.0 collective-permute-done.1.below_ref
  44.1 0.0 copy-done.1
  44.1 0.0 copy-done.2
  44.1 0.0 copy-done.3
  44.2 0.0 copy-done.4
  44.2 2.7 %shard_map.141 = f32[32,4,128]{2,1,0:T(4,128)S(1)} custom-call(bf16[32,136,128]{2,1,0:T(8,128)(2,1)S(1)} %all-to-all-done.recv_ref, bf16[16,64,128]{2,1,0:T(8,128)(2,1)S(1)} %copy-done, bf16[16,8,128]{2,1,0:T(8,128)(2,1)S(1)} %collective-permute-done.above_ref, bf16[16,8,128]{2,1,0:T(8,128)(2,1)S(1)} %collective-permute-done.1.below_ref, ...), custom_call_target="tpu_custom_call" | custom-call | tf_op jit(solution)/shard_map/pallas_call | solution.py:369
  46.8 15.4 %all_to_all.10 = f32[32,4,128]{2,1,0:T(4,128)S(1)} all-to-all(f32[32,4,128]{2,1,0:T(4,128)S(1)} %shard_map.141), channel_id=1, replica_groups=mesh['strip'=16,'date'=32] {'date'}, dimensions={0} | all-to-all | bytes 131072 | tf_op jit(solution)/shard_map/all_to_all | solution.py:388
  62.3 0.0 copy-done.5
  62.3 1.0 %shard_map.142 = (f32[2,2,32]{2,1,0:T(2,128)}, f32[2,2,16]{2,1,0:T(2,128)}) custom-call(f32[32,128]{1,0:T(8,128)S(1)} %copy-done.5, f32[128,128]{1,0:T(8,128)S(1)} %bitcast.9, f32[2,16,16,128]{3,2,1,0:T(8,128)S(1)} %reshape.18.firsts_ref, f32[16,32,128]{2,1,0:T(8,128)S(1)} %pad.4.seconds_ref), custom_call_target="tpu_custom_call" | custom-call | tf_op jit(solution)/shard_map/pallas_call | solution.py:389
  (1 shorter events, 0.0 us)
Async XLA Ops:
  0.6 13.4 %copy-start = (bf16[16,64,128]{2,1,0:T(8,128)(2,1)S(1)}, bf16[16,64,128]{2,1,0:T(8,128)(2,1)}, u32[]{:S(2)}) copy-start(bf16[16,64,128]{2,1,0:T(8,128)(2,1)} %images_ref.1) | copy-start | bytes 786436
  0.6 19.0 %copy-start.6 = (f32[2,2,16,512]{3,2,1,0:T(8,128)S(1)}, f32[2,2,16,512]{3,2,1,0:T(8,128)}, u32[]{:S(2)}) copy-start(f32[2,2,16,512]{3,2,1,0:T(8,128)} %param.14) | copy-start | bytes 393220
  4.1 40.0 %all-to-all-start = ((bf16[32,136,128]{2,1,0:T(8,128)(2,1)}), bf16[32,136,128]{2,1,0:T(8,128)(2,1)S(1)}, u32[]{:S(2)}, u32[]{:S(2)}) async-start(bf16[32,136,128]{2,1,0:T(8,128)(2,1)} %get-tuple-element.10), calls=%async_computation | async-start | bytes 2228224 | tf_op jit(solution)/shard_map/all_to_all | solution.py:367
  14.1 30.0 %collective-permute-start = (bf16[16,8,128]{2,1,0:T(8,128)(2,1)S(1)}, bf16[16,8,128]{2,1,0:T(8,128)(2,1)S(1)}, u32[]{:S(2)}, u32[]{:S(2)}) collective-permute-start(bf16[16,8,128]{2,1,0:T(8,128)(2,1)S(1)} %get-tuple-element.17), channel_id=1, source_target_pairs={{0,32},{32,64},{64,96},{96,128},{128,160},{160,192},{192,224},{224... | collective-permute-start | bytes 98312 | tf_op jit(solution)/shard_map/ppermute | solution.py:327
  16.0 28.1 %collective-permute-start.1 = (bf16[16,8,128]{2,1,0:T(8,128)(2,1)S(1)}, bf16[16,8,128]{2,1,0:T(8,128)(2,1)S(1)}, u32[]{:S(2)}, u32[]{:S(2)}) collective-permute-start(bf16[16,8,128]{2,1,0:T(8,128)(2,1)S(1)} %get-tuple-element.16), channel_id=1, source_target_pairs={{32,0},{64,32},{96,64},{128,96},{160,128},{192,160},{224,192},{256... | collective-permute-start | bytes 98312 | tf_op jit(solution)/shard_map/ppermute | solution.py:330
  23.8 20.3 %copy-start.1 = (bf16[64,64]{1,0:T(8,128)(2,1)S(1)}, bf16[64,64]{1,0:T(8,128)(2,1)}, u32[]{:S(2)}) copy-start(bf16[64,64]{1,0:T(8,128)(2,1)} %constant.15.clone.forward_hbm.forward_ref) | copy-start | bytes 24580
  23.8 20.3 %copy-start.2 = (bf16[128,256]{1,0:T(8,128)(2,1)S(1)}, bf16[128,256]{1,0:T(8,128)(2,1)}, u32[]{:S(2)}) copy-start(bf16[128,256]{1,0:T(8,128)(2,1)} %constant.14.clone.table_ref) | copy-start | bytes 196612
  23.8 20.3 %copy-start.3 = (bf16[128,128]{1,0:T(8,128)(2,1)S(1)}, bf16[128,128]{1,0:T(8,128)(2,1)}, u32[]{:S(2)}) copy-start(bf16[128,128]{1,0:T(8,128)(2,1)} %constant.17.clone.across_ref) | copy-start | bytes 98308
  23.8 20.3 %copy-start.4 = (bf16[64,64]{1,0:T(8,128)(2,1)S(1)}, bf16[64,64]{1,0:T(8,128)(2,1)}, u32[]{:S(2)}) copy-start(bf16[64,64]{1,0:T(8,128)(2,1)} %constant.16.clone.form_ref) | copy-start | bytes 24580
  24.1 38.1 %copy-start.5 = (f32[32,128]{1,0:T(8,128)S(1)}, f32[32,128]{1,0:T(8,128)}, u32[]{:S(2)}) copy-start(f32[32,128]{1,0:T(8,128)} %get-tuple-element.9.own_ref) | copy-start | bytes 49156

commit v7 on v5

--- a/solution.py
+++ b/solution.py
@@ -255,7 +255,7 @@
         value = ref[:CHIP, :]
         stack += [jnp.where(even, value, 0.0), jnp.where(even, 0.0, value)]
     weights = weights.astype(BF16)
-    found = sum(dot_nt(weights, part) for part in parts_of(jnp.concatenate(stack, axis=0), 3))
+    found = sum(dot_nt(weights, part) for part in parts_of(jnp.concatenate(stack, axis=0), 2))
     norm = found[0:1, :LANES] + 1e-6
     tall = found[0:1, LANES : 2 * LANES] / norm
     wide = found[1:2, 2 * LANES :] / norm
@@ -267,8 +267,8 @@
     chosen = (row == fact[1:2]).astype(F32).astype(BF16)
     value = jnp.where(row8 < 2, down, across)
     value = jnp.where((row8 < 4) & ((row8 % 2 == 0) == (lane8 < CHIP)), value, 0.0)
-    sums = dot_nt(jnp.concatenate(parts_of(value, 3), axis=0), chosen)
-    sums = sums[:8] + sums[8:16] + sums[16:24]
+    sums = dot_nt(jnp.concatenate(parts_of(value, 2), axis=0), chosen)
+    sums = sums[:8] + sums[8:16]
     sums = jnp.where((lane8 - CHIP) // dates == row8, sums, 0.0)
     sums = jnp.sum(sums, axis=0, keepdims=True)
     sums = jnp.where(low, fact[6:7], sums)
@@ -301,18 +301,18 @@
         [jnp.sum(seconds_ref[date] * facts, axis=0, keepdims=True) for date in range(dates)],
         axis=0,
     )
-    gained = sum(dot_nt(pieces, part) for part in parts_of(total, 3))
+    gained = sum(dot_nt(pieces, part) for part in parts_of(total, 2))
     for axis in range(2):
         rows = result_ref[pl.ds(axis, blocks, stride=4), :]
-        value = sum(dot(partner, part) for part in parts_of(rows, 3))
+        value = sum(dot(partner, part) for part in parts_of(rows, 2))
         value = jnp.where(mine, value, 0.0)
-        value = sum(dot_nt(chips, part) for part in parts_of(value, 3))
+        value = sum(dot_nt(chips, part) for part in parts_of(value, 2))
         offsets_ref[axis] = value[:2]
         total = jnp.zeros((dates, LANES), F32)
         for date in range(dates):
             here = jnp.sum(jnp.where(first == date, rows, 0.0), axis=0, keepdims=True)
             total = total + firsts_ref[axis, date] * here
-        lost = sum(dot_nt(chips, part) for part in parts_of(total, 3))
+        lost = sum(dot_nt(chips, part) for part in parts_of(total, 2))
         series_ref[axis] = gained[2 * axis : 2 * axis + 2] - lost[:2]
 
 

time: 63.9 us -> 63.1 us (0.987)
  blocking collectives: 15.7 us -> 14.9 us
    all_to_all x1, blocking collectives: 15.7 us -> 14.9 us  [body(): lax.all_to_all(result, 'date', split_axis=0, concat_axis=0, tiled=True)]
where the time goes in v7:
time: 63.1 us; the launch traced here: 62.7 us
  waiting for transfers between devices  19.3 us (31%)
  starting transfers between devices  15.5 us (25%)
  blocking collectives  14.9 us (24%)
  Pallas kernels  6.44 us (10%)
  local copies, waits for them, and re-layouts  3.52 us (6%)
  other arithmetic  1.56 us (2%)
  between operations  1.51 us (2%)
    all_to_all x1, waiting for transfers between devices, body(): recv = lax.all_to_all(send, 'date', split_axis=0, concat_axis=0, tiled=True)  19.3 us
    all_to_all x1, blocking collectives, body(): lax.all_to_all(result, 'date', split_axis=0, concat_axis=0, tiled=True)  14.9 us
    all_to_all x1, starting transfers between devices, body(): recv = lax.all_to_all(send, 'date', split_axis=0, concat_axis=0, tiled=True)  9.96 us
    ppermute x1, starting transfers between devices, body(): lax.ppermute(images[:, :SMAX, :], 'strip', [(i + 1, i) for i in range(end...  3.64 us
    pallas_call x1, Pallas kernels, body(): pl.pallas_call(match_kernel, out_shape=jax.ShapeDtypeStruct((blocks, 4, c...  2.74 us
    pallas_call x1, Pallas kernels, body(): pl.pallas_call(pack_kernel, out_shape=(jax.ShapeDtypeStruct((blocks, 2 *...  2.73 us
    concatenate x1, local copies, waits for them, and re-layouts, body(): turned = jnp.concatenate([turned, turned], axis=4)  2.16 us
    ppermute x1, starting transfers between devices, body(): lax.ppermute(images[:, length - SMAX:, :], 'strip', [(i, i + 1) for i in...  1.92 us
  transfers between devices with their start and end apart: 3, of which 1 were waited for; matrix products, arithmetic and copies ran while one was open for 8% of the time, Pallas kernels for 0%

profile of v7, /device:TPU:448, one launch (start us, length us, event | category | flops | bytes accessed | tf_op | source)
XLA Modules:
  0.0 62.7 jit_solution(18191483953652853041)
XLA Ops:
  0.6 0.0 copy-start
  0.6 0.0 copy-start.6
  1.3 2.7 %shard_map.140 = (bf16[32,136,128]{2,1,0:T(8,128)(2,1)}, f32[32,128]{1,0:T(8,128)}) custom-call(s32[32]{0:T(128)} %first_hbm.1, s32[32]{0:T(128)} %bitcast.14, s32[32]{0:T(128)} %second_hbm.1, s32[1]{0:T(128)S(6)} %copy.28.count_hbm, s32[2,2,32]{2,1,0:T(2,128)} %bitcast.13, s32[2]{0:T(128)} %anchors_hbm.1, bf16[16,64,128]{2,1,0:T(8,128)(2,1)} %images_ref.1, ...), custom_call_target="tpu_custom_call" | custom-call | tf_op jit(solution)/shard_map/pallas_call | solution.py:339
  4.1 10.0 %all-to-all-start = ((bf16[32,136,128]{2,1,0:T(8,128)(2,1)}), bf16[32,136,128]{2,1,0:T(8,128)(2,1)S(1)}, u32[]{:S(2)}, u32[]{:S(2)}) async-start(bf16[32,136,128]{2,1,0:T(8,128)(2,1)} %get-tuple-element.10), calls=%async_computation | async-start | bytes 2228224 | tf_op jit(solution)/shard_map/all_to_all | solution.py:368
  14.0 0.0 copy-done
  14.1 1.9 %collective-permute-start = (bf16[16,8,128]{2,1,0:T(8,128)(2,1)S(1)}, bf16[16,8,128]{2,1,0:T(8,128)(2,1)S(1)}, u32[]{:S(2)}, u32[]{:S(2)}) collective-permute-start(bf16[16,8,128]{2,1,0:T(8,128)(2,1)S(1)} %get-tuple-element.17), channel_id=1, source_target_pairs={{0,32},{32,64},{64,96},{96,128},{128,160},{160,192},{192,224},{224... | collective-permute-start | bytes 98312 | tf_op jit(solution)/shard_map/ppermute | solution.py:328
  16.0 3.6 %collective-permute-start.1 = (bf16[16,8,128]{2,1,0:T(8,128)(2,1)S(1)}, bf16[16,8,128]{2,1,0:T(8,128)(2,1)S(1)}, u32[]{:S(2)}, u32[]{:S(2)}) collective-permute-start(bf16[16,8,128]{2,1,0:T(8,128)(2,1)S(1)} %get-tuple-element.16), channel_id=1, source_target_pairs={{32,0},{64,32},{96,64},{128,96},{160,128},{192,160},{224,192},{256... | collective-permute-start | bytes 98312 | tf_op jit(solution)/shard_map/ppermute | solution.py:331
  19.7 0.0 copy-done.6
  19.7 0.4 reshape.17
  20.0 1.6 %pad_maximum_fusion = f32[2,16,16,2,64]{1,4,2,3,0:T(8,128)} fusion(f32[2,16,16,2,32]{1,4,2,3,0:T(8,128)S(1)} %bitcast.10), kind=kLoop, calls=%fused_computation | loop fusion | flops 65536 | bytes 393216 | tf_op jit(solution)/shard_map/concatenate | solution.py:333
  21.6 2.2 %copy.25 = f32[2,16,16,2,64]{4,3,2,1,0:T(2,128)S(1)} copy(f32[2,16,16,2,64]{1,4,2,3,0:T(8,128)} %pad_maximum_fusion) | data formatting | bytes 524288 | tf_op jit(solution)/shard_map/concatenate | solution.py:333
  23.8 0.0 copy-start.1
  23.8 0.0 copy-start.2
  23.8 0.0 copy-start.3
  23.8 0.0 copy-start.4
  23.8 0.3 reshape.18.firsts_ref
  24.1 0.0 copy-start.5
  24.1 0.3 copy.26
  24.4 0.2 copy.27
  24.6 0.1 pad.4.seconds_ref
  24.8 19.3 %all-to-all-done.recv_ref = bf16[32,136,128]{2,1,0:T(8,128)(2,1)S(1)} async-done(((bf16[32,136,128]{2,1,0:T(8,128)(2,1)}), bf16[32,136,128]{2,1,0:T(8,128)(2,1)S(1)}, u32[]{:S(2)}, u32[]{:S(2)}) %all-to-all-start) | async-done | bytes 1114144 | tf_op jit(solution)/shard_map/all_to_all | solution.py:368
  44.1 0.0 collective-permute-done.above_ref
  44.1 0.0 collective-permute-done.1.below_ref
  44.1 0.0 copy-done.1
  44.1 0.0 copy-done.2
  44.1 0.0 copy-done.3
  44.1 0.0 copy-done.4
  44.1 2.7 %shard_map.141 = f32[32,4,128]{2,1,0:T(4,128)S(1)} custom-call(bf16[32,136,128]{2,1,0:T(8,128)(2,1)S(1)} %all-to-all-done.recv_ref, bf16[16,64,128]{2,1,0:T(8,128)(2,1)S(1)} %copy-done, bf16[16,8,128]{2,1,0:T(8,128)(2,1)S(1)} %collective-permute-done.above_ref, bf16[16,8,128]{2,1,0:T(8,128)(2,1)S(1)} %collective-permute-done.1.below_ref, ...), custom_call_target="tpu_custom_call" | custom-call | tf_op jit(solution)/shard_map/pallas_call | solution.py:370
  46.9 14.9 %all_to_all.10 = f32[32,4,128]{2,1,0:T(4,128)S(1)} all-to-all(f32[32,4,128]{2,1,0:T(4,128)S(1)} %shard_map.141), channel_id=1, replica_groups=mesh['strip'=16,'date'=32] {'date'}, dimensions={0} | all-to-all | bytes 131072 | tf_op jit(solution)/shard_map/all_to_all | solution.py:390
  61.8 0.0 copy-done.5
  61.8 1.0 %shard_map.142 = (f32[2,2,32]{2,1,0:T(2,128)}, f32[2,2,16]{2,1,0:T(2,128)}) custom-call(f32[32,128]{1,0:T(8,128)S(1)} %copy-done.5, f32[128,128]{1,0:T(8,128)S(1)} %bitcast.9, f32[2,16,16,128]{3,2,1,0:T(8,128)S(1)} %reshape.18.firsts_ref, f32[16,32,128]{2,1,0:T(8,128)S(1)} %pad.4.seconds_ref), custom_call_target="tpu_custom_call" | custom-call | tf_op jit(solution)/shard_map/pallas_call | solution.py:391
  (1 shorter events, 0.0 us)
Async XLA Ops:
  0.6 13.4 %copy-start = (bf16[16,64,128]{2,1,0:T(8,128)(2,1)S(1)}, bf16[16,64,128]{2,1,0:T(8,128)(2,1)}, u32[]{:S(2)}) copy-start(bf16[16,64,128]{2,1,0:T(8,128)(2,1)} %images_ref.1) | copy-start | bytes 786436
  0.6 19.0 %copy-start.6 = (f32[2,2,16,512]{3,2,1,0:T(8,128)S(1)}, f32[2,2,16,512]{3,2,1,0:T(8,128)}, u32[]{:S(2)}) copy-start(f32[2,2,16,512]{3,2,1,0:T(8,128)} %param.14) | copy-start | bytes 393220
  4.1 40.0 %all-to-all-start = ((bf16[32,136,128]{2,1,0:T(8,128)(2,1)}), bf16[32,136,128]{2,1,0:T(8,128)(2,1)S(1)}, u32[]{:S(2)}, u32[]{:S(2)}) async-start(bf16[32,136,128]{2,1,0:T(8,128)(2,1)} %get-tuple-element.10), calls=%async_computation | async-start | bytes 2228224 | tf_op jit(solution)/shard_map/all_to_all | solution.py:368
  14.1 30.0 %collective-permute-start = (bf16[16,8,128]{2,1,0:T(8,128)(2,1)S(1)}, bf16[16,8,128]{2,1,0:T(8,128)(2,1)S(1)}, u32[]{:S(2)}, u32[]{:S(2)}) collective-permute-start(bf16[16,8,128]{2,1,0:T(8,128)(2,1)S(1)} %get-tuple-element.17), channel_id=1, source_target_pairs={{0,32},{32,64},{64,96},{96,128},{128,160},{160,192},{192,224},{224... | collective-permute-start | bytes 98312 | tf_op jit(solution)/shard_map/ppermute | solution.py:328
  16.0 28.1 %collective-permute-start.1 = (bf16[16,8,128]{2,1,0:T(8,128)(2,1)S(1)}, bf16[16,8,128]{2,1,0:T(8,128)(2,1)S(1)}, u32[]{:S(2)}, u32[]{:S(2)}) collective-permute-start(bf16[16,8,128]{2,1,0:T(8,128)(2,1)S(1)} %get-tuple-element.16), channel_id=1, source_target_pairs={{32,0},{64,32},{96,64},{128,96},{160,128},{192,160},{224,192},{256... | collective-permute-start | bytes 98312 | tf_op jit(solution)/shard_map/ppermute | solution.py:331
  23.8 20.3 %copy-start.1 = (bf16[64,64]{1,0:T(8,128)(2,1)S(1)}, bf16[64,64]{1,0:T(8,128)(2,1)}, u32[]{:S(2)}) copy-start(bf16[64,64]{1,0:T(8,128)(2,1)} %constant.15.clone.forward_hbm.forward_ref) | copy-start | bytes 24580
  23.8 20.3 %copy-start.2 = (bf16[128,256]{1,0:T(8,128)(2,1)S(1)}, bf16[128,256]{1,0:T(8,128)(2,1)}, u32[]{:S(2)}) copy-start(bf16[128,256]{1,0:T(8,128)(2,1)} %constant.14.clone.table_ref) | copy-start | bytes 196612
  23.8 20.3 %copy-start.3 = (bf16[128,128]{1,0:T(8,128)(2,1)S(1)}, bf16[128,128]{1,0:T(8,128)(2,1)}, u32[]{:S(2)}) copy-start(bf16[128,128]{1,0:T(8,128)(2,1)} %constant.17.clone.across_ref) | copy-start | bytes 98308
  23.8 20.3 %copy-start.4 = (bf16[64,64]{1,0:T(8,128)(2,1)S(1)}, bf16[64,64]{1,0:T(8,128)(2,1)}, u32[]{:S(2)}) copy-start(bf16[64,64]{1,0:T(8,128)(2,1)} %constant.16.clone.form_ref) | copy-start | bytes 24580
  24.1 37.6 %copy-start.5 = (f32[32,128]{1,0:T(8,128)S(1)}, f32[32,128]{1,0:T(8,128)}, u32[]{:S(2)}) copy-start(f32[32,128]{1,0:T(8,128)} %get-tuple-element.9.own_ref) | copy-start | bytes 49156

commit v8 on v5

--- a/solution.py
+++ b/solution.py
@@ -12,7 +12,7 @@
 SMAX = 8
 CHIP = 64
 LANES = 128
-BATCH = 32
+BATCH = 28
 F32 = jnp.float32
 BF16 = jnp.bfloat16
 

time: 63.9 us -> 64.9 us (1.016)
  blocking collectives: 15.7 us -> 16.9 us
    all_to_all x1, blocking collectives: 15.7 us -> 16.9 us  [body(): lax.all_to_all(result, 'date', split_axis=0, concat_axis=0, tiled=True)]
where the time goes in v8:
time: 64.9 us; the launch traced here: 64.7 us
  waiting for transfers between devices  19.3 us (30%)
  blocking collectives  16.9 us (26%)
  starting transfers between devices  15.5 us (24%)
  Pallas kernels  6.42 us (10%)
  local copies, waits for them, and re-layouts  3.52 us (5%)
  other arithmetic  1.56 us (2%)
  between operations  1.51 us (2%)
    all_to_all x1, waiting for transfers between devices, body(): recv = lax.all_to_all(send, 'date', split_axis=0, concat_axis=0, tiled=True)  19.3 us
    all_to_all x1, blocking collectives, body(): lax.all_to_all(result, 'date', split_axis=0, concat_axis=0, tiled=True)  16.9 us
    all_to_all x1, starting transfers between devices, body(): recv = lax.all_to_all(send, 'date', split_axis=0, concat_axis=0, tiled=True)  9.96 us
    ppermute x1, starting transfers between devices, body(): lax.ppermute(images[:, :SMAX, :], 'strip', [(i + 1, i) for i in range(end...  3.64 us
    pallas_call x1, Pallas kernels, body(): pl.pallas_call(pack_kernel, out_shape=(jax.ShapeDtypeStruct((blocks, 2 *...  2.72 us
    pallas_call x1, Pallas kernels, body(): pl.pallas_call(match_kernel, out_shape=jax.ShapeDtypeStruct((blocks, 4, c...  2.7 us
    concatenate x1, local copies, waits for them, and re-layouts, body(): turned = jnp.concatenate([turned, turned], axis=4)  2.16 us
    ppermute x1, starting transfers between devices, body(): lax.ppermute(images[:, length - SMAX:, :], 'strip', [(i, i + 1) for i in...  1.92 us
  transfers between devices with their start and end apart: 3, of which 1 were waited for; matrix products, arithmetic and copies ran while one was open for 8% of the time, Pallas kernels for 0%

profile of v8, /device:TPU:448, one launch (start us, length us, event | category | flops | bytes accessed | tf_op | source)
XLA Modules:
  0.0 64.7 jit_solution(16812939111403368738)
XLA Ops:
  0.6 0.0 copy-start
  0.6 0.0 copy-start.6
  1.3 2.7 %shard_map.140 = (bf16[32,136,128]{2,1,0:T(8,128)(2,1)}, f32[32,128]{1,0:T(8,128)}) custom-call(s32[32]{0:T(128)} %first_hbm.1, s32[32]{0:T(128)} %bitcast.14, s32[32]{0:T(128)} %second_hbm.1, s32[1]{0:T(128)S(6)} %copy.28.count_hbm, s32[2,2,32]{2,1,0:T(2,128)} %bitcast.13, s32[2]{0:T(128)} %anchors_hbm.1, bf16[16,64,128]{2,1,0:T(8,128)(2,1)} %images_ref.1, ...), custom_call_target="tpu_custom_call" | custom-call | tf_op jit(solution)/shard_map/pallas_call | solution.py:339
  4.1 10.0 %all-to-all-start = ((bf16[32,136,128]{2,1,0:T(8,128)(2,1)}), bf16[32,136,128]{2,1,0:T(8,128)(2,1)S(1)}, u32[]{:S(2)}, u32[]{:S(2)}) async-start(bf16[32,136,128]{2,1,0:T(8,128)(2,1)} %get-tuple-element.10), calls=%async_computation | async-start | bytes 2228224 | tf_op jit(solution)/shard_map/all_to_all | solution.py:368
  14.0 0.0 copy-done
  14.1 1.9 %collective-permute-start = (bf16[16,8,128]{2,1,0:T(8,128)(2,1)S(1)}, bf16[16,8,128]{2,1,0:T(8,128)(2,1)S(1)}, u32[]{:S(2)}, u32[]{:S(2)}) collective-permute-start(bf16[16,8,128]{2,1,0:T(8,128)(2,1)S(1)} %get-tuple-element.17), channel_id=1, source_target_pairs={{0,32},{32,64},{64,96},{96,128},{128,160},{160,192},{192,224},{224... | collective-permute-start | bytes 98312 | tf_op jit(solution)/shard_map/ppermute | solution.py:328
  16.0 3.6 %collective-permute-start.1 = (bf16[16,8,128]{2,1,0:T(8,128)(2,1)S(1)}, bf16[16,8,128]{2,1,0:T(8,128)(2,1)S(1)}, u32[]{:S(2)}, u32[]{:S(2)}) collective-permute-start(bf16[16,8,128]{2,1,0:T(8,128)(2,1)S(1)} %get-tuple-element.16), channel_id=1, source_target_pairs={{32,0},{64,32},{96,64},{128,96},{160,128},{192,160},{224,192},{256... | collective-permute-start | bytes 98312 | tf_op jit(solution)/shard_map/ppermute | solution.py:331
  19.7 0.0 copy-done.6
  19.7 0.4 reshape.17
  20.0 1.6 %pad_maximum_fusion = f32[2,16,16,2,64]{1,4,2,3,0:T(8,128)} fusion(f32[2,16,16,2,32]{1,4,2,3,0:T(8,128)S(1)} %bitcast.10), kind=kLoop, calls=%fused_computation | loop fusion | flops 65536 | bytes 393216 | tf_op jit(solution)/shard_map/concatenate | solution.py:333
  21.6 2.2 %copy.25 = f32[2,16,16,2,64]{4,3,2,1,0:T(2,128)S(1)} copy(f32[2,16,16,2,64]{1,4,2,3,0:T(8,128)} %pad_maximum_fusion) | data formatting | bytes 524288 | tf_op jit(solution)/shard_map/concatenate | solution.py:333
  23.8 0.0 copy-start.1
  23.8 0.0 copy-start.2
  23.8 0.0 copy-start.3
  23.8 0.0 copy-start.4
  23.8 0.3 reshape.18.firsts_ref
  24.1 0.0 copy-start.5
  24.1 0.3 copy.26
  24.4 0.2 copy.27
  24.6 0.1 pad.4.seconds_ref
  24.8 19.3 %all-to-all-done.recv_ref = bf16[32,136,128]{2,1,0:T(8,128)(2,1)S(1)} async-done(((bf16[32,136,128]{2,1,0:T(8,128)(2,1)}), bf16[32,136,128]{2,1,0:T(8,128)(2,1)S(1)}, u32[]{:S(2)}, u32[]{:S(2)}) %all-to-all-start) | async-done | bytes 1114144 | tf_op jit(solution)/shard_map/all_to_all | solution.py:368
  44.1 0.0 collective-permute-done.above_ref
  44.1 0.0 collective-permute-done.1.below_ref
  44.1 0.0 copy-done.1
  44.1 0.0 copy-done.2
  44.1 0.0 copy-done.3
  44.1 0.0 copy-done.4
  44.1 2.7 %shard_map.141 = f32[32,4,128]{2,1,0:T(4,128)S(1)} custom-call(bf16[32,136,128]{2,1,0:T(8,128)(2,1)S(1)} %all-to-all-done.recv_ref, bf16[16,64,128]{2,1,0:T(8,128)(2,1)S(1)} %copy-done, bf16[16,8,128]{2,1,0:T(8,128)(2,1)S(1)} %collective-permute-done.above_ref, bf16[16,8,128]{2,1,0:T(8,128)(2,1)S(1)} %collective-permute-done.1.below_ref, ...), custom_call_target="tpu_custom_call" | custom-call | tf_op jit(solution)/shard_map/pallas_call | solution.py:370
  46.8 16.9 %all_to_all.10 = f32[32,4,128]{2,1,0:T(4,128)S(1)} all-to-all(f32[32,4,128]{2,1,0:T(4,128)S(1)} %shard_map.141), channel_id=1, replica_groups=mesh['strip'=16,'date'=32] {'date'}, dimensions={0} | all-to-all | bytes 131072 | tf_op jit(solution)/shard_map/all_to_all | solution.py:390
  63.7 0.0 copy-done.5
  63.7 1.0 %shard_map.142 = (f32[2,2,32]{2,1,0:T(2,128)}, f32[2,2,16]{2,1,0:T(2,128)}) custom-call(f32[32,128]{1,0:T(8,128)S(1)} %copy-done.5, f32[128,128]{1,0:T(8,128)S(1)} %bitcast.9, f32[2,16,16,128]{3,2,1,0:T(8,128)S(1)} %reshape.18.firsts_ref, f32[16,32,128]{2,1,0:T(8,128)S(1)} %pad.4.seconds_ref), custom_call_target="tpu_custom_call" | custom-call | tf_op jit(solution)/shard_map/pallas_call | solution.py:391
  (1 shorter events, 0.0 us)
Async XLA Ops:
  0.6 13.4 %copy-start = (bf16[16,64,128]{2,1,0:T(8,128)(2,1)S(1)}, bf16[16,64,128]{2,1,0:T(8,128)(2,1)}, u32[]{:S(2)}) copy-start(bf16[16,64,128]{2,1,0:T(8,128)(2,1)} %images_ref.1) | copy-start | bytes 786436
  0.6 19.0 %copy-start.6 = (f32[2,2,16,512]{3,2,1,0:T(8,128)S(1)}, f32[2,2,16,512]{3,2,1,0:T(8,128)}, u32[]{:S(2)}) copy-start(f32[2,2,16,512]{3,2,1,0:T(8,128)} %param.14) | copy-start | bytes 393220
  4.1 40.0 %all-to-all-start = ((bf16[32,136,128]{2,1,0:T(8,128)(2,1)}), bf16[32,136,128]{2,1,0:T(8,128)(2,1)S(1)}, u32[]{:S(2)}, u32[]{:S(2)}) async-start(bf16[32,136,128]{2,1,0:T(8,128)(2,1)} %get-tuple-element.10), calls=%async_computation | async-start | bytes 2228224 | tf_op jit(solution)/shard_map/all_to_all | solution.py:368
  14.1 30.0 %collective-permute-start = (bf16[16,8,128]{2,1,0:T(8,128)(2,1)S(1)}, bf16[16,8,128]{2,1,0:T(8,128)(2,1)S(1)}, u32[]{:S(2)}, u32[]{:S(2)}) collective-permute-start(bf16[16,8,128]{2,1,0:T(8,128)(2,1)S(1)} %get-tuple-element.17), channel_id=1, source_target_pairs={{0,32},{32,64},{64,96},{96,128},{128,160},{160,192},{192,224},{224... | collective-permute-start | bytes 98312 | tf_op jit(solution)/shard_map/ppermute | solution.py:328
  16.0 28.1 %collective-permute-start.1 = (bf16[16,8,128]{2,1,0:T(8,128)(2,1)S(1)}, bf16[16,8,128]{2,1,0:T(8,128)(2,1)S(1)}, u32[]{:S(2)}, u32[]{:S(2)}) collective-permute-start(bf16[16,8,128]{2,1,0:T(8,128)(2,1)S(1)} %get-tuple-element.16), channel_id=1, source_target_pairs={{32,0},{64,32},{96,64},{128,96},{160,128},{192,160},{224,192},{256... | collective-permute-start | bytes 98312 | tf_op jit(solution)/shard_map/ppermute | solution.py:331
  23.8 20.3 %copy-start.1 = (bf16[64,64]{1,0:T(8,128)(2,1)S(1)}, bf16[64,64]{1,0:T(8,128)(2,1)}, u32[]{:S(2)}) copy-start(bf16[64,64]{1,0:T(8,128)(2,1)} %constant.15.clone.forward_hbm.forward_ref) | copy-start | bytes 24580
  23.8 20.3 %copy-start.2 = (bf16[128,256]{1,0:T(8,128)(2,1)S(1)}, bf16[128,256]{1,0:T(8,128)(2,1)}, u32[]{:S(2)}) copy-start(bf16[128,256]{1,0:T(8,128)(2,1)} %constant.14.clone.table_ref) | copy-start | bytes 196612
  23.8 20.3 %copy-start.3 = (bf16[128,128]{1,0:T(8,128)(2,1)S(1)}, bf16[128,128]{1,0:T(8,128)(2,1)}, u32[]{:S(2)}) copy-start(bf16[128,128]{1,0:T(8,128)(2,1)} %constant.17.clone.across_ref) | copy-start | bytes 98308
  23.8 20.3 %copy-start.4 = (bf16[64,64]{1,0:T(8,128)(2,1)S(1)}, bf16[64,64]{1,0:T(8,128)(2,1)}, u32[]{:S(2)}) copy-start(bf16[64,64]{1,0:T(8,128)(2,1)} %constant.16.clone.form_ref) | copy-start | bytes 24580
  24.1 39.6 %copy-start.5 = (f32[32,128]{1,0:T(8,128)S(1)}, f32[32,128]{1,0:T(8,128)}, u32[]{:S(2)}) copy-start(f32[32,128]{1,0:T(8,128)} %get-tuple-element.9.own_ref) | copy-start | bytes 49156
